TPU v7x, 128 devices: a whole 4x4x4 slice. The times are simulated.
128 devices in a mesh: ctx: 8 (over z, x_hi), exp: 16 (over y, x_lo, core).
Axes of the slice: x: 4 (x_hi: 2, x_lo: 2; x = x_hi * 2 + x_lo), y: 4, z: 4, core: 2. Of those that a mesh axis runs over, the one named last changes fastest.
Arguments:
- query_rows: bfloat16 [16, 1024, 5120], P('exp', 'ctx'), may hold values from -5 to 5
- key_rows: bfloat16 [16, 1024, 1024], P('exp', 'ctx'), may hold values from -5 to 5
- value_rows: bfloat16 [16, 1024, 1024], P('exp', 'ctx'), may hold values from -6 to 6
- stream: bfloat16 [16, 1024, 5120], P('exp', 'ctx'), may hold values from -33 to 33
- out_grad: bfloat16 [16, 1024, 5120], P('exp', 'ctx'), may hold values from -6 to 6
- route_weight: float32 [16, 1024], P('exp', 'ctx'), may hold values from 0.2 to 1
- expert_ids: int32 [16, 1024, 1], P('exp', 'ctx'), may hold values from 0 to 15
- span_order: int32 [16], replicated, may hold values from 0 to 15, each once
- norm_gain: float32 [5120], replicated, may hold values from 0.1 to 1.9
- expert_gate: bfloat16 [16, 5120, 4096], P('exp', None, 'ctx'), may hold values from -0.078125 to 0.078125
- expert_in: bfloat16 [16, 5120, 4096], P('exp', None, 'ctx'), may hold values from -0.078125 to 0.078125
- expert_out: bfloat16 [16, 4096, 5120], P('exp', 'ctx'), may hold values from -0.09375 to 0.09375
Outputs:
- grad_stream: bfloat16 [16, 1024, 5120], P('exp', 'ctx')
- grad_query: bfloat16 [16, 1024, 5120], P('exp', 'ctx')
- grad_key: bfloat16 [16, 1024, 1024], P('exp', 'ctx')
- grad_value: bfloat16 [16, 1024, 1024], P('exp', 'ctx')
All inputs are finite; a program needn't handle non-finite values.
Results may differ from a plain program's by a relative error of at most 0.039.
Values may be sent and summed in bfloat16 or wider, within the bound.
No kernel may reach another device: no remote copies, remote signals or barrier semaphores. Data moves between devices by JAX's collectives and lax.ppermute only.
A program may use at most 192 MiB of HBM per device.

v0:
```python
import jax
import jax.numpy as jnp
from jax import lax
from jax.sharding import PartitionSpec as P

H = 40
KVH = 8
DH = 128


EPSILON = 1e-05


def normalize(stream_f, norm_gain):
    return (
        stream_f
        * lax.rsqrt(jnp.mean(stream_f * stream_f, axis=-1, keepdims=True) + EPSILON)
        * norm_gain
    )


def stored_positions(storage, span_order, span_len):
    matched = (storage // span_len)[:, None] == jnp.arange(span_order.shape[0], dtype=jnp.int32)[
        None, :
    ]
    return (
        jnp.sum(jnp.where(matched, span_order[None, :], 0), axis=1) * span_len + storage % span_len
    )


def expert_partial(arrived, w_gate_one, w_in_one, w_out_one):
    model_width = arrived.shape[-1]
    inputs = arrived[0].reshape(-1, model_width)
    cotangent = arrived[1].reshape(-1, model_width)
    gate_pre = jnp.dot(inputs, w_gate_one, preferred_element_type=jnp.float32)
    up_pre = jnp.dot(inputs, w_in_one, preferred_element_type=jnp.float32)
    backed = jnp.einsum("rd,fd->rf", cotangent, w_out_one, preferred_element_type=jnp.float32)
    gate_sig = jax.nn.sigmoid(gate_pre)
    grad_gate = (backed * up_pre * gate_sig * (1.0 + gate_pre * (1.0 - gate_sig))).astype(
        jnp.bfloat16
    )
    grad_up = (backed * gate_pre * gate_sig).astype(jnp.bfloat16)
    block_term = jnp.einsum("rf,df->rd", grad_gate, w_gate_one, preferred_element_type=jnp.float32)
    block_term = block_term + jnp.einsum(
        "rf,df->rd", grad_up, w_in_one, preferred_element_type=jnp.float32
    )
    return block_term.astype(jnp.bfloat16).reshape(arrived.shape[1], arrived.shape[2], model_width)


def attend_rows(query_b, keys_all, values_all, grad_b, query_pos, key_pos):
    group_size = H // KVH
    factor = DH ** (-0.5)
    queries = query_b.reshape(-1, KVH, group_size, DH)
    grad_heads = grad_b.reshape(-1, KVH, group_size, DH)
    keys_r = keys_all.reshape(-1, KVH, DH)
    values_r = values_all.reshape(-1, KVH, DH)
    scores = (
        jnp.einsum("tkgd,skd->kgts", queries, keys_r, preferred_element_type=jnp.float32) * factor
    )
    visible = key_pos[None, :] <= query_pos[:, None]
    scores = jnp.where(visible, scores, -1e30)
    row_peak = jnp.max(scores, axis=-1, keepdims=True)
    weights = jnp.exp(scores - row_peak)
    attn_probs = weights / jnp.sum(weights, axis=-1, keepdims=True)
    probs_b = attn_probs.astype(jnp.bfloat16)
    attended = jnp.einsum("kgts,skd->tkgd", probs_b, values_r, preferred_element_type=jnp.float32)
    row_delta = jnp.sum(grad_heads.astype(jnp.float32) * attended, axis=-1)
    dprobs = jnp.einsum("tkgd,skd->kgts", grad_heads, values_r, preferred_element_type=jnp.float32)
    dscores = (attn_probs * (dprobs - jnp.transpose(row_delta, (1, 2, 0))[..., None])).astype(
        jnp.bfloat16
    )
    grad_q = (
        jnp.einsum("kgts,skd->tkgd", dscores, keys_r, preferred_element_type=jnp.float32) * factor
    )
    key_part = (
        jnp.einsum("kgts,tkgd->skd", dscores, queries, preferred_element_type=jnp.float32) * factor
    )
    value_part = jnp.einsum(
        "kgts,tkgd->skd", probs_b, grad_heads, preferred_element_type=jnp.float32
    )
    return (
        grad_q.reshape(query_b.shape).astype(jnp.bfloat16),
        key_part.reshape(keys_all.shape),
        value_part.reshape(values_all.shape),
    )


def body(
    query_rows,
    key_rows,
    value_rows,
    stream,
    out_grad,
    route_weight,
    expert_ids,
    span_order,
    norm_gain,
    expert_gate,
    expert_in,
    expert_out,
):
    tokens = stream.shape[1]
    model_width = stream.shape[2]
    ctx_count = lax.axis_size("ctx")
    exp_count = lax.axis_size("exp")
    capacity = tokens // (2 * exp_count)
    gathered_keys, gathered_values = (
        lax.all_gather(key_rows, "ctx", axis=1, tiled=True),
        lax.all_gather(value_rows, "ctx", axis=1, tiled=True),
    )
    stream_f = stream[0].astype(jnp.float32)
    normed = normalize(stream_f, norm_gain)
    normed_b = normed.astype(jnp.bfloat16)
    out_grad_f = out_grad[0].astype(jnp.float32)
    routed_b = (out_grad_f * route_weight[0][:, None]).astype(jnp.bfloat16)
    expert_col = expert_ids[0, :, 0]
    onehot = (expert_col[:, None] == jnp.arange(exp_count, dtype=jnp.int32)[None, :]).astype(
        jnp.int32
    )
    slot_rank = jnp.sum((jnp.cumsum(onehot, axis=0) - 1) * onehot, axis=1)
    kept_rows = slot_rank < capacity
    slot_of = expert_col * capacity + jnp.minimum(slot_rank, capacity - 1)
    dispatch = (
        (slot_of[None, :] == jnp.arange(exp_count * capacity, dtype=jnp.int32)[:, None])
        & kept_rows[None, :]
    ).astype(jnp.bfloat16)
    stacked = jnp.stack([normed_b, routed_b])
    outgoing = jnp.einsum(
        "jt,std->sjd", dispatch, stacked, preferred_element_type=jnp.float32
    ).astype(jnp.bfloat16)
    outgoing = outgoing.reshape(2, exp_count, capacity, model_width)
    w_gate_one = expert_gate[0]
    w_in_one = expert_in[0]
    w_out_one = expert_out[0]
    copies = jnp.broadcast_to(outgoing[:, None], (2, ctx_count, exp_count, capacity, model_width))
    copies = copies.reshape(2, ctx_count * exp_count, capacity, model_width)
    partials = expert_partial(
        lax.all_to_all(copies, ("ctx", "exp"), split_axis=1, concat_axis=1, tiled=True),
        w_gate_one,
        w_in_one,
        w_out_one,
    )
    returned = lax.all_to_all(partials, ("ctx", "exp"), split_axis=0, concat_axis=0, tiled=True)
    summed = jnp.sum(
        returned.reshape(ctx_count, exp_count * capacity, model_width).astype(jnp.float32), axis=0
    )
    input_grad = jnp.take(summed, slot_of, axis=0) * kept_rows[:, None].astype(jnp.float32)

    def normed_of(values):
        return normalize(values, norm_gain)

    _, pullback = jax.vjp(normed_of, stream_f)
    stream_grad = pullback(input_grad)[0]
    grad_total = (out_grad_f + stream_grad).astype(jnp.bfloat16)
    span_len = tokens // 2
    local_rows = lax.axis_index("ctx") * tokens + jnp.arange(tokens, dtype=jnp.int32)
    query_pos = stored_positions(local_rows, span_order, span_len)
    key_pos = stored_positions(
        jnp.arange(tokens * ctx_count, dtype=jnp.int32), span_order, span_len
    )
    grad_q, key_part, value_part = attend_rows(
        query_rows[0], gathered_keys[0], gathered_values[0], grad_total, query_pos, key_pos
    )
    key_sum, value_sum = (
        lax.psum_scatter(
            key_part[None].astype(jnp.bfloat16), "ctx", scatter_dimension=1, tiled=True
        ).astype(jnp.float32),
        lax.psum_scatter(
            value_part[None].astype(jnp.bfloat16), "ctx", scatter_dimension=1, tiled=True
        ).astype(jnp.float32),
    )
    return (
        grad_total[None],
        grad_q[None],
        key_sum.astype(jnp.bfloat16),
        value_sum.astype(jnp.bfloat16),
    )


def solution(mesh):
    return jax.shard_map(
        body,
        mesh=mesh,
        in_specs=(
            P("exp", "ctx", None),
            P("exp", "ctx", None),
            P("exp", "ctx", None),
            P("exp", "ctx", None),
            P("exp", "ctx", None),
            P("exp", "ctx"),
            P("exp", "ctx", None),
            P(),
            P(),
            P("exp", None, "ctx"),
            P("exp", None, "ctx"),
            P("exp", "ctx", None),
        ),
        out_specs=(
            P("exp", "ctx", None),
            P("exp", "ctx", None),
            P("exp", "ctx", None),
            P("exp", "ctx", None),
        ),
        check_vma=False,
    )
```

profile of v0, /device:TPU:0, one launch (start us, length us, event | category | flops | bytes accessed | tf_op | source)
XLA Modules:
  0.0 538.0 jit_solution(17240316908349119674)
XLA Ops:
  7.2 1.7 fusion.30
  8.8 0.7 fusion.47
  9.8 0.8 select_reduce_fusion.2
  10.6 0.7 fusion.68
  11.3 2.4 multiply_convert_fusion.1
  13.7 0.5 fusion.8
  14.3 0.5 broadcast_in_dim.83
  14.8 0.6 copy.69
  15.4 6.3 %broadcast_in_dim.84 = bf16[2,8,16,4,5120]{4,3,0,2,1:T(4,128)(2,1)} broadcast(bf16[2,16,4,5120]{3,2,0,1:T(4,128)(2,1)S(1)} %copy.69), dimensions={0,2,3,4} | broadcast | bytes 11796480 | tf_op jit(solution)/shard_map/broadcast_in_dim | solution.py:135
  21.8 11.6 %all-to-all-start = ((bf16[2,128,4,5120]{3,2,0,1:T(4,128)(2,1)}), bf16[2,128,4,5120]{3,2,0,1:T(4,128)(2,1)}, u32[]{:S(2)}, u32[]{:S(2)}) async-start(bf16[2,128,4,5120]{3,2,0,1:T(4,128)(2,1)} %bitcast.137), calls=%async_computation | async-start | bytes 20971520 | tf_op jit(solution)/shard_map/all_to_all | solution.py:138
  33.4 0.8 copy.70
  34.3 0.2 all-gather.5.cloned.1.call-start
  34.5 0.8 copy.77
  35.4 1.8 copy.74
  37.3 1.8 copy.76
  39.1 1.4 copy.71
  40.5 121.6 %all-to-all-done = bf16[2,128,4,5120]{3,2,0,1:T(4,128)(2,1)} async-done(((bf16[2,128,4,5120]{3,2,0,1:T(4,128)(2,1)}), bf16[2,128,4,5120]{3,2,0,1:T(4,128)(2,1)}, u32[]{:S(2)}, u32[]{:S(2)}) %all-to-all-start) | async-done | bytes 10485792 | tf_op jit(solution)/shard_map/all_to_all | solution.py:138
  162.2 11.3 %fusion.69 = (bf16[1,128,4,5120]{3,2,0,1:T(4,128)(2,1)}, bf16[1,128,4,5120]{3,2,0,1:T(4,128)(2,1)}) fusion(bf16[2,128,4,5120]{3,2,0,1:T(4,128)(2,1)} %all-to-all-done), kind=kLoop, calls=%fused_computation.106 | loop fusion | bytes 20971520 | tf_op jit(solution)/shard_map/slice | solution.py:33
  173.4 8.9 %reshape_squeeze.16 = bf16[512,5120]{1,0:T(8,128)(2,1)} reshape(bf16[1,128,4,5120]{3,2,0,1:T(4,128)(2,1)} %get-tuple-element.22) | data formatting | bytes 10485760 | tf_op jit(solution)/shard_map/reshape;squeeze | solution.py:33
  182.4 9.0 %reshape_squeeze.15 = bf16[512,5120]{1,0:T(8,128)(2,1)} reshape(bf16[1,128,4,5120]{3,2,0,1:T(4,128)(2,1)} %get-tuple-element.23) | data formatting | bytes 10485760 | tf_op jit(solution)/shard_map/reshape;squeeze | solution.py:34
  191.4 6.6 %fusion.11 = f32[512,512]{1,0:T(8,128)S(1)} fusion(bf16[512,5120]{1,0:T(8,128)(2,1)} %reshape_squeeze.16, bf16[1,5120,512]{2,1,0:T(8,128)(2,1)} %param.21), kind=kOutput, calls=%fused_computation.18 | convolution fusion | flops 2684354560 | bytes 11534336 | tf_op jit(solution)/shard_map/dot_general | solution.py:35
  198.0 5.6 %fusion.16 = f32[512,512]{1,0:T(8,128)S(1)} fusion(bf16[512,5120]{1,0:T(8,128)(2,1)S(1)} %copy-done.5, bf16[1,512,5120]{2,1,0:T(8,128)(2,1)} %param.23), kind=kOutput, calls=%fused_computation.23 | convolution fusion | flops 2684354560 | bytes 11534336 | tf_op jit(solution)/shard_map/rd,fd->rf/dot_general | solution.py:37
  203.7 1.0 copy-done.14
  204.6 5.7 %fusion.43 = bf16[512,512]{1,0:T(8,128)(2,1)S(1)} fusion(f32[512,512]{1,0:T(8,128)S(1)} %fusion.16, bf16[512,5120]{1,0:T(8,128)(2,1)S(1)} %bitcast.145, bf16[1,5120,512]{2,1,0:T(8,128)(2,1)} %param.22, f32[512,512]{1,0:T(8,128)S(1)} %fusion.11), kind=kOutput, calls=%fused_computation.54 | convolution fusion | flops 2686976000 | bytes 13107200 | tf_op jit(solution)/shard_map/dot_general | solution.py:36
  210.4 2.9 fusion.9
  213.3 8.6 %add_convert_fusion = bf16[512,5120]{1,0:T(8,128)(2,1)} fusion(f32[512,5120]{1,0:T(8,128)S(1)} %fusion.9, bf16[1,5120,512]{2,1,0:T(8,128)(2,1)} %param.22, f32[512,512]{1,0:T(8,128)} %copy-done.14, f32[512,512]{1,0:T(8,128)} %copy-done.13), kind=kOutput, calls=%fused_computation.11 | convolution fusion | flops 2691170304 | bytes 23068672 | tf_op jit(solution)/shard_map/rf,df->rd/dot_general | solution.py:44
  221.8 9.3 %reshape.344 = bf16[128,4,5120]{2,1,0:T(4,128)(2,1)} reshape(bf16[512,5120]{1,0:T(8,128)(2,1)} %add_convert_fusion) | data formatting | bytes 10485760 | tf_op jit(solution)/shard_map/reshape | solution.py:47
  231.2 26.2 %all-to-all-start.1 = ((bf16[128,4,5120]{2,1,0:T(4,128)(2,1)}), bf16[128,4,5120]{2,1,0:T(4,128)(2,1)}, u32[]{:S(2)}, u32[]{:S(2)}) async-start(bf16[128,4,5120]{2,1,0:T(4,128)(2,1)} %reshape.344), calls=%async_computation.1 | async-start | bytes 10485760 | tf_op jit(solution)/shard_map/all_to_all | solution.py:143
  258.0 12.2 %fusion.70 = (f32[8,5,128]{2,1,0:T(8,128)S(1)}, f32[8,5,128,1024]{2,3,1,0:T(8,128)}) fusion(pred[128,1024]{0,1:T(8,128)(4,1)S(1)} %broadcast_compare_fusion, bf16[1024,8,128,1]{0,2,3,1:T(8,128)(2,1)} %bitcast.148, bf16[128,8,5,128]{0,3,2,1:T(8,128)(2,1)S(1)} %bitcast.153), kind=kOutput, calls=%fused_computation.107 | convolution fusion | flops 1363149824 | bytes 24530944 | tf_op jit(solution)/shard_map/sub | solution.py:63
  270.3 12.4 %fusion.7 = bf16[8,5,128,1024]{2,3,1,0:T(8,128)(2,1)} fusion(f32[8,5,128,1024]{2,3,1,0:T(8,128)} %get-tuple-element.29, f32[8,5,128]{2,1,0:T(8,128)S(1)} %get-tuple-element.28), kind=kLoop, calls=%fused_computation.13 | loop fusion | flops 10485760 | bytes 31477760 | tf_op jit(solution)/shard_map/convert_element_type | solution.py:65
  282.7 38.9 %all-to-all-done.1 = bf16[128,4,5120]{2,1,0:T(4,128)(2,1)} async-done(((bf16[128,4,5120]{2,1,0:T(4,128)(2,1)}), bf16[128,4,5120]{2,1,0:T(4,128)(2,1)}, u32[]{:S(2)}, u32[]{:S(2)}) %all-to-all-start.1) | async-done | bytes 5242912 | tf_op jit(solution)/shard_map/all_to_all | solution.py:143
  321.6 9.7 %reshape.346 = f32[8,64,5120]{2,1,0:T(8,128)} reshape(bf16[128,4,5120]{2,1,0:T(4,128)(2,1)} %all-to-all-done.1) | data formatting | bytes 15728640 | tf_op jit(solution)/shard_map/convert_element_type | solution.py:145
  331.2 4.7 reduce_sum.82
  335.9 2.9 gather_fusion
  338.8 3.3 copy.75
  342.2 2.1 fusion.31
  344.3 3.9 fusion.22
  348.2 6.8 %fusion.26 = f32[128,8,5]{0,2,1:T(8,128)S(1)} fusion(bf16[128,8,5,128]{0,3,2,1:T(8,128)(2,1)} %fusion.22, bf16[1024,8,128,1]{0,2,3,1:T(8,128)(2,1)} %bitcast.150, bf16[8,5,128,1024]{2,3,1,0:T(8,128)(2,1)} %fusion.7), kind=kOutput, calls=%fused_computation.38 | convolution fusion | flops 1344138240 | bytes 13914112 | tf_op jit(solution)/shard_map/kgts,skd->tkgd/dot_general | solution.py:66
  355.0 12.7 %fusion.2 = bf16[8,5,128,1024]{2,3,1,0:T(8,128)(2,1)} fusion(f32[8,5,128]{2,1,0:T(8,128)S(1)} %bitcast.154, f32[8,5,128,1024]{2,3,1,0:T(8,128)} %get-tuple-element.29, f32[8,5,128]{2,1,0:T(8,128)S(1)} %get-tuple-element.28, bf16[128,8,5,128]{0,3,2,1:T(8,128)(2,1)S(1)} %copy-done.2, bf16[1024,8,128,1]{0,2,3,1:T(8,128)(2,1)} %bitcast.151), kind=kOutput, calls=%fused_computation.4 | convolution fusion | flops 1363148800 | bytes 34906112 | tf_op jit(solution)/shard_map/tkgd,skd->kgts/dot_general | solution.py:68
  367.7 9.0 %fusion.18 = bf16[8,1024,128]{1,2,0:T(8,128)(2,1)} fusion(bf16[8,5,128,1024]{2,3,1,0:T(8,128)(2,1)} %fusion.2, bf16[128,8,5,128]{0,3,2,1:T(8,128)(2,1)} %bitcast.152), kind=kOutput, calls=%fused_computation.27 | convolution fusion | flops 1344274432 | bytes 13893632 | tf_op jit(solution)/shard_map/kgts,tkgd->skd/dot_general | solution.py:76
  376.7 4.0 copy.84
  380.7 9.1 %bitcast_convert_fusion = bf16[8,128,1024]{2,1,0:T(8,128)(2,1)} fusion(bf16[128,8,5,128]{0,3,2,1:T(8,128)(2,1)} %fusion.22, bf16[8,5,128,1024]{2,3,1,0:T(8,128)(2,1)} %fusion.7), kind=kOutput, calls=%fused_computation.25 | convolution fusion | flops 1343225856 | bytes 13893632 | tf_op jit(solution)/shard_map/kgts,tkgd->skd/dot_general | solution.py:78
  389.8 3.9 copy.86
  393.8 7.5 %multiply_convert_fusion = bf16[8,5,128,128]{2,3,1,0:T(8,128)(2,1)} fusion(bf16[1024,8,128,1]{0,2,3,1:T(8,128)(2,1)} %bitcast.149, bf16[8,5,128,1024]{2,3,1,0:T(8,128)(2,1)} %fusion.2), kind=kOutput, calls=%fused_computation.47 | convolution fusion | flops 1343488000 | bytes 13893632 | tf_op jit(solution)/shard_map/kgts,skd->tkgd/dot_general | solution.py:73
  401.3 2.4 copy.87
  403.7 3.8 fusion.20
  407.5 45.7 %reduce-scatter.3.cloned.1.call-done = bf16[1,128,1024]{2,1,0:T(8,128)(2,1)} async-done(((bf16[1,1024,1024]{2,1,0:T(8,128)(2,1)}), bf16[1,128,1024]{2,1,0:T(8,128)(2,1)}) %reduce-scatter.3.cloned.1.call-update) | async-done | bytes 262160 | tf_op jit(solution)/shard_map/reduce_scatter | solution.py:165
  453.3 78.2 %reduce-scatter.5.cloned.1.call-done = bf16[1,128,1024]{2,1,0:T(8,128)(2,1)} async-done(((bf16[1,1024,1024]{2,1,0:T(8,128)(2,1)}), bf16[1,128,1024]{2,1,0:T(8,128)(2,1)}) %reduce-scatter.5.cloned.1.call-update) | async-done | bytes 262160 | tf_op jit(solution)/shard_map/reduce_scatter | solution.py:168
  (61 shorter events, 1.0 us)
Async XLA Ops:
  21.7 11.7 %copy-start.9 = (bf16[1,128,1024]{2,1,0:T(8,128)(2,1)S(1)}, bf16[1,128,1024]{2,1,0:T(8,128)(2,1)}, u32[]{:S(2)}) copy-start(bf16[1,128,1024]{2,1,0:T(8,128)(2,1)} %param.13) | copy-start | bytes 786436
  21.7 12.8 %copy-start.10 = (bf16[1,128,1024]{2,1,0:T(8,128)(2,1)S(1)}, bf16[1,128,1024]{2,1,0:T(8,128)(2,1)}, u32[]{:S(2)}) copy-start(bf16[1,128,1024]{2,1,0:T(8,128)(2,1)} %param.14) | copy-start | bytes 786436
  21.7 13.7 %copy-start.8 = (f32[5120]{0:T(1024)S(1)}, f32[5120]{0:T(1024)}, u32[]{:S(2)}) copy-start(f32[5120]{0:T(1024)} %param.20) | copy-start | bytes 61444
  21.7 13.7 %copy-start.3 = (bf16[1,128,5120]{2,1,0:T(8,128)(2,1)S(1)}, bf16[1,128,5120]{2,1,0:T(8,128)(2,1)}, u32[]{:S(2)}) copy-start(bf16[1,128,5120]{2,1,0:T(8,128)(2,1)} %param.16) | copy-start | bytes 3932164
  21.8 140.4 %all-to-all-start = ((bf16[2,128,4,5120]{3,2,0,1:T(4,128)(2,1)}), bf16[2,128,4,5120]{3,2,0,1:T(4,128)(2,1)}, u32[]{:S(2)}, u32[]{:S(2)}) async-start(bf16[2,128,4,5120]{3,2,0,1:T(4,128)(2,1)} %bitcast.137), calls=%async_computation | async-start | bytes 20971520 | tf_op jit(solution)/shard_map/all_to_all | solution.py:138
  33.4 224.6 %all-gather.3.cloned.1.call-start = ((), (), s32[]{:S(2)}) async-start(), calls=%async_computation.4 | async-start | bytes 2359296 | tf_op jit(solution)/shard_map/all_gather | solution.py:108
  34.3 3.0 copy-start.1
  34.3 313.9 %all-gather.5.cloned.1.call-start = ((), (), s32[]{:S(2)}) async-start(), calls=%async_computation.5 | async-start | bytes 2359296 | tf_op jit(solution)/shard_map/all_gather | solution.py:109
  37.3 1.8 copy-start.6
  182.4 22.2 %slice-start.2 = ((s8[5242880]{0:T(1024)(128)(4,1)}), s8[1048576]{0:T(1024)(128)(4,1)S(1)}, s32[]{:S(2)}) async-start(s8[5242880]{0:T(1024)(128)(4,1)} %bitcast.144), calls=%async_computation.10 | async-start | bytes 2097152
  191.4 6.6 %copy-start.5 = (bf16[512,5120]{1,0:T(8,128)(2,1)S(1)}, bf16[512,5120]{1,0:T(8,128)(2,1)}, u32[]{:S(2)}) copy-start(bf16[512,5120]{1,0:T(8,128)(2,1)} %reshape_squeeze.15) | copy-start | bytes 15728644
  191.4 13.3 %slice-start.3 = ((s8[5242880]{0:T(1024)(128)(4,1)}), s8[4194304]{0:T(1024)(128)(4,1)S(1)}, s32[]{:S(2)}) async-start(s8[5242880]{0:T(1024)(128)(4,1)} %bitcast.144), calls=%async_computation.11 | async-start | bytes 8388608
  198.0 5.7 %copy-start.13 = (f32[512,512]{1,0:T(8,128)}, f32[512,512]{1,0:T(8,128)S(1)}, u32[]{:S(2)}) copy-start(f32[512,512]{1,0:T(8,128)S(1)} %fusion.11) | copy-start | bytes 3145732
  198.0 12.3 %slice-start = ((s8[5242880]{0:T(1024)(128)(4,1)}), s8[4194304]{0:T(1024)(128)(4,1)S(1)}, s32[]{:S(2)}) async-start(s8[5242880]{0:T(1024)(128)(4,1)} %bitcast.142), calls=%async_computation.8 | async-start | bytes 8388608
  203.6 1.0 copy-start.14
  204.6 5.7 %slice-start.1 = ((s8[5242880]{0:T(1024)(128)(4,1)}), s8[1048576]{0:T(1024)(128)(4,1)S(1)}, s32[]{:S(2)}) async-start(s8[5242880]{0:T(1024)(128)(4,1)} %bitcast.142), calls=%async_computation.9 | async-start | bytes 2097152
  231.2 26.3 %copy-start.11 = (s32[1,128,1]{1,2,0:T(1,128)S(1)}, s32[1,128,1]{1,2,0:T(1,128)}, u32[]{:S(2)}) copy-start(s32[1,128,1]{1,2,0:T(1,128)} %param.18) | copy-start | bytes 1540
  231.2 26.3 %copy-start.12 = (s32[16]{0:T(128)S(1)}, s32[16]{0:T(128)}, u32[]{:S(2)}) copy-start(s32[16]{0:T(128)} %param.19) | copy-start | bytes 196
  231.2 26.9 %copy-start.7 = (bf16[1,128,5120]{1,2,0:T(8,128)(2,1)S(1)}, bf16[1,128,5120]{1,2,0:T(8,128)(2,1)}, u32[]{:S(2)}) copy-start(bf16[1,128,5120]{1,2,0:T(8,128)(2,1)} %copy.71) | copy-start | bytes 3932164
  231.2 90.4 %all-to-all-start.1 = ((bf16[128,4,5120]{2,1,0:T(4,128)(2,1)}), bf16[128,4,5120]{2,1,0:T(4,128)(2,1)}, u32[]{:S(2)}, u32[]{:S(2)}) async-start(bf16[128,4,5120]{2,1,0:T(4,128)(2,1)} %reshape.344), calls=%async_computation.1 | async-start | bytes 10485760 | tf_op jit(solution)/shard_map/all_to_all | solution.py:143
  257.4 195.9 %reduce-scatter.3.cloned.1.call-start = ((), (), s32[]{:S(2)}) async-start(), calls=%async_computation.6 | async-start | bytes 2359296 | tf_op jit(solution)/shard_map/reduce_scatter | solution.py:165
  338.8 3.3 copy-start
  342.1 2.2 copy-start.4
  348.2 6.8 %copy-start.2 = (bf16[128,8,5,128]{0,3,2,1:T(8,128)(2,1)S(1)}, bf16[128,8,5,128]{0,3,2,1:T(8,128)(2,1)}, u32[]{:S(2)}) copy-start(bf16[128,8,5,128]{0,3,2,1:T(8,128)(2,1)} %fusion.22) | copy-start | bytes 3932164
  380.6 150.8 %reduce-scatter.5.cloned.1.call-start = ((), (), s32[]{:S(2)}) async-start(), calls=%async_computation.7 | async-start | bytes 2359296 | tf_op jit(solution)/shard_map/reduce_scatter | solution.py:168
Sparse Core Ops, SparseCore 0:
  37.0 141.5 all-gather.2
  181.4 61.4 all-gather.4
  380.8 72.4 reduce-scatter.2
  457.4 73.9 reduce-scatter.4
where the time goes:
time: 540 us; the launch traced here: 538 us
  waiting for transfers between devices  284 us (53%)
  matrix products  87.3 us (16%)
  local copies, waits for them, and re-layouts  80 us (15%)
  starting transfers between devices  38.1 us (7%)
  other arithmetic  33.9 us (6%)
  between operations  14.1 us (3%)
    all_to_all x1, waiting for transfers between devices, body(): lax.all_to_all(copies, ('ctx', 'exp'), split_axis=1, concat_axis=1, tiled...  122 us
    reduce_scatter x1, waiting for transfers between devices, body(): lax.psum_scatter(value_part[None].astype(jnp.bfloat16), 'ctx', scatter_di...  78.2 us
    reduce_scatter x1, waiting for transfers between devices, body(): lax.psum_scatter(key_part[None].astype(jnp.bfloat16), 'ctx', scatter_dime...  45.7 us
    all_to_all x1, waiting for transfers between devices, body(): lax.all_to_all(partials, ('ctx', 'exp'), split_axis=0, concat_axis=0, til...  38.9 us
    all_to_all x1, starting transfers between devices, body(): lax.all_to_all(partials, ('ctx', 'exp'), split_axis=0, concat_axis=0, til...  26.2 us
    dot_general x1, matrix products, attend_rows(): jnp.einsum('tkgd,skd->kgts', grad_heads, values_r, preferred_element_type...  12.7 us
    convert_element_type x1, other arithmetic, attend_rows(): probs_b = attn_probs.astype(jnp.bfloat16)  12.4 us
    sub x1, matrix products, attend_rows(): weights = jnp.exp(scores - row_peak)  12.2 us
  transfers between devices with their start and end apart: 6, of which 4 were waited for; matrix products, arithmetic and copies ran while one was open for 28% of the time, Pallas kernels for 0%

commit v1 on v0

v1 whole, which is shorter than its diff:
```python
import functools

import jax
import jax.numpy as jnp
from jax import lax
from jax.experimental import pallas as pl
from jax.experimental.pallas import tpu as pltpu
from jax.sharding import PartitionSpec as P

D = 5120
H = 40
KVH = 8
DH = 128
GROUP = H // KVH
EXPERTS = 16
CAP = 4
TOK = 128
SEQ = 1024
SPAN = 64
SPANS = SEQ // SPAN
FFD = 512
EPSILON = 1e-05
F32 = jnp.float32
BF16 = jnp.bfloat16
QB = 256
NQ = SEQ // QB
GW = GROUP * DH
IN_CHUNKS = 2
OUT_CHUNKS = 2
DI = D // IN_CHUNKS
DO = D // OUT_CHUNKS
KB = 512
SHIFTS = (1, 3, 2)
FACTOR = DH ** (-0.5)


def nn(a, b):
    return lax.dot_general(a, b, (((1,), (0,)), ((), ())), preferred_element_type=F32)


def nt(a, b):
    return lax.dot_general(a, b, (((1,), (1,)), ((), ())), preferred_element_type=F32)


def tn(a, b):
    return lax.dot_general(a, b, (((0,), (0,)), ((), ())), preferred_element_type=F32)


def iota(shape, dim):
    return lax.broadcasted_iota(jnp.int32, shape, dim)


def params(mb=48):
    return pltpu.CompilerParams(vmem_limit_bytes=mb * 1024 * 1024)


def sds(shape, dtype=BF16):
    return jax.ShapeDtypeStruct(shape, dtype)


VM = pl.BlockSpec(memory_space=pltpu.VMEM)


def dispatch_kernel(stream, out_grad, weight, ids, gain, *outs):
    rows, picks = outs[:-1], outs[-1]
    onehot = ids[...] == iota((TOK, 128), 1)
    onehot_f = onehot.astype(F32)
    lower = (iota((TOK, TOK), 1) < iota((TOK, TOK), 0)).astype(BF16)
    before = nn(lower, onehot_f.astype(BF16))
    rank = jnp.sum(before * onehot_f, axis=1, keepdims=True).astype(jnp.int32)
    lane = iota((TOK, 128), 1)
    target = ids[...] * 8 + rank
    kept = rank < CAP
    pick_n = ((lane == target) & kept).astype(BF16)
    pick_r = ((lane == target + CAP) & kept).astype(BF16)
    pick = jnp.concatenate([pick_n, pick_r], axis=0)
    picks[...] = pick
    total = jnp.zeros((TOK, 1), F32)
    for at in range(0, D, 640):
        part = stream[:, at:at + 640].astype(F32)
        total = total + jnp.sum(part * part, axis=1, keepdims=True)
    scale = lax.rsqrt(total / D + EPSILON)
    for chunk in range(IN_CHUNKS):
        for at in range(0, DI, 640):
            cols = slice(chunk * DI + at, chunk * DI + at + 640)
            normed = stream[:, cols].astype(F32) * scale * gain[:, cols]
            routed = out_grad[:, cols].astype(F32) * weight[...]
            both = jnp.concatenate([normed.astype(BF16), routed.astype(BF16)], axis=0)
            rows[chunk][:, at:at + 640] = tn(pick, both).astype(BF16)


def dispatch(stream, out_grad, weight, ids, gain):
    return pl.pallas_call(
        dispatch_kernel,
        out_shape=[sds((TOK, DI))] * IN_CHUNKS + [sds((2 * TOK, 128))],
        in_specs=[VM] * 5,
        out_specs=[VM] * (IN_CHUNKS + 1),
        compiler_params=params(),
        name="dispatch",
    )(stream, out_grad, weight, ids, gain)


def split_rows():
    out = iota((128, 128), 0)
    inn = iota((128, 128), 1)
    want = ((out >> 5) & 1) * 64 + ((out >> 2) & 7) * 8 + (out >> 6) * 4 + (out & 3)
    return (inn == want).astype(BF16)


def project_kernel(first, last, counts, *refs):
    n_pieces = len(counts)
    pieces = refs[:n_pieces]
    w_gate, w_in, w_out = refs[n_pieces:n_pieces + 3]
    rest = refs[n_pieces + 3:]
    if not first:
        carried, rest = rest[:3], rest[3:]
    if last:
        outs, rest = rest[:2], rest[2:]
    else:
        outs, rest = rest[:3], rest[3:]
    x_at, r_at, gate, up, backed = rest
    step = pl.program_id(0)

    @pl.when(step == 0)
    def _():
        if first:
            gate[...] = jnp.zeros_like(gate)
            up[...] = jnp.zeros_like(up)
            backed[...] = jnp.zeros_like(backed)
        else:
            gate[...] = carried[0][...]
            up[...] = carried[1][...]
            backed[...] = carried[2][...]

    mover = split_rows()
    groups = []
    for ref, count in zip(pieces, counts):
        for at in range(count):
            groups.append(ref[at * 64:(at + 1) * 64, :])
    for at in range(0, len(groups), 2):
        moved = nn(mover, jnp.concatenate(groups[at:at + 2], axis=0)).astype(BF16)
        x_at[at * 32:at * 32 + 64, :] = moved[:64]
        r_at[at * 32:at * 32 + 64, :] = moved[64:]
    gate[...] += nn(x_at[...], w_gate[0])
    up[...] += nn(x_at[...], w_in[0])
    backed[...] += nt(r_at[...], w_out[0])

    @pl.when(step == pl.num_programs(0) - 1)
    def _():
        if last:
            sig = jax.nn.sigmoid(gate[...])
            outs[0][...] = (
                backed[...] * up[...] * sig * (1.0 + gate[...] * (1.0 - sig))
            ).astype(BF16)
            outs[1][...] = (backed[...] * gate[...] * sig).astype(BF16)
        else:
            outs[0][...] = gate[...]
            outs[1][...] = up[...]
            outs[2][...] = backed[...]


def project(chunk, pieces, carried, w_gate, w_in, w_out):
    first, last = chunk == 0, chunk == IN_CHUNKS - 1
    counts = tuple(p.shape[0] // 64 for p in pieces)
    base = chunk * (DI // KB)
    rows = sum(counts) * 32
    whole = pl.BlockSpec((rows, FFD), lambda i: (0, 0))
    in_specs = [pl.BlockSpec((p.shape[0], KB), lambda i: (0, i)) for p in pieces]
    in_specs += [
        pl.BlockSpec((1, KB, FFD), lambda i: (0, base + i, 0)),
        pl.BlockSpec((1, KB, FFD), lambda i: (0, base + i, 0)),
        pl.BlockSpec((1, FFD, KB), lambda i: (0, 0, base + i)),
    ]
    in_specs += [whole] * len(carried)
    outs = [sds((rows, FFD))] * 2 if last else [sds((rows, FFD), F32)] * 3
    return pl.pallas_call(
        functools.partial(project_kernel, first, last, counts),
        grid=(DI // KB,),
        out_shape=outs,
        in_specs=in_specs,
        out_specs=[whole] * len(outs),
        scratch_shapes=[pltpu.VMEM((rows, KB), BF16)] * 2 + [pltpu.VMEM((rows, FFD), F32)] * 3,
        compiler_params=params(),
        cost_estimate=pl.CostEstimate(
            flops=6 * rows * DI * FFD, bytes_accessed=30 * 1024 * 1024 // IN_CHUNKS, transcendentals=0
        ),
        name="project",
    )(*pieces, w_gate, w_in, w_out, *carried)


TERM_ROWS = (64, 64, 64, 64, 128, 128)


def term_kernel(grad_gate, grad_up, w_gate, w_in, *outs):
    block = nt(grad_gate[...], w_gate[0]) + nt(grad_up[...], w_in[0])
    block = block.astype(BF16)
    at = 0
    for ref, rows in zip(outs, TERM_ROWS):
        ref[...] = block[at:at + rows]
        at += rows


def terms(chunk, grad_gate, grad_up, w_gate, w_in):
    base = chunk * (DO // KB)
    whole = pl.BlockSpec(grad_gate.shape, lambda i: (0, 0))
    weight = pl.BlockSpec((1, KB, FFD), lambda i: (0, base + i, 0))
    return pl.pallas_call(
        term_kernel,
        grid=(DO // KB,),
        out_shape=[sds((r, DO)) for r in TERM_ROWS],
        in_specs=[whole, whole, weight, weight],
        out_specs=[pl.BlockSpec((r, KB), lambda i: (0, i)) for r in TERM_ROWS],
        compiler_params=params(),
        cost_estimate=pl.CostEstimate(
            flops=4 * 512 * DO * FFD, bytes_accessed=16 * 1024 * 1024 // OUT_CHUNKS, transcendentals=0
        ),
        name="terms",
    )(grad_gate, grad_up, w_gate, w_in)


def settle_kernel(a_own, a_swap, b_own, b1, b3, b2, out):
    half = DO // 2
    a = a_own[...] + a_swap[...].astype(F32)
    b = b_own[...] + b1[...].astype(F32) + b3[...].astype(F32) + b2[...].astype(F32)
    both = jnp.concatenate([a, b], axis=0).astype(BF16)
    stacked = jnp.concatenate([both[:, :half], both[:, half:]], axis=0)
    o = iota((128, 128), 0)
    want = ((o >> 2) & 1) * 64 + (o >> 3) * 4 + (o & 3)
    mover = (iota((128, 128), 1) == want).astype(BF16)
    out[...] = nn(mover, stacked).astype(BF16)


def settle(*args):
    return pl.pallas_call(
        settle_kernel,
        out_shape=sds((128, DO // 2)),
        in_specs=[VM] * 6,
        out_specs=VM,
        compiler_params=params(),
        name="settle",
    )(*args)


def finish_kernel(stream, out_grad, gain, picks, *refs):
    parts, (grad, grad_cut, scaled) = refs[:OUT_CHUNKS], refs[OUT_CHUNKS:]
    half = DO // 2
    square = jnp.zeros((TOK, 1), F32)
    dots = jnp.zeros((TOK, 1), F32)
    for chunk in range(OUT_CHUNKS):
        for at in range(0, half, 640):
            got = nn(picks[...], parts[chunk][:, at:at + 640])
            for side in range(2):
                cols = slice(chunk * DO + side * half + at, chunk * DO + side * half + at + 640)
                x = stream[:, cols].astype(F32)
                u = got[side * TOK:(side + 1) * TOK] * gain[:, cols]
                square = square + jnp.sum(x * x, axis=1, keepdims=True)
                dots = dots + jnp.sum(x * u, axis=1, keepdims=True)
                scaled[:, cols] = u
    r = lax.rsqrt(square / D + EPSILON)
    coef = dots * (r * r * r) / D
    for group in range(KVH):
        cols = slice(group * GW, (group + 1) * GW)
        x = stream[:, cols].astype(F32)
        total = out_grad[:, cols].astype(F32) + (scaled[:, cols] * r - x * coef)
        total = total.astype(BF16)
        grad[:, cols] = total
        grad_cut[group] = total


def finish(stream, out_grad, gain, picks, parts):
    return pl.pallas_call(
        finish_kernel,
        out_shape=[sds((TOK, D)), sds((KVH, TOK, GW))],
        in_specs=[VM] * (4 + len(parts)),
        out_specs=[VM] * 2,
        scratch_shapes=[pltpu.VMEM((TOK, D), F32)],
        compiler_params=params(),
        name="finish",
    )(stream, out_grad, gain, picks, *parts)


def probs_kernel(order, rows, probs, q_out, kv_out, q_at, kv_at):
    head = pl.program_id(0)

    @pl.when(head == 0)
    def _():
        for s in range(SPANS):
            to = pl.ds(pl.multiple_of(order[s] * SPAN, SPAN), SPAN)
            block = rows[s * SPAN:(s + 1) * SPAN, :]
            for g in range(GROUP):
                q_at[g, to, :] = block[:, g * DH:(g + 1) * DH]
            kv_at[0, to, :] = block[:, GW:GW + DH]
            kv_at[1, to, :] = block[:, GW + DH:GW + 2 * DH]
        q_out[...] = q_at[...]
        kv_out[...] = kv_at[...]

    for i in range(NQ):
        n = QB * (i + 1)
        q = q_at[head, i * QB:n, :]
        scores = nt(kv_at[0, 0:n, :], q) * FACTOR
        visible = iota((n, QB), 0) <= iota((n, QB), 1) + i * QB
        scores = jnp.where(visible, scores, -1e30)
        peak = jnp.max(scores, axis=0, keepdims=True)
        weights = jnp.exp(scores - peak)
        weights = weights / jnp.sum(weights, axis=0, keepdims=True)
        probs[0, i, 0:n, :] = weights.astype(BF16)


def make_probs(order, rows):
    return pl.pallas_call(
        probs_kernel,
        grid_spec=pltpu.PrefetchScalarGridSpec(
            num_scalar_prefetch=1,
            grid=(GROUP,),
            in_specs=[pl.BlockSpec((SEQ, GW + 2 * DH), lambda h, o: (0, 0))],
            out_specs=[
                pl.BlockSpec((1, NQ, SEQ, QB), lambda h, o: (h, 0, 0, 0)),
                pl.BlockSpec((GROUP, SEQ, DH), lambda h, o: (0, 0, 0)),
                pl.BlockSpec((2, SEQ, DH), lambda h, o: (0, 0, 0)),
            ],
            scratch_shapes=[
                pltpu.VMEM((GROUP, SEQ, DH), BF16),
                pltpu.VMEM((2, SEQ, DH), BF16),
            ],
        ),
        out_shape=[
            sds((GROUP, NQ, SEQ, QB)),
            sds((GROUP, SEQ, DH)),
            sds((2, SEQ, DH)),
        ],
        compiler_params=params(),
        cost_estimate=pl.CostEstimate(
            flops=2 * GROUP * SEQ * SEQ * DH, bytes_accessed=14 * 1024 * 1024, transcendentals=GROUP * SEQ * SEQ
        ),
        name="probs",
    )(order, rows)


def attend_kernel(order, probs, q, kv, grads, out, g_at, kt_at, dq_at, dk_at, dv_at):
    head = pl.program_id(0)

    @pl.when(head == 0)
    def _():
        for s in range(SPANS):
            to = pl.ds(pl.multiple_of(order[s] * SPAN, SPAN), SPAN)
            block = grads[s * SPAN:(s + 1) * SPAN, :]
            for g in range(GROUP):
                g_at[g, to, :] = block[:, g * DH:(g + 1) * DH]
        kt_at[...] = kv[0].T
        dk_at[...] = jnp.zeros_like(dk_at)
        dv_at[...] = jnp.zeros_like(dv_at)

    for i in range(NQ):
        n = QB * (i + 1)
        g_i = g_at[head, i * QB:n, :]
        q_i = q[head, i * QB:n, :]
        p_b = probs[0, i, 0:n, :]
        p = p_b.astype(F32)
        dp = nt(kv[1, 0:n, :], g_i)
        delta = jnp.sum(p * dp, axis=0, keepdims=True)
        ds = (p * (dp - delta)).astype(BF16)
        dv_at[0:n, :] += nn(p_b, g_i)
        dk_at[0:n, :] += nn(ds, q_i)
        dq_at[i * QB:n, :] = (nn(kt_at[:, 0:n], ds) * FACTOR).T.astype(BF16)
    for s in range(SPANS):
        at = pl.ds(pl.multiple_of(order[s] * SPAN, SPAN), SPAN)
        to = slice(s * SPAN, (s + 1) * SPAN)
        out[to, pl.ds(pl.multiple_of(head * DH, DH), DH)] = dq_at[at, :]

    @pl.when(head == GROUP - 1)
    def _():
        for s in range(SPANS):
            at = pl.ds(pl.multiple_of(order[s] * SPAN, SPAN), SPAN)
            to = slice(s * SPAN, (s + 1) * SPAN)
            out[to, GW:GW + DH] = (dk_at[at, :] * FACTOR).astype(BF16)
            out[to, GW + DH:GW + 2 * DH] = dv_at[at, :].astype(BF16)


def attend(order, probs, q, kv, grads):
    return pl.pallas_call(
        attend_kernel,
        grid_spec=pltpu.PrefetchScalarGridSpec(
            num_scalar_prefetch=1,
            grid=(GROUP,),
            in_specs=[
                pl.BlockSpec((1, NQ, SEQ, QB), lambda h, o: (h, 0, 0, 0)),
                pl.BlockSpec((GROUP, SEQ, DH), lambda h, o: (0, 0, 0)),
                pl.BlockSpec((2, SEQ, DH), lambda h, o: (0, 0, 0)),
                pl.BlockSpec((SEQ, GW), lambda h, o: (0, 0)),
            ],
            out_specs=pl.BlockSpec((SEQ, GW + 2 * DH), lambda h, o: (0, 0)),
            scratch_shapes=[
                pltpu.VMEM((GROUP, SEQ, DH), BF16),
                pltpu.VMEM((DH, SEQ), BF16),
                pltpu.VMEM((SEQ, DH), BF16),
                pltpu.VMEM((SEQ, DH), F32),
                pltpu.VMEM((SEQ, DH), F32),
            ],
        ),
        out_shape=sds((SEQ, GW + 2 * DH)),
        compiler_params=params(),
        cost_estimate=pl.CostEstimate(
            flops=8 * GROUP * SEQ * SEQ * DH, bytes_accessed=16 * 1024 * 1024, transcendentals=0
        ),
        name="attend",
    )(order, probs, q, kv, grads)


def along_z(x, shift):
    pairs = [(c, ((c // 2 + shift) % 4) * 2 + c % 2) for c in range(8)]
    return lax.ppermute(x, "ctx", pairs)


def across_x(x):
    return lax.ppermute(x, "ctx", [(c, c ^ 1) for c in range(8)])


def gather_pieces(shard):
    a, b = shard[:64], shard[64:]
    a_x = across_x(a)
    b_z = [along_z(b, k) for k in SHIFTS]
    a_both = jnp.concatenate([a, a_x], axis=0)
    a_z = [along_z(a_both, k) for k in SHIFTS]
    b_x = [across_x(p) for p in [b] + b_z]
    return [a_both] + a_z + [b] + b_z + b_x


def scatter_sums(groups):
    a_own, b_own, b_far = groups[0], groups[4], groups[5]
    b_got = across_x(b_far)
    a_got = [along_z(g, -k) for g, k in zip(groups[1:4], SHIFTS)]
    b_sum = b_own.astype(F32) + b_got.astype(F32)
    b_low = b_sum.astype(BF16)
    b_back = [
        along_z(b_low[32 * (at + 1):32 * (at + 2)], -k) for at, k in enumerate(SHIFTS)
    ]
    a_sum = a_own.astype(F32)
    for got in a_got:
        a_sum = a_sum + got.astype(F32)
    a_swap = across_x(a_sum[32:].astype(BF16))
    return settle(a_sum[:32], a_swap, b_sum[:32], *b_back)


def swap_exp(x):
    return lax.all_to_all(x, "exp", split_axis=0, concat_axis=0, tiled=True)


def swap_ctx(x):
    return lax.all_to_all(x, "ctx", split_axis=0, concat_axis=0, tiled=True)


def body(
    query_rows,
    key_rows,
    value_rows,
    stream,
    out_grad,
    route_weight,
    expert_ids,
    span_order,
    norm_gain,
    expert_gate,
    expert_in,
    expert_out,
):
    gain = norm_gain.reshape(1, D)
    by_head = jnp.concatenate(
        [
            query_rows[0].reshape(TOK, KVH, GW),
            key_rows[0].reshape(TOK, KVH, DH),
            value_rows[0].reshape(TOK, KVH, DH),
        ],
        axis=2,
    ).transpose(1, 0, 2)
    *outgoing, picks = dispatch(
        stream[0], out_grad[0], route_weight.reshape(TOK, 1), expert_ids[0], gain
    )
    qkv = swap_ctx(by_head).reshape(SEQ, GW + 2 * DH)
    shards = [swap_exp(o.reshape(EXPERTS, 8, DI)).reshape(TOK, DI) for o in outgoing]
    probs, q_sorted, kv_sorted = make_probs(span_order, qkv)
    carried = []
    for chunk, shard in enumerate(shards):
        carried = project(
            chunk, gather_pieces(shard), carried, expert_gate, expert_in, expert_out
        )
    grad_gate, grad_up = carried
    parts = []
    for chunk in range(OUT_CHUNKS):
        settled = scatter_sums(terms(chunk, grad_gate, grad_up, expert_gate, expert_in))
        parts.append(swap_exp(settled.reshape(EXPERTS, 8, DO // 2)).reshape(TOK, DO // 2))
    grad_total, grad_cut = finish(stream[0], out_grad[0], gain, picks, parts)
    grads = swap_ctx(grad_cut).reshape(SEQ, GW)
    result = attend(span_order, probs, q_sorted, kv_sorted, grads)
    back = swap_ctx(result.reshape(KVH, TOK, GW + 2 * DH)).transpose(1, 0, 2)
    return (
        grad_total[None],
        back[:, :, :GW].reshape(1, TOK, D),
        back[:, :, GW:GW + DH].reshape(1, TOK, KVH * DH),
        back[:, :, GW + DH:].reshape(1, TOK, KVH * DH),
    )


def solution(mesh):
    rows = P("exp", "ctx", None)
    return jax.shard_map(
        body,
        mesh=mesh,
        in_specs=(
            rows,
            rows,
            rows,
            rows,
            rows,
            P("exp", "ctx"),
            rows,
            P(),
            P(),
            P("exp", None, "ctx"),
            P("exp", None, "ctx"),
            rows,
        ),
        out_specs=(rows, rows, rows, rows),
        check_vma=False,
    )
```

time: 540 us -> 331 us (0.61)
  waiting for transfers between devices: 284 us -> 118 us
  matrix products: 87.3 us -> 0 us
  local copies, waits for them, and re-layouts: 80 us -> 11.2 us
  Pallas kernels: 0 us -> 63.5 us
  starting transfers between devices: 38.1 us -> 88.1 us
  blocking collectives: 0 us -> 45.9 us
  other arithmetic: 33.9 us -> 2.28 us
  between operations: 14.1 us -> 1.01 us
    reduce_scatter x2 -> x0, waiting for transfers between devices: 124 us -> none  [the longest x1 78.2 us: body(): lax.psum_scatter(value_part[None].astype(jnp.bfloat16), 'ctx', scatter_di...]
    all_to_all x2 -> x5, waiting for transfers between devices: 161 us -> 40.6 us  [the longest x2 30.8 us: swap_ctx(): return lax.all_to_all(x, 'ctx', split_axis=0, concat_axis=0, tiled=True)]
    ppermute x0 -> x38, waiting for transfers between devices: none -> 77.1 us  [the longest x14 40.8 us: across_x(): return lax.ppermute(x, 'ctx', [(c, c ^ 1) for c in range(8)])]
    dot_general x11 -> x0, matrix products: 75.1 us -> none  [the longest x1 12.7 us: attend_rows(): jnp.einsum('tkgd,skd->kgts', grad_heads, values_r, preferred_element_type...]
    ppermute x0 -> x38, starting transfers between devices: none -> 65.7 us  [the longest x24 40 us: along_z(): return lax.ppermute(x, 'ctx', pairs)]
    pallas_call x0 -> x10, Pallas kernels: none -> 63.5 us  [the longest x2 20.3 us: project(): pl.pallas_call(functools.partial(project_kernel, first, last, counts), gr...]
    all_to_all x0 -> x2, blocking collectives: none -> 45.9 us  [the longest x1 28.2 us: swap_ctx(): return lax.all_to_all(x, 'ctx', split_axis=0, concat_axis=0, tiled=True)]
    convert_element_type x6 -> x2, other arithmetic: 23.9 us -> 0.38 us  [scatter_sums(): b_low = b_sum.astype(BF16)]
  transfers between devices with their start and end apart: 6 -> 43, of which waited for: 4 -> 25; matrix products, arithmetic and copies ran while one was open for 28% -> 1% of each run, Pallas kernels for 0% -> 9%
where the time goes in v1:
time: 331 us; the launch traced here: 330 us
  waiting for transfers between devices  118 us (36%)
  starting transfers between devices  88.1 us (27%)
  Pallas kernels  63.5 us (19%)
  blocking collectives  45.9 us (14%)
  local copies, waits for them, and re-layouts  11.2 us (3%)
    ppermute x14, waiting for transfers between devices, across_x(): return lax.ppermute(x, 'ctx', [(c, c ^ 1) for c in range(8)])  40.8 us
    ppermute x24, starting transfers between devices, along_z(): return lax.ppermute(x, 'ctx', pairs)  40 us
    ppermute x24, waiting for transfers between devices, along_z(): return lax.ppermute(x, 'ctx', pairs)  36.3 us
    all_to_all x2, waiting for transfers between devices, swap_ctx(): return lax.all_to_all(x, 'ctx', split_axis=0, concat_axis=0, tiled=True)  30.8 us
    all_to_all x1, blocking collectives, swap_ctx(): return lax.all_to_all(x, 'ctx', split_axis=0, concat_axis=0, tiled=True)  28.2 us
    ppermute x14, starting transfers between devices, across_x(): return lax.ppermute(x, 'ctx', [(c, c ^ 1) for c in range(8)])  25.7 us
    pallas_call x2, Pallas kernels, project(): pl.pallas_call(functools.partial(project_kernel, first, last, counts), gr...  20.3 us
    all_to_all x1, blocking collectives, swap_exp(): return lax.all_to_all(x, 'exp', split_axis=0, concat_axis=0, tiled=True)  17.7 us
  transfers between devices with their start and end apart: 43, of which 25 were waited for; matrix products, arithmetic and copies ran while one was open for 1% of the time, Pallas kernels for 9%

profile of v1, /device:TPU:0, one launch (start us, length us, event | category | flops | bytes accessed | tf_op | source)
XLA Modules:
  0.0 329.7 jit_solution(10112575952782024405)
XLA Ops:
  5.5 2.0 dispatch.1
  7.5 17.7 %all_to_all.35 = bf16[16,8,2560]{2,1,0:T(8,128)(2,1)S(1)} all-to-all(bf16[16,8,2560]{2,1,0:T(8,128)(2,1)S(1)} %bitcast.43), channel_id=1, replica_groups=mesh['ctx'=8,'exp'=16] {'exp'}, dimensions={0} | all-to-all | bytes 1310720 | tf_op jit(solution)/shard_map/all_to_all | solution.py:445
  25.3 3.6 %all-to-all-start = ((bf16[16,8,2560]{2,1,0:T(8,128)(2,1)}), bf16[16,8,2560]{2,1,0:T(8,128)(2,1)S(1)}, u32[]{:S(2)}, u32[]{:S(2)}) async-start(bf16[16,8,2560]{2,1,0:T(8,128)(2,1)} %bitcast.5), calls=%async_computation | async-start | bytes 1310720 | tf_op jit(solution)/shard_map/all_to_all | solution.py:445
  28.9 2.8 collective-permute-start.18
  31.7 3.9 %collective-permute-start.17 = (bf16[64,2560]{1,0:T(8,128)(2,1)S(1)}, bf16[64,2560]{1,0:T(8,128)(2,1)S(1)}, u32[]{:S(2)}, u32[]{:S(2)}) collective-permute-start(bf16[64,2560]{1,0:T(8,128)(2,1)S(1)} %get-tuple-element.66.refs_4_), channel_id=1, source_target_pairs={{0,64},{16,80},{32,96},{48,112},{64,0},{80,16},{96,32},{112,48},{1... | collective-permute-start | bytes 983048 | tf_op jit(solution)/shard_map/ppermute | solution.py:411
  38.4 3.2 all-to-all-done
  41.6 12.4 %collective-permute-done.11 = bf16[64,2560]{1,0:T(8,128)(2,1)S(1)} collective-permute-done((bf16[64,2560]{1,0:T(8,128)(2,1)S(1)}, bf16[64,2560]{1,0:T(8,128)(2,1)S(1)}, u32[]{:S(2)}, u32[]{:S(2)}) %collective-permute-start.11) | collective-permute-done | bytes 327712 | tf_op jit(solution)/shard_map/ppermute | solution.py:415
  54.8 2.7 collective-permute-start.7
  57.6 3.9 %collective-permute-start.6 = (bf16[64,2560]{1,0:T(8,128)(2,1)S(1)}, bf16[64,2560]{1,0:T(8,128)(2,1)S(1)}, u32[]{:S(2)}, u32[]{:S(2)}) collective-permute-start(bf16[64,2560]{1,0:T(8,128)(2,1)S(1)} %get-tuple-element.68.refs_4_), channel_id=1, source_target_pairs={{0,64},{16,80},{32,96},{48,112},{64,0},{80,16},{96,32},{112,48},{1... | collective-permute-start | bytes 983048 | tf_op jit(solution)/shard_map/ppermute | solution.py:411
  63.5 2.7 collective-permute-done
  66.9 6.2 %collective-permute-done.7.refs_8_ = bf16[64,2560]{1,0:T(8,128)(2,1)S(1)} collective-permute-done((bf16[64,2560]{1,0:T(8,128)(2,1)S(1)}, bf16[64,2560]{1,0:T(8,128)(2,1)S(1)}, u32[]{:S(2)}, u32[]{:S(2)}) %collective-permute-start.7) | collective-permute-done | bytes 327712 | tf_op jit(solution)/shard_map/ppermute | solution.py:415
  74.0 4.0 %collective-permute-start.14 = (bf16[128,2560]{1,0:T(8,128)(2,1)S(1)}, bf16[128,2560]{1,0:T(8,128)(2,1)S(1)}, u32[]{:S(2)}, u32[]{:S(2)}) collective-permute-start(bf16[128,2560]{1,0:T(8,128)(2,1)S(1)} %pad_maximum_fusion.1.refs_0_), channel_id=1, source_target_pairs={{0,64},{16,80},{32,96},{48,112},{64,0},{80,16},{96,32},{112,48},{1... | collective-permute-start | bytes 1966088 | tf_op jit(solution)/shard_map/ppermute | solution.py:411
  80.2 2.6 collective-permute-start.19
  82.7 4.5 %collective-permute-done.20.refs_10_ = bf16[64,2560]{1,0:T(8,128)(2,1)S(1)} collective-permute-done((bf16[64,2560]{1,0:T(8,128)(2,1)S(1)}, bf16[64,2560]{1,0:T(8,128)(2,1)S(1)}, u32[]{:S(2)}, u32[]{:S(2)}) %collective-permute-start.20) | collective-permute-done | bytes 327712 | tf_op jit(solution)/shard_map/ppermute | solution.py:415
  88.1 6.2 %collective-permute-done.19.refs_9_ = bf16[64,2560]{1,0:T(8,128)(2,1)S(1)} collective-permute-done((bf16[64,2560]{1,0:T(8,128)(2,1)S(1)}, bf16[64,2560]{1,0:T(8,128)(2,1)S(1)}, u32[]{:S(2)}, u32[]{:S(2)}) %collective-permute-start.19) | collective-permute-done | bytes 327712 | tf_op jit(solution)/shard_map/ppermute | solution.py:415
  94.2 3.9 %collective-permute-start.3 = (bf16[128,2560]{1,0:T(8,128)(2,1)S(1)}, bf16[128,2560]{1,0:T(8,128)(2,1)S(1)}, u32[]{:S(2)}, u32[]{:S(2)}) collective-permute-start(bf16[128,2560]{1,0:T(8,128)(2,1)S(1)} %pad_maximum_fusion.refs_0_), channel_id=1, source_target_pairs={{0,64},{16,80},{32,96},{48,112},{64,0},{80,16},{96,32},{112,48},{1... | collective-permute-start | bytes 1966088 | tf_op jit(solution)/shard_map/ppermute | solution.py:411
  100.1 4.0 %collective-permute-start.2 = (bf16[128,2560]{1,0:T(8,128)(2,1)S(1)}, bf16[128,2560]{1,0:T(8,128)(2,1)S(1)}, u32[]{:S(2)}, u32[]{:S(2)}) collective-permute-start(bf16[128,2560]{1,0:T(8,128)(2,1)S(1)} %pad_maximum_fusion.refs_0_), channel_id=1, source_target_pairs={{0,96},{16,112},{32,0},{48,16},{64,32},{80,48},{96,64},{112,80},{1... | collective-permute-start | bytes 1966088 | tf_op jit(solution)/shard_map/ppermute | solution.py:411
  104.1 4.6 %collective-permute-done.13.refs_2_ = bf16[128,2560]{1,0:T(8,128)(2,1)S(1)} collective-permute-done((bf16[128,2560]{1,0:T(8,128)(2,1)S(1)}, bf16[128,2560]{1,0:T(8,128)(2,1)S(1)}, u32[]{:S(2)}, u32[]{:S(2)}) %collective-permute-start.13) | collective-permute-done | bytes 655392 | tf_op jit(solution)/shard_map/ppermute | solution.py:411
  108.7 2.7 collective-permute-start.9
  112.3 10.4 %project.2 = (f32[512,512]{1,0:T(8,128)}, f32[512,512]{1,0:T(8,128)}, f32[512,512]{1,0:T(8,128)}) custom-call(bf16[128,2560]{1,0:T(8,128)(2,1)S(1)} %pad_maximum_fusion.1.refs_0_, bf16[128,2560]{1,0:T(8,128)(2,1)S(1)} %collective-permute-done.12.refs_1_, bf16[128,2560]{1,0:T(8,128)(2,1)S(1)} %collective-permute-done.13.refs_2_, ...), custom_call_target="tpu_custom_call" | custom-call | flops 4026531840 | bytes 15728640 | tf_op jit(solution)/shard_map/project/pallas_call | solution.py:176
  122.7 2.5 collective-permute-done.8.refs_9_
  125.2 8.1 %collective-permute-done.2.refs_2_ = bf16[128,2560]{1,0:T(8,128)(2,1)S(1)} collective-permute-done((bf16[128,2560]{1,0:T(8,128)(2,1)S(1)}, bf16[128,2560]{1,0:T(8,128)(2,1)S(1)}, u32[]{:S(2)}, u32[]{:S(2)}) %collective-permute-start.2) | collective-permute-done | bytes 655392 | tf_op jit(solution)/shard_map/ppermute | solution.py:411
  133.3 9.9 %project.3 = (bf16[512,512]{1,0:T(8,128)(2,1)S(1)}, bf16[512,512]{1,0:T(8,128)(2,1)S(1)}) custom-call(bf16[128,2560]{1,0:T(8,128)(2,1)S(1)} %pad_maximum_fusion.refs_0_, bf16[128,2560]{1,0:T(8,128)(2,1)S(1)} %collective-permute-done.1.refs_1_, bf16[128,2560]{1,0:T(8,128)(2,1)S(1)} %collective-permute-done.2.refs_2_, bf16[128,2560]{1,0:T(8,128)(2,1)} %copy-done.9, ...), custom_call_target="tpu_custom_call" | custom-call | flops 4026531840 | bytes 15728640 | tf_op jit(solution)/shard_map/project/pallas_call | solution.py:176
  143.3 6.0 %terms.3 = (bf16[64,2560]{1,0:T(8,128)(2,1)S(1)}, bf16[64,2560]{1,0:T(8,128)(2,1)S(1)}, bf16[64,2560]{1,0:T(8,128)(2,1)S(1)}, bf16[64,2560]{1,0:T(8,128)(2,1)S(1...) custom-call(bf16[512,512]{1,0:T(8,128)(2,1)S(1)} %get-tuple-element.35.grad_gate, ...), custom_call_target="tpu_custom_call" | custom-call | flops 2684354560 | bytes 8388608 | tf_op jit(solution)/shard_map/terms/pallas_call | solution.py:207
  149.3 2.7 collective-permute-start.30
  153.8 2.7 collective-permute-start.34
  156.5 6.0 %terms.2 = (bf16[64,2560]{1,0:T(8,128)(2,1)S(1)}, bf16[64,2560]{1,0:T(8,128)(2,1)S(1)}, bf16[64,2560]{1,0:T(8,128)(2,1)S(1)}, bf16[64,2560]{1,0:T(8,128)(2,1)S(1...) custom-call(bf16[512,512]{1,0:T(8,128)(2,1)S(1)} %get-tuple-element.35.grad_gate, ...), custom_call_target="tpu_custom_call" | custom-call | flops 2684354560 | bytes 8388608 | tf_op jit(solution)/shard_map/terms/pallas_call | solution.py:207
  164.0 3.1 collective-permute-done.30
  167.1 2.5 collective-permute-done.31
  169.6 2.7 collective-permute-start.24
  172.2 2.7 collective-permute-start.26
  175.2 5.0 %collective-permute-done.22 = bf16[64,2560]{1,0:T(8,128)(2,1)S(1)} collective-permute-done((bf16[64,2560]{1,0:T(8,128)(2,1)S(1)}, bf16[64,2560]{1,0:T(8,128)(2,1)S(1)}, u32[]{:S(2)}, u32[]{:S(2)}) %collective-permute-start.22) | collective-permute-done | bytes 327712 | tf_op jit(solution)/shard_map/ppermute | solution.py:411
  180.2 2.7 collective-permute-start.33
  182.9 2.2 collective-permute-done.24
  188.9 2.5 collective-permute-done.26
  197.7 5.1 %all-to-all-start.3 = ((bf16[16,8,1280]{2,1,0:T(8,128)(2,1)}), bf16[16,8,1280]{2,1,0:T(8,128)(2,1)S(1)}, u32[]{:S(2)}, u32[]{:S(2)}) async-start(bf16[16,8,1280]{2,1,0:T(8,128)(2,1)} %bitcast.13), calls=%async_computation.3 | async-start | bytes 655360 | tf_op jit(solution)/shard_map/all_to_all | solution.py:445
  207.1 4.4 %collective-permute-done.29.b2 = bf16[32,2560]{1,0:T(8,128)(2,1)S(1)} collective-permute-done((bf16[32,2560]{1,0:T(8,128)(2,1)S(1)}, bf16[32,2560]{1,0:T(8,128)(2,1)S(1)}, u32[]{:S(2)}, u32[]{:S(2)}) %collective-permute-start.29) | collective-permute-done | bytes 163872 | tf_op jit(solution)/shard_map/ppermute | solution.py:411
  211.5 3.0 collective-permute-done.28.b3
  215.5 5.6 %all-to-all-start.2 = ((bf16[16,8,1280]{2,1,0:T(8,128)(2,1)}), bf16[16,8,1280]{2,1,0:T(8,128)(2,1)S(1)}, u32[]{:S(2)}, u32[]{:S(2)}) async-start(bf16[16,8,1280]{2,1,0:T(8,128)(2,1)} %bitcast.11), calls=%async_computation.2 | async-start | bytes 655360 | tf_op jit(solution)/shard_map/all_to_all | solution.py:445
  223.2 6.6 %all-to-all-done.2 = bf16[16,8,1280]{2,1,0:T(8,128)(2,1)S(1)} async-done(((bf16[16,8,1280]{2,1,0:T(8,128)(2,1)}), bf16[16,8,1280]{2,1,0:T(8,128)(2,1)S(1)}, u32[]{:S(2)}, u32[]{:S(2)}) %all-to-all-start.2) | async-done | bytes 327712 | tf_op jit(solution)/shard_map/all_to_all | solution.py:445
  229.9 4.4 %all-to-all-start.4 = ((bf16[8,128,896]{2,1,0:T(8,128)(2,1)}), bf16[8,128,896]{2,1,0:T(8,128)(2,1)}, u32[]{:S(2)}, u32[]{:S(2)}) async-start(bf16[8,128,896]{2,1,0:T(8,128)(2,1)} %maximum_bitcast_fusion), calls=%async_computation.4 | async-start | bytes 3670016 | tf_op jit(solution)/shard_map/all_to_all | solution.py:449
  234.3 2.9 finish.1
  238.3 21.4 %all-to-all-done.4 = bf16[8,128,896]{2,1,0:T(8,128)(2,1)} async-done(((bf16[8,128,896]{2,1,0:T(8,128)(2,1)}), bf16[8,128,896]{2,1,0:T(8,128)(2,1)}, u32[]{:S(2)}, u32[]{:S(2)}) %all-to-all-start.4) | async-done | bytes 1835040 | tf_op jit(solution)/shard_map/all_to_all | solution.py:449
  259.7 3.7 %all-to-all-start.5 = ((bf16[8,128,640]{2,1,0:T(8,128)(2,1)}), bf16[8,128,640]{2,1,0:T(8,128)(2,1)S(1)}, u32[]{:S(2)}, u32[]{:S(2)}) async-start(bf16[8,128,640]{2,1,0:T(8,128)(2,1)} %copy-done.4), calls=%async_computation.5 | async-start | bytes 2621440 | tf_op jit(solution)/shard_map/all_to_all | solution.py:449
  263.4 9.8 %probs.1 = (bf16[5,4,1024,256]{3,2,1,0:T(8,128)(2,1)}, bf16[5,1024,128]{2,1,0:T(8,128)(2,1)S(1)}, bf16[2,1024,128]{2,1,0:T(8,128)(2,1)S(1)}) custom-call(s32[16]{0:T(128)S(1)} %copy-done.7, bf16[1024,896]{1,0:T(8,128)(2,1)} %bitcast.17.rows), custom_call_target="tpu_custom_call" | custom-call | flops 1342177280 | bytes 14680064 | tf_op jit(solution)/shard_map/probs/pallas_call | solution.py:310
  273.2 9.4 %all-to-all-done.5 = bf16[8,128,640]{2,1,0:T(8,128)(2,1)S(1)} async-done(((bf16[8,128,640]{2,1,0:T(8,128)(2,1)}), bf16[8,128,640]{2,1,0:T(8,128)(2,1)S(1)}, u32[]{:S(2)}, u32[]{:S(2)}) %all-to-all-start.5) | async-done | bytes 1310752 | tf_op jit(solution)/shard_map/all_to_all | solution.py:449
  282.7 14.3 %attend.1 = bf16[1024,896]{1,0:T(8,128)(2,1)S(1)} custom-call(s32[16]{0:T(128)S(1)} %copy-done.7, bf16[5,4,1024,256]{3,2,1,0:T(8,128)(2,1)} %get-tuple-element.50.probs, bf16[5,1024,128]{2,1,0:T(8,128)(2,1)S(1)} %get-tuple-element.51.q, bf16[2,1024,128]{2,1,0:T(8,128)(2,1)S(1)} %get-tuple-element.52.kv, bf16[1024,640]{1,0:T(8,128)(2,1)S(1)} %bitcast.42), custom_call_target="tpu_custom_call" | custom-call | flops 5368709120 | bytes 16777216 | tf_op jit(solution)/shard_map/attend/pallas_call | solution.py:380
  297.0 28.2 %all_to_all.36 = bf16[8,128,896]{2,1,0:T(8,128)(2,1)S(1)} all-to-all(bf16[8,128,896]{2,1,0:T(8,128)(2,1)S(1)} %bitcast.39), channel_id=1, replica_groups=mesh['ctx'=8,'exp'=16] {'ctx'}, dimensions={0} | all-to-all | bytes 3670016 | tf_op jit(solution)/shard_map/all_to_all | solution.py:449
  (107 shorter events, 44.6 us)
Async XLA Ops:
  25.3 16.3 %all-to-all-start = ((bf16[16,8,2560]{2,1,0:T(8,128)(2,1)}), bf16[16,8,2560]{2,1,0:T(8,128)(2,1)S(1)}, u32[]{:S(2)}, u32[]{:S(2)}) async-start(bf16[16,8,2560]{2,1,0:T(8,128)(2,1)} %bitcast.5), calls=%async_computation | async-start | bytes 1310720 | tf_op jit(solution)/shard_map/all_to_all | solution.py:445
  28.9 25.9 %collective-permute-start.18 = (bf16[64,2560]{1,0:T(8,128)(2,1)S(1)}, bf16[64,2560]{1,0:T(8,128)(2,1)S(1)}, u32[]{:S(2)}, u32[]{:S(2)}) collective-permute-start(bf16[64,2560]{1,0:T(8,128)(2,1)S(1)} %get-tuple-element.66.refs_4_), channel_id=1, source_target_pairs={{0,16},{16,0},{32,48},{48,32},{64,80},{80,64},{96,112},{112,96},{1... | collective-permute-start | bytes 983048 | tf_op jit(solution)/shard_map/ppermute | solution.py:415
  31.7 25.9 %collective-permute-start.17 = (bf16[64,2560]{1,0:T(8,128)(2,1)S(1)}, bf16[64,2560]{1,0:T(8,128)(2,1)S(1)}, u32[]{:S(2)}, u32[]{:S(2)}) collective-permute-start(bf16[64,2560]{1,0:T(8,128)(2,1)S(1)} %get-tuple-element.66.refs_4_), channel_id=1, source_target_pairs={{0,64},{16,80},{32,96},{48,112},{64,0},{80,16},{96,32},{112,48},{1... | collective-permute-start | bytes 983048 | tf_op jit(solution)/shard_map/ppermute | solution.py:411
  35.6 25.9 %collective-permute-start.16 = (bf16[64,2560]{1,0:T(8,128)(2,1)S(1)}, bf16[64,2560]{1,0:T(8,128)(2,1)S(1)}, u32[]{:S(2)}, u32[]{:S(2)}) collective-permute-start(bf16[64,2560]{1,0:T(8,128)(2,1)S(1)} %get-tuple-element.66.refs_4_), channel_id=1, source_target_pairs={{0,96},{16,112},{32,0},{48,16},{64,32},{80,48},{96,64},{112,80},{1... | collective-permute-start | bytes 983048 | tf_op jit(solution)/shard_map/ppermute | solution.py:411
  36.3 25.9 %collective-permute-start.15 = (bf16[64,2560]{1,0:T(8,128)(2,1)S(1)}, bf16[64,2560]{1,0:T(8,128)(2,1)S(1)}, u32[]{:S(2)}, u32[]{:S(2)}) collective-permute-start(bf16[64,2560]{1,0:T(8,128)(2,1)S(1)} %get-tuple-element.66.refs_4_), channel_id=1, source_target_pairs={{0,32},{16,48},{32,64},{48,80},{64,96},{80,112},{96,0},{112,16},{1... | collective-permute-start | bytes 983048 | tf_op jit(solution)/shard_map/ppermute | solution.py:411
  37.6 16.4 %collective-permute-start.11 = (bf16[64,2560]{1,0:T(8,128)(2,1)S(1)}, bf16[64,2560]{1,0:T(8,128)(2,1)S(1)}, u32[]{:S(2)}, u32[]{:S(2)}) collective-permute-start(bf16[64,2560]{1,0:T(8,128)(2,1)S(1)} %get-tuple-element.67), channel_id=1, source_target_pairs={{0,16},{16,0},{32,48},{48,32},{64,80},{80,64},{96,112},{112,96},{1... | collective-permute-start | bytes 983048 | tf_op jit(solution)/shard_map/ppermute | solution.py:415
  54.0 12.1 %collective-permute-start = (bf16[64,2560]{1,0:T(8,128)(2,1)S(1)}, bf16[64,2560]{1,0:T(8,128)(2,1)S(1)}, u32[]{:S(2)}, u32[]{:S(2)}) collective-permute-start(bf16[64,2560]{1,0:T(8,128)(2,1)S(1)} %get-tuple-element.69), channel_id=1, source_target_pairs={{0,16},{16,0},{32,48},{48,32},{64,80},{80,64},{96,112},{112,96},{1... | collective-permute-start | bytes 983048 | tf_op jit(solution)/shard_map/ppermute | solution.py:415
  54.8 18.3 %collective-permute-start.7 = (bf16[64,2560]{1,0:T(8,128)(2,1)S(1)}, bf16[64,2560]{1,0:T(8,128)(2,1)S(1)}, u32[]{:S(2)}, u32[]{:S(2)}) collective-permute-start(bf16[64,2560]{1,0:T(8,128)(2,1)S(1)} %get-tuple-element.68.refs_4_), channel_id=1, source_target_pairs={{0,16},{16,0},{32,48},{48,32},{64,80},{80,64},{96,112},{112,96},{1... | collective-permute-start | bytes 983048 | tf_op jit(solution)/shard_map/ppermute | solution.py:415
  57.6 16.4 %collective-permute-start.6 = (bf16[64,2560]{1,0:T(8,128)(2,1)S(1)}, bf16[64,2560]{1,0:T(8,128)(2,1)S(1)}, u32[]{:S(2)}, u32[]{:S(2)}) collective-permute-start(bf16[64,2560]{1,0:T(8,128)(2,1)S(1)} %get-tuple-element.68.refs_4_), channel_id=1, source_target_pairs={{0,64},{16,80},{32,96},{48,112},{64,0},{80,16},{96,32},{112,48},{1... | collective-permute-start | bytes 983048 | tf_op jit(solution)/shard_map/ppermute | solution.py:411
  61.5 16.5 %collective-permute-start.5 = (bf16[64,2560]{1,0:T(8,128)(2,1)S(1)}, bf16[64,2560]{1,0:T(8,128)(2,1)S(1)}, u32[]{:S(2)}, u32[]{:S(2)}) collective-permute-start(bf16[64,2560]{1,0:T(8,128)(2,1)S(1)} %get-tuple-element.68.refs_4_), channel_id=1, source_target_pairs={{0,96},{16,112},{32,0},{48,16},{64,32},{80,48},{96,64},{112,80},{1... | collective-permute-start | bytes 983048 | tf_op jit(solution)/shard_map/ppermute | solution.py:411
  62.2 16.8 %collective-permute-start.4 = (bf16[64,2560]{1,0:T(8,128)(2,1)S(1)}, bf16[64,2560]{1,0:T(8,128)(2,1)S(1)}, u32[]{:S(2)}, u32[]{:S(2)}) collective-permute-start(bf16[64,2560]{1,0:T(8,128)(2,1)S(1)} %get-tuple-element.68.refs_4_), channel_id=1, source_target_pairs={{0,32},{16,48},{32,64},{48,80},{64,96},{80,112},{96,0},{112,16},{1... | collective-permute-start | bytes 983048 | tf_op jit(solution)/shard_map/ppermute | solution.py:411
  66.1 14.0 %collective-permute-start.21 = (bf16[64,2560]{1,0:T(8,128)(2,1)S(1)}, bf16[64,2560]{1,0:T(8,128)(2,1)S(1)}, u32[]{:S(2)}, u32[]{:S(2)}) collective-permute-start(bf16[64,2560]{1,0:T(8,128)(2,1)S(1)} %collective-permute-done.17.refs_7_), channel_id=1, source_target_pairs={{0,16},{16,0},{32,48},{48,32},{64,80},{80,64},{96,112},{112,96},{1... | collective-permute-start | bytes 983048 | tf_op jit(solution)/shard_map/ppermute | solution.py:415
  73.2 14.0 %collective-permute-start.20 = (bf16[64,2560]{1,0:T(8,128)(2,1)S(1)}, bf16[64,2560]{1,0:T(8,128)(2,1)S(1)}, u32[]{:S(2)}, u32[]{:S(2)}) collective-permute-start(bf16[64,2560]{1,0:T(8,128)(2,1)S(1)} %collective-permute-done.16.refs_6_), channel_id=1, source_target_pairs={{0,16},{16,0},{32,48},{48,32},{64,80},{80,64},{96,112},{112,96},{1... | collective-permute-start | bytes 983048 | tf_op jit(solution)/shard_map/ppermute | solution.py:415
  74.0 30.1 %collective-permute-start.14 = (bf16[128,2560]{1,0:T(8,128)(2,1)S(1)}, bf16[128,2560]{1,0:T(8,128)(2,1)S(1)}, u32[]{:S(2)}, u32[]{:S(2)}) collective-permute-start(bf16[128,2560]{1,0:T(8,128)(2,1)S(1)} %pad_maximum_fusion.1.refs_0_), channel_id=1, source_target_pairs={{0,64},{16,80},{32,96},{48,112},{64,0},{80,16},{96,32},{112,48},{1... | collective-permute-start | bytes 1966088 | tf_op jit(solution)/shard_map/ppermute | solution.py:411
  78.0 30.7 %collective-permute-start.13 = (bf16[128,2560]{1,0:T(8,128)(2,1)S(1)}, bf16[128,2560]{1,0:T(8,128)(2,1)S(1)}, u32[]{:S(2)}, u32[]{:S(2)}) collective-permute-start(bf16[128,2560]{1,0:T(8,128)(2,1)S(1)} %pad_maximum_fusion.1.refs_0_), channel_id=1, source_target_pairs={{0,96},{16,112},{32,0},{48,16},{64,32},{80,48},{96,64},{112,80},{1... | collective-permute-start | bytes 1966088 | tf_op jit(solution)/shard_map/ppermute | solution.py:411
  79.0 32.4 %collective-permute-start.12 = (bf16[128,2560]{1,0:T(8,128)(2,1)S(1)}, bf16[128,2560]{1,0:T(8,128)(2,1)S(1)}, u32[]{:S(2)}, u32[]{:S(2)}) collective-permute-start(bf16[128,2560]{1,0:T(8,128)(2,1)S(1)} %pad_maximum_fusion.1.refs_0_), channel_id=1, source_target_pairs={{0,32},{16,48},{32,64},{48,80},{64,96},{80,112},{96,0},{112,16},{1... | collective-permute-start | bytes 1966088 | tf_op jit(solution)/shard_map/ppermute | solution.py:411
  80.2 14.0 %collective-permute-start.19 = (bf16[64,2560]{1,0:T(8,128)(2,1)S(1)}, bf16[64,2560]{1,0:T(8,128)(2,1)S(1)}, u32[]{:S(2)}, u32[]{:S(2)}) collective-permute-start(bf16[64,2560]{1,0:T(8,128)(2,1)S(1)} %collective-permute-done.15.refs_5_), channel_id=1, source_target_pairs={{0,16},{16,0},{32,48},{48,32},{64,80},{80,64},{96,112},{112,96},{1... | collective-permute-start | bytes 983048 | tf_op jit(solution)/shard_map/ppermute | solution.py:415
  87.2 12.9 %collective-permute-start.10 = (bf16[64,2560]{1,0:T(8,128)(2,1)S(1)}, bf16[64,2560]{1,0:T(8,128)(2,1)S(1)}, u32[]{:S(2)}, u32[]{:S(2)}) collective-permute-start(bf16[64,2560]{1,0:T(8,128)(2,1)S(1)} %collective-permute-done.6.refs_7_), channel_id=1, source_target_pairs={{0,16},{16,0},{32,48},{48,32},{64,80},{80,64},{96,112},{112,96},{1... | collective-permute-start | bytes 983048 | tf_op jit(solution)/shard_map/ppermute | solution.py:415
  94.2 31.0 %collective-permute-start.3 = (bf16[128,2560]{1,0:T(8,128)(2,1)S(1)}, bf16[128,2560]{1,0:T(8,128)(2,1)S(1)}, u32[]{:S(2)}, u32[]{:S(2)}) collective-permute-start(bf16[128,2560]{1,0:T(8,128)(2,1)S(1)} %pad_maximum_fusion.refs_0_), channel_id=1, source_target_pairs={{0,64},{16,80},{32,96},{48,112},{64,0},{80,16},{96,32},{112,48},{1... | collective-permute-start | bytes 1966088 | tf_op jit(solution)/shard_map/ppermute | solution.py:411
  100.1 33.2 %collective-permute-start.2 = (bf16[128,2560]{1,0:T(8,128)(2,1)S(1)}, bf16[128,2560]{1,0:T(8,128)(2,1)S(1)}, u32[]{:S(2)}, u32[]{:S(2)}) collective-permute-start(bf16[128,2560]{1,0:T(8,128)(2,1)S(1)} %pad_maximum_fusion.refs_0_), channel_id=1, source_target_pairs={{0,96},{16,112},{32,0},{48,16},{64,32},{80,48},{96,64},{112,80},{1... | collective-permute-start | bytes 1966088 | tf_op jit(solution)/shard_map/ppermute | solution.py:411
  104.1 29.2 %collective-permute-start.1 = (bf16[128,2560]{1,0:T(8,128)(2,1)S(1)}, bf16[128,2560]{1,0:T(8,128)(2,1)S(1)}, u32[]{:S(2)}, u32[]{:S(2)}) collective-permute-start(bf16[128,2560]{1,0:T(8,128)(2,1)S(1)} %pad_maximum_fusion.refs_0_), channel_id=1, source_target_pairs={{0,32},{16,48},{32,64},{48,80},{64,96},{80,112},{96,0},{112,16},{1... | collective-permute-start | bytes 1966088 | tf_op jit(solution)/shard_map/ppermute | solution.py:411
  108.7 13.9 %collective-permute-start.9 = (bf16[64,2560]{1,0:T(8,128)(2,1)S(1)}, bf16[64,2560]{1,0:T(8,128)(2,1)S(1)}, u32[]{:S(2)}, u32[]{:S(2)}) collective-permute-start(bf16[64,2560]{1,0:T(8,128)(2,1)S(1)} %collective-permute-done.5.refs_6_), channel_id=1, source_target_pairs={{0,16},{16,0},{32,48},{48,32},{64,80},{80,64},{96,112},{112,96},{1... | collective-permute-start | bytes 983048 | tf_op jit(solution)/shard_map/ppermute | solution.py:415
  111.4 13.8 %collective-permute-start.8 = (bf16[64,2560]{1,0:T(8,128)(2,1)S(1)}, bf16[64,2560]{1,0:T(8,128)(2,1)S(1)}, u32[]{:S(2)}, u32[]{:S(2)}) collective-permute-start(bf16[64,2560]{1,0:T(8,128)(2,1)S(1)} %collective-permute-done.4.refs_5_), channel_id=1, source_target_pairs={{0,16},{16,0},{32,48},{48,32},{64,80},{80,64},{96,112},{112,96},{1... | collective-permute-start | bytes 983048 | tf_op jit(solution)/shard_map/ppermute | solution.py:415
  149.3 17.8 %collective-permute-start.30 = (bf16[64,2560]{1,0:T(8,128)(2,1)S(1)}, bf16[64,2560]{1,0:T(8,128)(2,1)S(1)}, u32[]{:S(2)}, u32[]{:S(2)}) collective-permute-start(bf16[64,2560]{1,0:T(8,128)(2,1)S(1)} %get-tuple-element.44), channel_id=1, source_target_pairs={{0,96},{16,112},{32,0},{48,16},{64,32},{80,48},{96,64},{112,80},{1... | collective-permute-start | bytes 983048 | tf_op jit(solution)/shard_map/ppermute | solution.py:411
  152.0 17.6 %collective-permute-start.31 = (bf16[64,2560]{1,0:T(8,128)(2,1)S(1)}, bf16[64,2560]{1,0:T(8,128)(2,1)S(1)}, u32[]{:S(2)}, u32[]{:S(2)}) collective-permute-start(bf16[64,2560]{1,0:T(8,128)(2,1)S(1)} %get-tuple-element.45), channel_id=1, source_target_pairs={{0,32},{16,48},{32,64},{48,80},{64,96},{80,112},{96,0},{112,16},{1... | collective-permute-start | bytes 983048 | tf_op jit(solution)/shard_map/ppermute | solution.py:411
  152.0 20.3 %collective-permute-start.32 = (bf16[64,2560]{1,0:T(8,128)(2,1)S(1)}, bf16[64,2560]{1,0:T(8,128)(2,1)S(1)}, u32[]{:S(2)}, u32[]{:S(2)}) collective-permute-start(bf16[64,2560]{1,0:T(8,128)(2,1)S(1)} %get-tuple-element.46), channel_id=1, source_target_pairs={{0,64},{16,80},{32,96},{48,112},{64,0},{80,16},{96,32},{112,48},{1... | collective-permute-start | bytes 983048 | tf_op jit(solution)/shard_map/ppermute | solution.py:411
  153.8 33.3 %collective-permute-start.34 = (bf16[128,2560]{1,0:T(8,128)(2,1)S(1)}, bf16[128,2560]{1,0:T(8,128)(2,1)S(1)}, u32[]{:S(2)}, u32[]{:S(2)}) collective-permute-start(bf16[128,2560]{1,0:T(8,128)(2,1)S(1)} %get-tuple-element.48), channel_id=1, source_target_pairs={{0,16},{16,0},{32,48},{48,32},{64,80},{80,64},{96,112},{112,96},{1... | collective-permute-start | bytes 1966088 | tf_op jit(solution)/shard_map/ppermute | solution.py:415
  162.5 17.7 %collective-permute-start.22 = (bf16[64,2560]{1,0:T(8,128)(2,1)S(1)}, bf16[64,2560]{1,0:T(8,128)(2,1)S(1)}, u32[]{:S(2)}, u32[]{:S(2)}) collective-permute-start(bf16[64,2560]{1,0:T(8,128)(2,1)S(1)} %get-tuple-element.38), channel_id=1, source_target_pairs={{0,96},{16,112},{32,0},{48,16},{64,32},{80,48},{96,64},{112,80},{1... | collective-permute-start | bytes 983048 | tf_op jit(solution)/shard_map/ppermute | solution.py:411
  167.1 15.8 %collective-permute-start.23 = (bf16[64,2560]{1,0:T(8,128)(2,1)S(1)}, bf16[64,2560]{1,0:T(8,128)(2,1)S(1)}, u32[]{:S(2)}, u32[]{:S(2)}) collective-permute-start(bf16[64,2560]{1,0:T(8,128)(2,1)S(1)} %get-tuple-element.39), channel_id=1, source_target_pairs={{0,32},{16,48},{32,64},{48,80},{64,96},{80,112},{96,0},{112,16},{1... | collective-permute-start | bytes 983048 | tf_op jit(solution)/shard_map/ppermute | solution.py:411
  169.6 15.5 %collective-permute-start.24 = (bf16[64,2560]{1,0:T(8,128)(2,1)S(1)}, bf16[64,2560]{1,0:T(8,128)(2,1)S(1)}, u32[]{:S(2)}, u32[]{:S(2)}) collective-permute-start(bf16[64,2560]{1,0:T(8,128)(2,1)S(1)} %get-tuple-element.40), channel_id=1, source_target_pairs={{0,64},{16,80},{32,96},{48,112},{64,0},{80,16},{96,32},{112,48},{1... | collective-permute-start | bytes 983048 | tf_op jit(solution)/shard_map/ppermute | solution.py:411
  172.2 19.2 %collective-permute-start.26 = (bf16[128,2560]{1,0:T(8,128)(2,1)S(1)}, bf16[128,2560]{1,0:T(8,128)(2,1)S(1)}, u32[]{:S(2)}, u32[]{:S(2)}) collective-permute-start(bf16[128,2560]{1,0:T(8,128)(2,1)S(1)} %get-tuple-element.42), channel_id=1, source_target_pairs={{0,16},{16,0},{32,48},{48,32},{64,80},{80,64},{96,112},{112,96},{1... | collective-permute-start | bytes 1966088 | tf_op jit(solution)/shard_map/ppermute | solution.py:415
  180.2 13.1 %collective-permute-start.33 = (bf16[32,2560]{1,0:T(8,128)(2,1)S(1)}, bf16[32,2560]{1,0:T(8,128)(2,1)S(1)}, u32[]{:S(2)}, u32[]{:S(2)}) collective-permute-start(bf16[32,2560]{1,0:T(8,128)(2,1)S(1)} %slice.119), channel_id=1, source_target_pairs={{0,16},{16,0},{32,48},{48,32},{64,80},{80,64},{96,112},{112,96},{1... | collective-permute-start | bytes 491528 | tf_op jit(solution)/shard_map/ppermute | solution.py:415
  185.3 21.9 %collective-permute-start.25 = (bf16[32,2560]{1,0:T(8,128)(2,1)S(1)}, bf16[32,2560]{1,0:T(8,128)(2,1)S(1)}, u32[]{:S(2)}, u32[]{:S(2)}) collective-permute-start(bf16[32,2560]{1,0:T(8,128)(2,1)S(1)} %slice.120), channel_id=1, source_target_pairs={{0,16},{16,0},{32,48},{48,32},{64,80},{80,64},{96,112},{112,96},{1... | collective-permute-start | bytes 491528 | tf_op jit(solution)/shard_map/ppermute | solution.py:415
  187.4 7.0 %collective-permute-start.37 = (bf16[32,2560]{1,0:T(8,128)(2,1)S(1)}, bf16[32,2560]{1,0:T(8,128)(2,1)S(1)}, u32[]{:S(2)}, u32[]{:S(2)}) collective-permute-start(bf16[32,2560]{1,0:T(8,128)(2,1)S(1)} %get-tuple-element.60), channel_id=1, source_target_pairs={{0,64},{16,80},{32,96},{48,112},{64,0},{80,16},{96,32},{112,48},{1... | collective-permute-start | bytes 491528 | tf_op jit(solution)/shard_map/ppermute | solution.py:411
  187.5 8.3 %collective-permute-start.36 = (bf16[32,2560]{1,0:T(8,128)(2,1)S(1)}, bf16[32,2560]{1,0:T(8,128)(2,1)S(1)}, u32[]{:S(2)}, u32[]{:S(2)}) collective-permute-start(bf16[32,2560]{1,0:T(8,128)(2,1)S(1)} %get-tuple-element.61), channel_id=1, source_target_pairs={{0,32},{16,48},{32,64},{48,80},{64,96},{80,112},{96,0},{112,16},{1... | collective-permute-start | bytes 491528 | tf_op jit(solution)/shard_map/ppermute | solution.py:411
  191.4 5.3 %collective-permute-start.35 = (bf16[32,2560]{1,0:T(8,128)(2,1)S(1)}, bf16[32,2560]{1,0:T(8,128)(2,1)S(1)}, u32[]{:S(2)}, u32[]{:S(2)}) collective-permute-start(bf16[32,2560]{1,0:T(8,128)(2,1)S(1)} %get-tuple-element.62), channel_id=1, source_target_pairs={{0,96},{16,112},{32,0},{48,16},{64,32},{80,48},{96,64},{112,80},{1... | collective-permute-start | bytes 491528 | tf_op jit(solution)/shard_map/ppermute | solution.py:411
  197.7 17.8 %all-to-all-start.3 = ((bf16[16,8,1280]{2,1,0:T(8,128)(2,1)}), bf16[16,8,1280]{2,1,0:T(8,128)(2,1)S(1)}, u32[]{:S(2)}, u32[]{:S(2)}) async-start(bf16[16,8,1280]{2,1,0:T(8,128)(2,1)} %bitcast.13), calls=%async_computation.3 | async-start | bytes 655360 | tf_op jit(solution)/shard_map/all_to_all | solution.py:445
  202.9 8.6 %collective-permute-start.29 = (bf16[32,2560]{1,0:T(8,128)(2,1)S(1)}, bf16[32,2560]{1,0:T(8,128)(2,1)S(1)}, u32[]{:S(2)}, u32[]{:S(2)}) collective-permute-start(bf16[32,2560]{1,0:T(8,128)(2,1)S(1)} %get-tuple-element.63), channel_id=1, source_target_pairs={{0,64},{16,80},{32,96},{48,112},{64,0},{80,16},{96,32},{112,48},{1... | collective-permute-start | bytes 491528 | tf_op jit(solution)/shard_map/ppermute | solution.py:411
  203.8 10.7 %collective-permute-start.28 = (bf16[32,2560]{1,0:T(8,128)(2,1)S(1)}, bf16[32,2560]{1,0:T(8,128)(2,1)S(1)}, u32[]{:S(2)}, u32[]{:S(2)}) collective-permute-start(bf16[32,2560]{1,0:T(8,128)(2,1)S(1)} %get-tuple-element.64), channel_id=1, source_target_pairs={{0,32},{16,48},{32,64},{48,80},{64,96},{80,112},{96,0},{112,16},{1... | collective-permute-start | bytes 491528 | tf_op jit(solution)/shard_map/ppermute | solution.py:411
  205.0 9.5 %collective-permute-start.27 = (bf16[32,2560]{1,0:T(8,128)(2,1)S(1)}, bf16[32,2560]{1,0:T(8,128)(2,1)S(1)}, u32[]{:S(2)}, u32[]{:S(2)}) collective-permute-start(bf16[32,2560]{1,0:T(8,128)(2,1)S(1)} %get-tuple-element.65), channel_id=1, source_target_pairs={{0,96},{16,112},{32,0},{48,16},{64,32},{80,48},{96,64},{112,80},{1... | collective-permute-start | bytes 491528 | tf_op jit(solution)/shard_map/ppermute | solution.py:411
  207.1 14.0 %copy-start.10 = (bf16[1,128,1024]{2,1,0:T(8,128)(2,1)S(1)}, bf16[1,128,1024]{2,1,0:T(8,128)(2,1)}, u32[]{:S(2)}) copy-start(bf16[1,128,1024]{2,1,0:T(8,128)(2,1)} %param.13) | copy-start | bytes 786436
  207.1 14.1 %copy-start.11 = (bf16[1,128,1024]{2,1,0:T(8,128)(2,1)S(1)}, bf16[1,128,1024]{2,1,0:T(8,128)(2,1)}, u32[]{:S(2)}) copy-start(bf16[1,128,1024]{2,1,0:T(8,128)(2,1)} %param.14) | copy-start | bytes 786436
  215.5 14.3 %all-to-all-start.2 = ((bf16[16,8,1280]{2,1,0:T(8,128)(2,1)}), bf16[16,8,1280]{2,1,0:T(8,128)(2,1)S(1)}, u32[]{:S(2)}, u32[]{:S(2)}) async-start(bf16[16,8,1280]{2,1,0:T(8,128)(2,1)} %bitcast.11), calls=%async_computation.2 | async-start | bytes 655360 | tf_op jit(solution)/shard_map/all_to_all | solution.py:445
  223.2 11.1 %copy-start.1 = (bf16[1,128,5120]{2,1,0:T(8,128)(2,1)S(1)}, bf16[1,128,5120]{2,1,0:T(8,128)(2,1)}, u32[]{:S(2)}) copy-start(bf16[1,128,5120]{2,1,0:T(8,128)(2,1)} %param.15) | copy-start | bytes 3932164
  223.2 11.1 %copy-start.3 = (bf16[1,128,5120]{2,1,0:T(8,128)(2,1)S(1)}, bf16[1,128,5120]{2,1,0:T(8,128)(2,1)}, u32[]{:S(2)}) copy-start(bf16[1,128,5120]{2,1,0:T(8,128)(2,1)} %param.16) | copy-start | bytes 3932164
  223.2 11.1 %copy-start.6 = (f32[5120]{0:T(1024)S(1)}, f32[5120]{0:T(1024)}, u32[]{:S(2)}) copy-start(f32[5120]{0:T(1024)} %param.20) | copy-start | bytes 61444
  229.9 29.8 %all-to-all-start.4 = ((bf16[8,128,896]{2,1,0:T(8,128)(2,1)}), bf16[8,128,896]{2,1,0:T(8,128)(2,1)}, u32[]{:S(2)}, u32[]{:S(2)}) async-start(bf16[8,128,896]{2,1,0:T(8,128)(2,1)} %maximum_bitcast_fusion), calls=%async_computation.4 | async-start | bytes 3670016 | tf_op jit(solution)/shard_map/all_to_all | solution.py:449
  259.7 23.0 %all-to-all-start.5 = ((bf16[8,128,640]{2,1,0:T(8,128)(2,1)}), bf16[8,128,640]{2,1,0:T(8,128)(2,1)S(1)}, u32[]{:S(2)}, u32[]{:S(2)}) async-start(bf16[8,128,640]{2,1,0:T(8,128)(2,1)} %copy-done.4), calls=%async_computation.5 | async-start | bytes 2621440 | tf_op jit(solution)/shard_map/all_to_all | solution.py:449
  (7 other events, 22.0 us)

commit v2 on v1

v2 whole, which is shorter than its diff:
```python
import functools

import jax
import jax.numpy as jnp
from jax import lax
from jax.experimental import pallas as pl
from jax.experimental.pallas import tpu as pltpu
from jax.sharding import PartitionSpec as P

D = 5120
H = 40
KVH = 8
DH = 128
GROUP = H // KVH
EXPERTS = 16
CAP = 4
TOK = 128
SEQ = 1024
SPAN = 64
SPANS = SEQ // SPAN
FFD = 512
EPSILON = 1e-05
F32 = jnp.float32
BF16 = jnp.bfloat16
QB = 256
NQ = SEQ // QB
GW = GROUP * DH
HALF = D // 2
ROWS = 512
FIRST = 64
KB = 1024
TB = 1024
SHIFTS = (1, 3, 2)
FACTOR = DH ** (-0.5)


def nn(a, b):
    return lax.dot_general(a, b, (((1,), (0,)), ((), ())), preferred_element_type=F32)


def nt(a, b):
    return lax.dot_general(a, b, (((1,), (1,)), ((), ())), preferred_element_type=F32)


def tn(a, b):
    return lax.dot_general(a, b, (((0,), (0,)), ((), ())), preferred_element_type=F32)


def iota(shape, dim):
    return lax.broadcasted_iota(jnp.int32, shape, dim)


def params(mb=60):
    return pltpu.CompilerParams(vmem_limit_bytes=mb * 1024 * 1024)


def sds(shape, dtype=BF16):
    return jax.ShapeDtypeStruct(shape, dtype)


VM = pl.BlockSpec(memory_space=pltpu.VMEM)


def dispatch_kernel(stream, out_grad, weight, ids, gain, rows, picks):
    onehot = ids[...] == iota((TOK, 128), 1)
    onehot_f = onehot.astype(F32)
    lower = (iota((TOK, TOK), 1) < iota((TOK, TOK), 0)).astype(BF16)
    before = nn(lower, onehot_f.astype(BF16))
    rank = jnp.sum(before * onehot_f, axis=1, keepdims=True).astype(jnp.int32)
    lane = iota((TOK, 128), 1)
    target = ids[...] * 8 + rank
    kept = rank < CAP
    pick_n = ((lane == target) & kept).astype(BF16)
    pick_r = ((lane == target + CAP) & kept).astype(BF16)
    pick = jnp.concatenate([pick_n, pick_r], axis=0)
    picks[...] = pick
    total = jnp.zeros((TOK, 1), F32)
    for at in range(0, D, 640):
        part = stream[:, at:at + 640].astype(F32)
        total = total + jnp.sum(part * part, axis=1, keepdims=True)
    scale = lax.rsqrt(total / D + EPSILON)
    for at in range(0, D, 640):
        cols = slice(at, at + 640)
        normed = stream[:, cols].astype(F32) * scale * gain[:, cols]
        routed = out_grad[:, cols].astype(F32) * weight[...]
        both = jnp.concatenate([normed.astype(BF16), routed.astype(BF16)], axis=0)
        rows[:, cols] = tn(pick, both).astype(BF16)


def dispatch(stream, out_grad, weight, ids, gain):
    return pl.pallas_call(
        dispatch_kernel,
        out_shape=[sds((TOK, D)), sds((2 * TOK, 128))],
        in_specs=[VM] * 5,
        out_specs=[VM] * 2,
        compiler_params=params(24),
        name="dispatch",
    )(stream, out_grad, weight, ids, gain)


def sort_kernel(shard, *outs):
    out = iota((128, 128), 0)
    want = (out >> 6) * 64 + ((out >> 2) & 7) * 8 + ((out >> 5) & 1) * 4 + (out & 3)
    mover = (iota((128, 128), 1) == want).astype(BF16)
    for at in range(0, D, 1280):
        moved = nn(mover, shard[:, at:at + 1280]).astype(BF16)
        outs[0][:, at:at + 1280] = moved[:64]
        outs[1][:, at:at + 1280] = moved[64:]


def sort_rows(shard):
    return pl.pallas_call(
        sort_kernel,
        out_shape=[sds((64, D))] * 2,
        in_specs=[VM],
        out_specs=[VM] * 2,
        compiler_params=params(24),
        name="sort_rows",
    )(shard)


def project_kernel(*refs):
    tops = refs[:4]
    rests = refs[4:12]
    w_gate, w_in, w_out, grad_gate, grad_up, x_at, r_at, gate, up, backed = refs[12:]
    step = pl.program_id(0)

    @pl.when(step == 0)
    def _():
        gate[...] = jnp.zeros_like(gate)
        up[...] = jnp.zeros_like(up)
        backed[...] = jnp.zeros_like(backed)

    for at in range(8):
        top = tops[at // 2][(at % 2) * FIRST:(at % 2 + 1) * FIRST, :]
        low = rests[at]
        x_at[at * 64:at * 64 + 32, :] = top[:32]
        x_at[at * 64 + 32:at * 64 + 64, :] = low[:32]
        r_at[at * 64:at * 64 + 32, :] = top[32:]
        r_at[at * 64 + 32:at * 64 + 64, :] = low[32:]
    gate[...] += nn(x_at[...], w_gate[0])
    up[...] += nn(x_at[...], w_in[0])
    backed[...] += nt(r_at[...], w_out[0])

    @pl.when(step == pl.num_programs(0) - 1)
    def _():
        sig = jax.nn.sigmoid(gate[...])
        grad_gate[...] = (
            backed[...] * up[...] * sig * (1.0 + gate[...] * (1.0 - sig))
        ).astype(BF16)
        grad_up[...] = (backed[...] * gate[...] * sig).astype(BF16)


def project(pieces, w_gate, w_in, w_out):
    whole = pl.BlockSpec((ROWS, FFD), lambda i: (0, 0))
    in_specs = [pl.BlockSpec((p.shape[0], KB), lambda i: (0, i)) for p in pieces]
    in_specs += [
        pl.BlockSpec((1, KB, FFD), lambda i: (0, i, 0)),
        pl.BlockSpec((1, KB, FFD), lambda i: (0, i, 0)),
        pl.BlockSpec((1, FFD, KB), lambda i: (0, 0, i)),
    ]
    return pl.pallas_call(
        project_kernel,
        grid=(D // KB,),
        out_shape=[sds((ROWS, FFD))] * 2,
        in_specs=in_specs,
        out_specs=[whole] * 2,
        scratch_shapes=[pltpu.VMEM((ROWS, KB), BF16)] * 2
        + [pltpu.VMEM((ROWS, FFD), F32)] * 3,
        compiler_params=params(60),
        cost_estimate=pl.CostEstimate(
            flops=6 * ROWS * D * FFD, bytes_accessed=28 * 1024 * 1024, transcendentals=0
        ),
        name="project",
    )(*pieces, w_gate, w_in, w_out)


TERM_ROWS = (64, 64, 64, 64, 128, 128)


def term_kernel(grad_gate, grad_up, w_gate, w_in, *outs):
    block = nt(grad_gate[...], w_gate[0]) + nt(grad_up[...], w_in[0])
    block = block.astype(BF16)
    for k in range(4):
        for side in range(2):
            at = (2 * k + side) * 64
            outs[k][side * 32:(side + 1) * 32, :] = block[at:at + 32]
            outs[4 + side][k * 32:(k + 1) * 32, :] = block[at + 32:at + 64]


def terms(grad_gate, grad_up, w_gate, w_in):
    whole = pl.BlockSpec(grad_gate.shape, lambda i: (0, 0))
    weight = pl.BlockSpec((1, TB, FFD), lambda i: (0, i, 0))
    return pl.pallas_call(
        term_kernel,
        grid=(D // TB,),
        out_shape=[sds((r, D)) for r in TERM_ROWS],
        in_specs=[whole, whole, weight, weight],
        out_specs=[pl.BlockSpec((r, TB), lambda i: (0, i)) for r in TERM_ROWS],
        compiler_params=params(),
        cost_estimate=pl.CostEstimate(
            flops=4 * ROWS * D * FFD, bytes_accessed=16 * 1024 * 1024, transcendentals=0
        ),
        name="terms",
    )(grad_gate, grad_up, w_gate, w_in)


def settle_kernel(a_own, a_swap, b_own, b1, b3, b2, out):
    a = a_own[...] + a_swap[...].astype(F32)
    b = b_own[...] + b1[...].astype(F32) + b3[...].astype(F32) + b2[...].astype(F32)
    both = jnp.concatenate([a, b], axis=0).astype(BF16)
    stacked = jnp.concatenate([both[:, :HALF], both[:, HALF:]], axis=0)
    o = iota((128, 128), 0)
    want = ((o >> 2) & 1) * 64 + (o >> 3) * 4 + (o & 3)
    mover = (iota((128, 128), 1) == want).astype(BF16)
    out[...] = nn(mover, stacked).astype(BF16)


def settle(*args):
    return pl.pallas_call(
        settle_kernel,
        out_shape=sds((128, HALF)),
        in_specs=[VM] * 6,
        out_specs=VM,
        compiler_params=params(24),
        name="settle",
    )(*args)


def finish_kernel(stream, out_grad, gain, picks, part, grad, grad_cut, scaled):
    square = jnp.zeros((TOK, 1), F32)
    dots = jnp.zeros((TOK, 1), F32)
    for at in range(0, HALF, 640):
        got = nn(picks[...], part[:, at:at + 640])
        for half in range(2):
            cols = slice(half * HALF + at, half * HALF + at + 640)
            x = stream[:, cols].astype(F32)
            u = got[half * TOK:(half + 1) * TOK] * gain[:, cols]
            square = square + jnp.sum(x * x, axis=1, keepdims=True)
            dots = dots + jnp.sum(x * u, axis=1, keepdims=True)
            scaled[:, cols] = u
    r = lax.rsqrt(square / D + EPSILON)
    coef = dots * (r * r * r) / D
    for group in range(KVH):
        cols = slice(group * GW, (group + 1) * GW)
        x = stream[:, cols].astype(F32)
        total = out_grad[:, cols].astype(F32) + (scaled[:, cols] * r - x * coef)
        total = total.astype(BF16)
        grad[:, cols] = total
        grad_cut[group] = total


def finish(stream, out_grad, gain, picks, part):
    return pl.pallas_call(
        finish_kernel,
        out_shape=[sds((TOK, D)), sds((KVH, TOK, GW))],
        in_specs=[VM] * 5,
        out_specs=[VM] * 2,
        scratch_shapes=[pltpu.VMEM((TOK, D), F32)],
        compiler_params=params(24),
        name="finish",
    )(stream, out_grad, gain, picks, part)


def cut_kernel(q, k, v, out):
    for head in range(KVH):
        out[head, :, :GW] = q[:, head * GW:(head + 1) * GW]
        out[head, :, GW:GW + DH] = k[:, head * DH:(head + 1) * DH]
        out[head, :, GW + DH:] = v[:, head * DH:(head + 1) * DH]


def cut_heads(q, k, v):
    return pl.pallas_call(
        cut_kernel,
        out_shape=sds((KVH, TOK, GW + 2 * DH)),
        in_specs=[VM] * 3,
        out_specs=VM,
        compiler_params=params(),
        name="cut_heads",
    )(q, k, v)


def probs_kernel(order, rows, probs, attended, q_out, kv_out, q_at, kv_at, vt_at):
    head = pl.program_id(0)

    @pl.when(head == 0)
    def _():
        for s in range(SPANS):
            to = pl.ds(pl.multiple_of(order[s] * SPAN, SPAN), SPAN)
            block = rows[s * SPAN:(s + 1) * SPAN, :]
            for g in range(GROUP):
                q_at[g, to, :] = block[:, g * DH:(g + 1) * DH]
            kv_at[0, to, :] = block[:, GW:GW + DH]
            kv_at[1, to, :] = block[:, GW + DH:GW + 2 * DH]
        q_out[...] = q_at[...]
        kv_out[...] = kv_at[...]
        vt_at[...] = kv_at[1].T

    for i in range(NQ):
        n = QB * (i + 1)
        q = q_at[head, i * QB:n, :]
        scores = nt(kv_at[0, 0:n, :], q) * FACTOR
        visible = iota((n, QB), 0) <= iota((n, QB), 1) + i * QB
        scores = jnp.where(visible, scores, -1e30)
        peak = jnp.max(scores, axis=0, keepdims=True)
        weights = jnp.exp(scores - peak)
        weights = weights / jnp.sum(weights, axis=0, keepdims=True)
        weights_b = weights.astype(BF16)
        probs[0, i, 0:n, :] = weights_b
        attended[0, :, i * QB:n] = nn(vt_at[:, 0:n], weights_b)


def make_probs(order, rows):
    return pl.pallas_call(
        probs_kernel,
        grid_spec=pltpu.PrefetchScalarGridSpec(
            num_scalar_prefetch=1,
            grid=(GROUP,),
            in_specs=[pl.BlockSpec((SEQ, GW + 2 * DH), lambda h, o: (0, 0))],
            out_specs=[
                pl.BlockSpec((1, NQ, SEQ, QB), lambda h, o: (h, 0, 0, 0)),
                pl.BlockSpec((1, DH, SEQ), lambda h, o: (h, 0, 0)),
                pl.BlockSpec((GROUP, SEQ, DH), lambda h, o: (0, 0, 0)),
                pl.BlockSpec((2, SEQ, DH), lambda h, o: (0, 0, 0)),
            ],
            scratch_shapes=[
                pltpu.VMEM((GROUP, SEQ, DH), BF16),
                pltpu.VMEM((2, SEQ, DH), BF16),
                pltpu.VMEM((DH, SEQ), BF16),
            ],
        ),
        out_shape=[
            sds((GROUP, NQ, SEQ, QB)),
            sds((GROUP, DH, SEQ), F32),
            sds((GROUP, SEQ, DH)),
            sds((2, SEQ, DH)),
        ],
        compiler_params=params(),
        cost_estimate=pl.CostEstimate(
            flops=2 * GROUP * SEQ * SEQ * DH, bytes_accessed=14 * 1024 * 1024, transcendentals=GROUP * SEQ * SEQ
        ),
        name="probs",
    )(order, rows)


def attend_kernel(
    order, probs, attended, q, kv, grads, out, g_at, kt_at, dq_at, dk_at, dv_at
):
    head = pl.program_id(0)

    @pl.when(head == 0)
    def _():
        for s in range(SPANS):
            to = pl.ds(pl.multiple_of(order[s] * SPAN, SPAN), SPAN)
            block = grads[s * SPAN:(s + 1) * SPAN, :]
            for g in range(GROUP):
                g_at[g, to, :] = block[:, g * DH:(g + 1) * DH]
        kt_at[...] = kv[0].T
        dk_at[...] = jnp.zeros_like(dk_at)
        dv_at[...] = jnp.zeros_like(dv_at)

    g_t = g_at[head].T
    delta = jnp.sum(g_t.astype(F32) * attended[0], axis=0, keepdims=True)
    for i in range(NQ):
        n = QB * (i + 1)
        g_i = g_at[head, i * QB:n, :]
        q_i = q[head, i * QB:n, :]
        p_b = probs[0, i, 0:n, :]
        dp = nn(kv[1, 0:n, :], g_t[:, i * QB:n])
        ds = (p_b.astype(F32) * (dp - delta[:, i * QB:n])).astype(BF16)
        dv_at[0:n, :] += nn(p_b, g_i)
        dk_at[0:n, :] += nn(ds, q_i)
        dq_at[i * QB:n, :] = (nn(kt_at[:, 0:n], ds) * FACTOR).T.astype(BF16)
    for s in range(SPANS):
        at = pl.ds(pl.multiple_of(order[s] * SPAN, SPAN), SPAN)
        to = slice(s * SPAN, (s + 1) * SPAN)
        out[to, pl.ds(pl.multiple_of(head * DH, DH), DH)] = dq_at[at, :]

    @pl.when(head == GROUP - 1)
    def _():
        for s in range(SPANS):
            at = pl.ds(pl.multiple_of(order[s] * SPAN, SPAN), SPAN)
            to = slice(s * SPAN, (s + 1) * SPAN)
            out[to, GW:GW + DH] = (dk_at[at, :] * FACTOR).astype(BF16)
            out[to, GW + DH:GW + 2 * DH] = dv_at[at, :].astype(BF16)


def attend(order, probs, attended, q, kv, grads):
    return pl.pallas_call(
        attend_kernel,
        grid_spec=pltpu.PrefetchScalarGridSpec(
            num_scalar_prefetch=1,
            grid=(GROUP,),
            in_specs=[
                pl.BlockSpec((1, NQ, SEQ, QB), lambda h, o: (h, 0, 0, 0)),
                pl.BlockSpec((1, DH, SEQ), lambda h, o: (h, 0, 0)),
                pl.BlockSpec((GROUP, SEQ, DH), lambda h, o: (0, 0, 0)),
                pl.BlockSpec((2, SEQ, DH), lambda h, o: (0, 0, 0)),
                pl.BlockSpec((SEQ, GW), lambda h, o: (0, 0)),
            ],
            out_specs=pl.BlockSpec((SEQ, GW + 2 * DH), lambda h, o: (0, 0)),
            scratch_shapes=[
                pltpu.VMEM((GROUP, SEQ, DH), BF16),
                pltpu.VMEM((DH, SEQ), BF16),
                pltpu.VMEM((SEQ, DH), BF16),
                pltpu.VMEM((SEQ, DH), F32),
                pltpu.VMEM((SEQ, DH), F32),
            ],
        ),
        out_shape=sds((SEQ, GW + 2 * DH)),
        compiler_params=params(),
        cost_estimate=pl.CostEstimate(
            flops=8 * GROUP * SEQ * SEQ * DH, bytes_accessed=16 * 1024 * 1024, transcendentals=0
        ),
        name="attend",
    )(order, probs, attended, q, kv, grads)


def hold(x, *others):
    anywhere = pl.BlockSpec(memory_space=pl.ANY)
    return pl.pallas_call(
        lambda *refs: None,
        out_shape=sds(x.shape, x.dtype),
        in_specs=[anywhere] * (1 + len(others)),
        out_specs=anywhere,
        input_output_aliases={0: 0},
        name="hold",
    )(x, *others)


def along_z(x, shift):
    pairs = [(c, ((c // 2 + shift) % 4) * 2 + c % 2) for c in range(8)]
    return lax.ppermute(x, "ctx", pairs)


def across_x(x):
    return lax.ppermute(x, "ctx", [(c, c ^ 1) for c in range(8)])


def gather_pieces(shard):
    a, b = sort_rows(shard)
    a_x = across_x(a)
    b_z = [along_z(b, k) for k in SHIFTS]
    a_both = jnp.concatenate([a, a_x], axis=0)
    a_z = [along_z(a_both, k) for k in SHIFTS]
    rests = []
    for p in [b] + b_z:
        rests += [p, across_x(p)]
    return [a_both] + a_z + rests


def scatter_sums(groups, tie):
    a_own, b_own, b_far = groups[0], groups[4], groups[5]
    b_got = across_x(hold(b_far, tie))
    a_got = [along_z(g, -k) for g, k in zip(groups[1:4], SHIFTS)]
    b_sum = b_own.astype(F32) + b_got.astype(F32)
    b_low = b_sum.astype(BF16)
    b_back = [
        along_z(b_low[32 * (at + 1):32 * (at + 2)], -k) for at, k in enumerate(SHIFTS)
    ]
    a_sum = a_own.astype(F32)
    for got in a_got:
        a_sum = a_sum + got.astype(F32)
    a_swap = across_x(a_sum[32:].astype(BF16))
    return settle(a_sum[:32], a_swap, b_sum[:32], *b_back)


def swap_exp(x):
    return lax.all_to_all(x, "exp", split_axis=0, concat_axis=0, tiled=True)


def swap_ctx(x):
    return lax.all_to_all(x, "ctx", split_axis=0, concat_axis=0, tiled=True)


def body(
    query_rows,
    key_rows,
    value_rows,
    stream,
    out_grad,
    route_weight,
    expert_ids,
    span_order,
    norm_gain,
    expert_gate,
    expert_in,
    expert_out,
):
    gain = norm_gain.reshape(1, D)
    outgoing, picks = dispatch(
        stream[0], out_grad[0], route_weight.reshape(TOK, 1), expert_ids[0], gain
    )
    shard = swap_exp(outgoing.reshape(EXPERTS, 8, D)).reshape(TOK, D)
    pieces = gather_pieces(shard)
    by_head = hold(cut_heads(query_rows[0], key_rows[0], value_rows[0]), *pieces)
    qkv = swap_ctx(by_head).reshape(SEQ, GW + 2 * DH)
    grad_gate, grad_up = project(pieces, expert_gate, expert_in, expert_out)
    settled = scatter_sums(terms(grad_gate, grad_up, expert_gate, expert_in), qkv)
    part = swap_exp(settled.reshape(EXPERTS, 8, HALF)).reshape(TOK, HALF)
    probs, attended, q_sorted, kv_sorted = make_probs(span_order, qkv)
    grad_total, grad_cut = finish(stream[0], out_grad[0], gain, picks, part)
    grads = swap_ctx(grad_cut).reshape(SEQ, GW)
    result = attend(span_order, probs, attended, q_sorted, kv_sorted, grads)
    back = swap_ctx(result.reshape(KVH, TOK, GW + 2 * DH)).transpose(1, 0, 2)
    return (
        grad_total[None],
        back[:, :, :GW].reshape(1, TOK, D),
        back[:, :, GW:GW + DH].reshape(1, TOK, KVH * DH),
        back[:, :, GW + DH:].reshape(1, TOK, KVH * DH),
    )


def solution(mesh):
    rows = P("exp", "ctx", None)
    return jax.shard_map(
        body,
        mesh=mesh,
        in_specs=(
            rows,
            rows,
            rows,
            rows,
            rows,
            P("exp", "ctx"),
            rows,
            P(),
            P(),
            P("exp", None, "ctx"),
            P("exp", None, "ctx"),
            rows,
        ),
        out_specs=(rows, rows, rows, rows),
        check_vma=False,
    )
```

time: 331 us -> 301 us (0.909)
  starting transfers between devices: 88.1 us -> 50.9 us
  blocking collectives: 45.9 us -> 68.3 us
  waiting for transfers between devices: 118 us -> 104 us
    ppermute x24 -> x12, waiting for transfers between devices: 36.3 us -> 65.6 us  [along_z(): return lax.ppermute(x, 'ctx', pairs)]
    all_to_all x2, waiting for transfers between devices: 30.8 us -> 5.48 us  [swap_ctx(): return lax.all_to_all(x, 'ctx', split_axis=0, concat_axis=0, tiled=True)]
    all_to_all x1 -> x2, blocking collectives: 17.7 us -> 39.8 us  [swap_exp(): return lax.all_to_all(x, 'exp', split_axis=0, concat_axis=0, tiled=True)]
    ppermute x24 -> x12, starting transfers between devices: 40 us -> 21.6 us  [along_z(): return lax.ppermute(x, 'ctx', pairs)]
    all_to_all x3 -> x0, starting transfers between devices: 14.3 us -> none  [swap_exp(): return lax.all_to_all(x, 'exp', split_axis=0, concat_axis=0, tiled=True)]
    all_to_all x3 -> x0, waiting for transfers between devices: 9.8 us -> none  [swap_exp(): return lax.all_to_all(x, 'exp', split_axis=0, concat_axis=0, tiled=True)]
    ppermute x14 -> x7, starting transfers between devices: 25.7 us -> 17.8 us  [across_x(): return lax.ppermute(x, 'ctx', [(c, c ^ 1) for c in range(8)])]
    ppermute x14 -> x7, waiting for transfers between devices: 40.8 us -> 33.1 us  [across_x(): return lax.ppermute(x, 'ctx', [(c, c ^ 1) for c in range(8)])]
  transfers between devices with their start and end apart: 43 -> 21, of which waited for: 25 -> 13; matrix products, arithmetic and copies ran while one was open for 1% -> 1% of each run, Pallas kernels for 9% -> 14%
where the time goes in v2:
time: 301 us; the launch traced here: 300 us
  waiting for transfers between devices  104 us (35%)
  blocking collectives  68.3 us (23%)
  Pallas kernels  61.5 us (20%)
  starting transfers between devices  50.9 us (17%)
  local copies, waits for them, and re-layouts  11.9 us (4%)
    ppermute x12, waiting for transfers between devices, along_z(): return lax.ppermute(x, 'ctx', pairs)  65.6 us
    all_to_all x2, blocking collectives, swap_exp(): return lax.all_to_all(x, 'exp', split_axis=0, concat_axis=0, tiled=True)  39.8 us
    ppermute x7, waiting for transfers between devices, across_x(): return lax.ppermute(x, 'ctx', [(c, c ^ 1) for c in range(8)])  33.1 us
    all_to_all x1, blocking collectives, swap_ctx(): return lax.all_to_all(x, 'ctx', split_axis=0, concat_axis=0, tiled=True)  28.5 us
    ppermute x12, starting transfers between devices, along_z(): return lax.ppermute(x, 'ctx', pairs)  21.6 us
    ppermute x7, starting transfers between devices, across_x(): return lax.ppermute(x, 'ctx', [(c, c ^ 1) for c in range(8)])  17.8 us
    pallas_call x1, Pallas kernels, project(): pl.pallas_call(project_kernel, grid=(D // KB,), out_shape=[sds((ROWS, FFD...  14.6 us
    pallas_call x1, Pallas kernels, make_probs(): pl.pallas_call(probs_kernel, grid_spec=pltpu.PrefetchScalarGridSpec(num_s...  14.6 us
  transfers between devices with their start and end apart: 21, of which 13 were waited for; matrix products, arithmetic and copies ran while one was open for 1% of the time, Pallas kernels for 14%

profile of v2, /device:TPU:0, one launch (start us, length us, event | category | flops | bytes accessed | tf_op | source)
XLA Modules:
  0.0 299.7 jit_solution(16353474960612659465)
XLA Ops:
  0.6 0.8 copy.18.weight
  2.2 1.3 copy-done
  3.5 1.3 copy-done.2
  5.5 1.2 dispatch.1
  6.7 24.7 %all_to_all.25 = bf16[16,8,5120]{2,1,0:T(8,128)(2,1)S(1)} all-to-all(bf16[16,8,5120]{2,1,0:T(8,128)(2,1)S(1)} %bitcast.24), channel_id=1, replica_groups=mesh['ctx'=8,'exp'=16] {'exp'}, dimensions={0} | all-to-all | bytes 2621440 | tf_op jit(solution)/shard_map/all_to_all | solution.py:469
  31.9 4.0 %collective-permute-start.9 = (bf16[64,5120]{1,0:T(8,128)(2,1)S(1)}, bf16[64,5120]{1,0:T(8,128)(2,1)S(1)}, u32[]{:S(2)}, u32[]{:S(2)}) collective-permute-start(bf16[64,5120]{1,0:T(8,128)(2,1)S(1)} %get-tuple-element.25.refs_4_.refs_5_), channel_id=1, source_target_pairs={{0,64},{16,80},{32,96},{48,112},{64,0},{80,16},{96,32},{112,48},{1... | collective-permute-start | bytes 1966088 | tf_op jit(solution)/shard_map/ppermute | solution.py:433
  35.9 2.7 collective-permute-start
  39.3 1.3 collective-permute-start.5
  40.6 0.8 collective-permute-start.4
  41.5 10.0 %collective-permute-done.9.refs_10_.refs_11_ = bf16[64,5120]{1,0:T(8,128)(2,1)S(1)} collective-permute-done((bf16[64,5120]{1,0:T(8,128)(2,1)S(1)}, bf16[64,5120]{1,0:T(8,128)(2,1)S(1)}, u32[]{:S(2)}, u32[]{:S(2)}) %collective-permute-start.9) | collective-permute-done | bytes 655392 | tf_op jit(solution)/shard_map/ppermute | solution.py:433
  51.5 2.7 collective-permute-start.10
  54.3 0.8 collective-permute-done
  55.1 2.9 collective-permute-start.3
  58.0 8.6 %collective-permute-done.7.refs_8_.refs_9_ = bf16[64,5120]{1,0:T(8,128)(2,1)S(1)} collective-permute-done((bf16[64,5120]{1,0:T(8,128)(2,1)S(1)}, bf16[64,5120]{1,0:T(8,128)(2,1)S(1)}, u32[]{:S(2)}, u32[]{:S(2)}) %collective-permute-start.7) | collective-permute-done | bytes 655392 | tf_op jit(solution)/shard_map/ppermute | solution.py:433
  66.6 2.6 collective-permute-start.2
  69.2 2.8 collective-permute-start.8
  72.0 11.1 %collective-permute-done.10.refs_11_.refs_12_ = bf16[64,5120]{1,0:T(8,128)(2,1)S(1)} collective-permute-done((bf16[64,5120]{1,0:T(8,128)(2,1)S(1)}, bf16[64,5120]{1,0:T(8,128)(2,1)S(1)}, u32[]{:S(2)}, u32[]{:S(2)}) %collective-permute-start.10) | collective-permute-done | bytes 655392 | tf_op jit(solution)/shard_map/ppermute | solution.py:437
  83.1 2.7 collective-permute-start.6
  85.9 2.9 cut_heads.1.refs_0_
  88.8 8.5 %collective-permute-done.8.refs_9_.refs_10_ = bf16[64,5120]{1,0:T(8,128)(2,1)} collective-permute-done((bf16[64,5120]{1,0:T(8,128)(2,1)S(1)}, bf16[64,5120]{1,0:T(8,128)(2,1)}, u32[]{:S(2)}, u32[]{:S(2)}) %collective-permute-start.8) | collective-permute-done | bytes 655392 | tf_op jit(solution)/shard_map/ppermute | solution.py:437
  97.3 12.3 %collective-permute-done.6.refs_7_.refs_8_ = bf16[64,5120]{1,0:T(8,128)(2,1)} collective-permute-done((bf16[64,5120]{1,0:T(8,128)(2,1)}, bf16[64,5120]{1,0:T(8,128)(2,1)}, u32[]{:S(2)}, u32[]{:S(2)}) %collective-permute-start.6) | collective-permute-done | bytes 655392 | tf_op jit(solution)/shard_map/ppermute | solution.py:437
  109.6 11.9 %collective-permute-done.2.refs_2_.refs_3_ = bf16[128,5120]{1,0:T(8,128)(2,1)} collective-permute-done((bf16[128,5120]{1,0:T(8,128)(2,1)S(1)}, bf16[128,5120]{1,0:T(8,128)(2,1)}, u32[]{:S(2)}, u32[]{:S(2)}) %collective-permute-start.2) | collective-permute-done | bytes 1310752 | tf_op jit(solution)/shard_map/ppermute | solution.py:433
  121.4 6.1 %all-to-all-start.1 = ((bf16[8,128,896]{2,1,0:T(8,128)(2,1)}), bf16[8,128,896]{2,1,0:T(8,128)(2,1)S(1)}, u32[]{:S(2)}, u32[]{:S(2)}) async-start(bf16[8,128,896]{2,1,0:T(8,128)(2,1)} %hold.2), calls=%async_computation.1 | async-start | bytes 3670016 | tf_op jit(solution)/shard_map/all_to_all | solution.py:473
  127.5 14.6 %project.1 = (bf16[512,512]{1,0:T(8,128)(2,1)}, bf16[512,512]{1,0:T(8,128)(2,1)}) custom-call(bf16[128,5120]{1,0:T(8,128)(2,1)} %copy-done.8, bf16[128,5120]{1,0:T(8,128)(2,1)} %collective-permute-done.1.refs_1_.refs_2_, bf16[128,5120]{1,0:T(8,128)(2,1)} %collective-permute-done.2.refs_2_.refs_3_, bf16[128,5120]{1,0:T(8,128)(2,1)} %copy-done.9, ...), custom_call_target="tpu_custom_call" | custom-call | flops 8053063680 | bytes 29360128 | tf_op jit(solution)/shard_map/project/pallas_call | solution.py:162
  142.1 10.3 %terms.1 = (bf16[64,5120]{1,0:T(8,128)(2,1)}, bf16[64,5120]{1,0:T(8,128)(2,1)}, bf16[64,5120]{1,0:T(8,128)(2,1)}, bf16[64,5120]{1,0:T(8,128)(2,1)}, bf16[128,512...) custom-call(bf16[512,512]{1,0:T(8,128)(2,1)} %get-tuple-element.26.grad_gate, bf16[512,512]{1,0:T(8,128)(2,1)} %get-tuple-element.27.grad_up, ...), custom_call_target="tpu_custom_call" | custom-call | flops 5368709120 | bytes 16777216 | tf_op jit(solution)/shard_map/terms/pallas_call | solution.py:194
  152.4 3.2 %collective-permute-start.11 = (bf16[64,5120]{1,0:T(8,128)(2,1)}, bf16[64,5120]{1,0:T(8,128)(2,1)S(1)}, u32[]{:S(2)}, u32[]{:S(2)}) collective-permute-start(bf16[64,5120]{1,0:T(8,128)(2,1)} %get-tuple-element.29), channel_id=1, source_target_pairs={{0,96},{16,112},{32,0},{48,16},{64,32},{80,48},{96,64},{112,80},{1... | collective-permute-start | bytes 1966088 | tf_op jit(solution)/shard_map/ppermute | solution.py:433
  155.7 2.3 collective-permute-start.13
  158.0 1.2 copy-done.7
  159.2 3.0 collective-permute-start.15
  162.2 21.4 %collective-permute-done.11 = bf16[64,5120]{1,0:T(8,128)(2,1)S(1)} collective-permute-done((bf16[64,5120]{1,0:T(8,128)(2,1)}, bf16[64,5120]{1,0:T(8,128)(2,1)S(1)}, u32[]{:S(2)}, u32[]{:S(2)}) %collective-permute-start.11) | collective-permute-done | bytes 655392 | tf_op jit(solution)/shard_map/ppermute | solution.py:433
  183.7 3.4 %collective-permute-done.12 = bf16[64,5120]{1,0:T(8,128)(2,1)} collective-permute-done((bf16[64,5120]{1,0:T(8,128)(2,1)}, bf16[64,5120]{1,0:T(8,128)(2,1)}, u32[]{:S(2)}, u32[]{:S(2)}) %collective-permute-start.12) | collective-permute-done | bytes 655392 | tf_op jit(solution)/shard_map/ppermute | solution.py:433
  187.1 1.7 convert_add_fusion.1
  188.8 3.1 %collective-permute-start.14 = (bf16[32,5120]{1,0:T(8,128)(2,1)S(1)}, bf16[32,5120]{1,0:T(8,128)(2,1)S(1)}, u32[]{:S(2)}, u32[]{:S(2)}) collective-permute-start(bf16[32,5120]{1,0:T(8,128)(2,1)S(1)} %slice.47), channel_id=1, source_target_pairs={{0,16},{16,0},{32,48},{48,32},{64,80},{80,64},{96,112},{112,96},{1... | collective-permute-start | bytes 983048 | tf_op jit(solution)/shard_map/ppermute | solution.py:437
  193.0 1.3 collective-permute-start.17
  194.3 2.6 collective-permute-start.16
  197.5 6.7 %collective-permute-done.18.b2 = bf16[32,5120]{1,0:T(8,128)(2,1)S(1)} collective-permute-done((bf16[32,5120]{1,0:T(8,128)(2,1)S(1)}, bf16[32,5120]{1,0:T(8,128)(2,1)S(1)}, u32[]{:S(2)}, u32[]{:S(2)}) %collective-permute-start.18) | collective-permute-done | bytes 327712 | tf_op jit(solution)/shard_map/ppermute | solution.py:433
  204.2 3.4 %collective-permute-done.17.b3 = bf16[32,5120]{1,0:T(8,128)(2,1)S(1)} collective-permute-done((bf16[32,5120]{1,0:T(8,128)(2,1)S(1)}, bf16[32,5120]{1,0:T(8,128)(2,1)S(1)}, u32[]{:S(2)}, u32[]{:S(2)}) %collective-permute-start.17) | collective-permute-done | bytes 327712 | tf_op jit(solution)/shard_map/ppermute | solution.py:433
  208.1 15.1 %all_to_all.26 = bf16[16,8,2560]{2,1,0:T(8,128)(2,1)S(1)} all-to-all(bf16[16,8,2560]{2,1,0:T(8,128)(2,1)S(1)} %bitcast.23), channel_id=1, replica_groups=mesh['ctx'=8,'exp'=16] {'exp'}, dimensions={0} | all-to-all | bytes 1310720 | tf_op jit(solution)/shard_map/all_to_all | solution.py:469
  223.2 3.5 %finish.1 = (bf16[128,5120]{1,0:T(8,128)(2,1)}, bf16[8,128,640]{2,1,0:T(8,128)(2,1)}) custom-call(bf16[128,5120]{1,0:T(8,128)(2,1)S(1)} %bitcast.18, bf16[128,5120]{1,0:T(8,128)(2,1)S(1)} %bitcast.20, f32[1,5120]{1,0:T(1,128)S(1)} %bitcast.26, bf16[256,128]{1,0:T(8,128)(2,1)S(1)} %get-tuple-element.22.picks, bf16[128,2560]{1,0:T(8,128)(2,1)S(1)} %bitcast.22), custom_call_target="tpu_custom_call" | custom-call | tf_op jit(solution)/shard_map/finish/pallas_call | solution.py:254
  226.6 5.5 %all-to-all-start.3 = ((bf16[8,128,640]{2,1,0:T(8,128)(2,1)}), bf16[8,128,640]{2,1,0:T(8,128)(2,1)S(1)}, u32[]{:S(2)}, u32[]{:S(2)}) async-start(bf16[8,128,640]{2,1,0:T(8,128)(2,1)} %get-tuple-element.39), calls=%async_computation.3 | async-start | bytes 2621440 | tf_op jit(solution)/shard_map/all_to_all | solution.py:473
  232.1 14.6 %probs.1 = (bf16[5,4,1024,256]{3,2,1,0:T(8,128)(2,1)}, f32[5,128,1024]{2,1,0:T(8,128)}, bf16[5,1024,128]{2,1,0:T(8,128)(2,1)}, bf16[2,1024,128]{2,1,0:T(8,128)(2,1)}) custom-call(s32[16]{0:T(128)} %order.3, bf16[1024,896]{1,0:T(8,128)(2,1)} %bitcast.30), custom_call_target="tpu_custom_call" | custom-call | flops 1342177280 | bytes 14680064 | tf_op jit(solution)/shard_map/probs/pallas_call | solution.py:314
  246.7 5.5 %all-to-all-done.3 = bf16[8,128,640]{2,1,0:T(8,128)(2,1)S(1)} async-done(((bf16[8,128,640]{2,1,0:T(8,128)(2,1)}), bf16[8,128,640]{2,1,0:T(8,128)(2,1)S(1)}, u32[]{:S(2)}, u32[]{:S(2)}) %all-to-all-start.3) | async-done | bytes 1310752 | tf_op jit(solution)/shard_map/all_to_all | solution.py:473
  252.2 1.1 copy-done.10
  253.2 13.5 %attend.1 = bf16[1024,896]{1,0:T(8,128)(2,1)} custom-call(s32[16]{0:T(128)} %order.3, bf16[5,4,1024,256]{3,2,1,0:T(8,128)(2,1)} %get-tuple-element.35.probs, f32[5,128,1024]{2,1,0:T(8,128)} %get-tuple-element.36.attended, bf16[5,1024,128]{2,1,0:T(8,128)(2,1)} %get-tuple-element.37.q, bf16[2,1024,128]{2,1,0:T(8,128)(2,1)} %get-tuple-element.38.kv, ...), custom_call_target="tpu_custom_call" | custom-call | flops 5368709120 | bytes 16777216 | tf_op jit(solution)/shard_map/attend/pallas_call | solution.py:389
  266.8 28.5 %all_to_all.27 = bf16[8,128,896]{2,1,0:T(8,128)(2,1)S(1)} all-to-all(bf16[8,128,896]{2,1,0:T(8,128)(2,1)} %bitcast.31), channel_id=1, replica_groups=mesh['ctx'=8,'exp'=16] {'ctx'}, dimensions={0} | all-to-all | bytes 3670016 | tf_op jit(solution)/shard_map/all_to_all | solution.py:473
  296.3 1.5 reshape.53
  297.9 0.8 reshape.55
  298.9 0.8 reshape.54
  (60 shorter events, 6.3 us)
Async XLA Ops:
  2.2 1.3 copy-start
  3.5 1.3 copy-start.2
  4.8 0.7 copy-start.5
  31.9 23.2 %copy-start.4 = (bf16[64,5120]{1,0:T(8,128)(2,1)}, bf16[64,5120]{1,0:T(8,128)(2,1)S(1)}, u32[]{:S(2)}) copy-start(bf16[64,5120]{1,0:T(8,128)(2,1)S(1)} %get-tuple-element.25.refs_4_.refs_5_) | copy-start | bytes 1966084
  31.9 19.6 %collective-permute-start.9 = (bf16[64,5120]{1,0:T(8,128)(2,1)S(1)}, bf16[64,5120]{1,0:T(8,128)(2,1)S(1)}, u32[]{:S(2)}, u32[]{:S(2)}) collective-permute-start(bf16[64,5120]{1,0:T(8,128)(2,1)S(1)} %get-tuple-element.25.refs_4_.refs_5_), channel_id=1, source_target_pairs={{0,64},{16,80},{32,96},{48,112},{64,0},{80,16},{96,32},{112,48},{1... | collective-permute-start | bytes 1966088 | tf_op jit(solution)/shard_map/ppermute | solution.py:433
  35.9 19.2 %collective-permute-start = (bf16[64,5120]{1,0:T(8,128)(2,1)S(1)}, bf16[64,5120]{1,0:T(8,128)(2,1)S(1)}, u32[]{:S(2)}, u32[]{:S(2)}) collective-permute-start(bf16[64,5120]{1,0:T(8,128)(2,1)S(1)} %get-tuple-element.24), channel_id=1, source_target_pairs={{0,16},{16,0},{32,48},{48,32},{64,80},{80,64},{96,112},{112,96},{1... | collective-permute-start | bytes 1966088 | tf_op jit(solution)/shard_map/ppermute | solution.py:437
  38.6 28.0 %collective-permute-start.7 = (bf16[64,5120]{1,0:T(8,128)(2,1)S(1)}, bf16[64,5120]{1,0:T(8,128)(2,1)S(1)}, u32[]{:S(2)}, u32[]{:S(2)}) collective-permute-start(bf16[64,5120]{1,0:T(8,128)(2,1)S(1)} %get-tuple-element.25.refs_4_.refs_5_), channel_id=1, source_target_pairs={{0,96},{16,112},{32,0},{48,16},{64,32},{80,48},{96,64},{112,80},{1... | collective-permute-start | bytes 1966088 | tf_op jit(solution)/shard_map/ppermute | solution.py:433
  39.3 29.9 %collective-permute-start.5 = (bf16[64,5120]{1,0:T(8,128)(2,1)S(1)}, bf16[64,5120]{1,0:T(8,128)(2,1)}, u32[]{:S(2)}, u32[]{:S(2)}) collective-permute-start(bf16[64,5120]{1,0:T(8,128)(2,1)S(1)} %get-tuple-element.25.refs_4_.refs_5_), channel_id=1, source_target_pairs={{0,32},{16,48},{32,64},{48,80},{64,96},{80,112},{96,0},{112,16},{1... | collective-permute-start | bytes 1966088 | tf_op jit(solution)/shard_map/ppermute | solution.py:433
  40.6 28.6 %collective-permute-start.4 = (bf16[64,5120]{1,0:T(8,128)(2,1)S(1)}, bf16[64,5120]{1,0:T(8,128)(2,1)S(1)}, u32[]{:S(2)}, u32[]{:S(2)}) collective-permute-start(bf16[64,5120]{1,0:T(8,128)(2,1)S(1)} %get-tuple-element.25.refs_4_.refs_5_), channel_id=1, source_target_pairs={{0,16},{16,0},{32,48},{48,32},{64,80},{80,64},{96,112},{112,96},{1... | collective-permute-start | bytes 1966088 | tf_op jit(solution)/shard_map/ppermute | solution.py:437
  51.5 37.3 %copy-start.12 = (bf16[64,5120]{1,0:T(8,128)(2,1)}, bf16[64,5120]{1,0:T(8,128)(2,1)S(1)}, u32[]{:S(2)}) copy-start(bf16[64,5120]{1,0:T(8,128)(2,1)S(1)} %collective-permute-done.9.refs_10_.refs_11_) | copy-start | bytes 1966084
  51.5 31.6 %collective-permute-start.10 = (bf16[64,5120]{1,0:T(8,128)(2,1)S(1)}, bf16[64,5120]{1,0:T(8,128)(2,1)S(1)}, u32[]{:S(2)}, u32[]{:S(2)}) collective-permute-start(bf16[64,5120]{1,0:T(8,128)(2,1)S(1)} %collective-permute-done.9.refs_10_.refs_11_), channel_id=1, source_target_pairs={{0,16},{16,0},{32,48},{48,32},{64,80},{80,64},{96,112},{112,96},{1... | collective-permute-start | bytes 1966088 | tf_op jit(solution)/shard_map/ppermute | solution.py:437
  55.1 33.7 %copy-start.8 = (bf16[128,5120]{1,0:T(8,128)(2,1)}, bf16[128,5120]{1,0:T(8,128)(2,1)S(1)}, u32[]{:S(2)}) copy-start(bf16[128,5120]{1,0:T(8,128)(2,1)S(1)} %constant_dynamic-update-slice_fusion.refs_0_.refs_1_) | copy-start | bytes 3932164
  55.1 54.4 %collective-permute-start.3 = (bf16[128,5120]{1,0:T(8,128)(2,1)S(1)}, bf16[128,5120]{1,0:T(8,128)(2,1)S(1)}, u32[]{:S(2)}, u32[]{:S(2)}) collective-permute-start(bf16[128,5120]{1,0:T(8,128)(2,1)S(1)} %constant_dynamic-update-slice_fusion.refs_0_.refs_1_), channel_id=1, source_target_pairs={{0,64},{16,80},{32,96},{48,112},{64,0},{80,16},{96,32},{112,48},{1... | collective-permute-start | bytes 3932168 | tf_op jit(solution)/shard_map/ppermute | solution.py:433
  66.6 22.2 %copy-start.13 = (bf16[64,5120]{1,0:T(8,128)(2,1)}, bf16[64,5120]{1,0:T(8,128)(2,1)S(1)}, u32[]{:S(2)}) copy-start(bf16[64,5120]{1,0:T(8,128)(2,1)S(1)} %collective-permute-done.7.refs_8_.refs_9_) | copy-start | bytes 1966084
  66.6 54.8 %collective-permute-start.2 = (bf16[128,5120]{1,0:T(8,128)(2,1)S(1)}, bf16[128,5120]{1,0:T(8,128)(2,1)}, u32[]{:S(2)}, u32[]{:S(2)}) collective-permute-start(bf16[128,5120]{1,0:T(8,128)(2,1)S(1)} %constant_dynamic-update-slice_fusion.refs_0_.refs_1_), channel_id=1, source_target_pairs={{0,96},{16,112},{32,0},{48,16},{64,32},{80,48},{96,64},{112,80},{1... | collective-permute-start | bytes 3932168 | tf_op jit(solution)/shard_map/ppermute | solution.py:433
  69.2 52.2 %collective-permute-start.1 = (bf16[128,5120]{1,0:T(8,128)(2,1)S(1)}, bf16[128,5120]{1,0:T(8,128)(2,1)}, u32[]{:S(2)}, u32[]{:S(2)}) collective-permute-start(bf16[128,5120]{1,0:T(8,128)(2,1)S(1)} %constant_dynamic-update-slice_fusion.refs_0_.refs_1_), channel_id=1, source_target_pairs={{0,32},{16,48},{32,64},{48,80},{64,96},{80,112},{96,0},{112,16},{1... | collective-permute-start | bytes 3932168 | tf_op jit(solution)/shard_map/ppermute | solution.py:433
  69.2 13.9 %copy-start.14 = (bf16[64,5120]{1,0:T(8,128)(2,1)}, bf16[64,5120]{1,0:T(8,128)(2,1)S(1)}, u32[]{:S(2)}) copy-start(bf16[64,5120]{1,0:T(8,128)(2,1)S(1)} %collective-permute-done.4.refs_5_.refs_6_) | copy-start | bytes 1966084
  69.2 28.0 %collective-permute-start.8 = (bf16[64,5120]{1,0:T(8,128)(2,1)S(1)}, bf16[64,5120]{1,0:T(8,128)(2,1)}, u32[]{:S(2)}, u32[]{:S(2)}) collective-permute-start(bf16[64,5120]{1,0:T(8,128)(2,1)S(1)} %collective-permute-done.7.refs_8_.refs_9_), channel_id=1, source_target_pairs={{0,16},{16,0},{32,48},{48,32},{64,80},{80,64},{96,112},{112,96},{1... | collective-permute-start | bytes 1966088 | tf_op jit(solution)/shard_map/ppermute | solution.py:437
  83.1 2.7 copy-start.15
  83.1 26.4 %collective-permute-start.6 = (bf16[64,5120]{1,0:T(8,128)(2,1)}, bf16[64,5120]{1,0:T(8,128)(2,1)}, u32[]{:S(2)}, u32[]{:S(2)}) collective-permute-start(bf16[64,5120]{1,0:T(8,128)(2,1)} %collective-permute-done.5.refs_6_.refs_7_), channel_id=1, source_target_pairs={{0,16},{16,0},{32,48},{48,32},{64,80},{80,64},{96,112},{112,96},{1... | collective-permute-start | bytes 1966088 | tf_op jit(solution)/shard_map/ppermute | solution.py:437
  109.6 11.9 %copy-start.9 = (bf16[128,5120]{1,0:T(8,128)(2,1)}, bf16[128,5120]{1,0:T(8,128)(2,1)S(1)}, u32[]{:S(2)}) copy-start(bf16[128,5120]{1,0:T(8,128)(2,1)S(1)} %collective-permute-done.3.refs_3_.refs_4_) | copy-start | bytes 3932164
  121.4 36.6 %all-to-all-start.1 = ((bf16[8,128,896]{2,1,0:T(8,128)(2,1)}), bf16[8,128,896]{2,1,0:T(8,128)(2,1)S(1)}, u32[]{:S(2)}, u32[]{:S(2)}) async-start(bf16[8,128,896]{2,1,0:T(8,128)(2,1)} %hold.2), calls=%async_computation.1 | async-start | bytes 3670016 | tf_op jit(solution)/shard_map/all_to_all | solution.py:473
  152.4 31.2 %collective-permute-start.11 = (bf16[64,5120]{1,0:T(8,128)(2,1)}, bf16[64,5120]{1,0:T(8,128)(2,1)S(1)}, u32[]{:S(2)}, u32[]{:S(2)}) collective-permute-start(bf16[64,5120]{1,0:T(8,128)(2,1)} %get-tuple-element.29), channel_id=1, source_target_pairs={{0,96},{16,112},{32,0},{48,16},{64,32},{80,48},{96,64},{112,80},{1... | collective-permute-start | bytes 1966088 | tf_op jit(solution)/shard_map/ppermute | solution.py:433
  155.7 31.4 %collective-permute-start.12 = (bf16[64,5120]{1,0:T(8,128)(2,1)}, bf16[64,5120]{1,0:T(8,128)(2,1)}, u32[]{:S(2)}, u32[]{:S(2)}) collective-permute-start(bf16[64,5120]{1,0:T(8,128)(2,1)} %get-tuple-element.30), channel_id=1, source_target_pairs={{0,32},{16,48},{32,64},{48,80},{64,96},{80,112},{96,0},{112,16},{1... | collective-permute-start | bytes 1966088 | tf_op jit(solution)/shard_map/ppermute | solution.py:433
  155.7 31.4 %collective-permute-start.13 = (bf16[64,5120]{1,0:T(8,128)(2,1)}, bf16[64,5120]{1,0:T(8,128)(2,1)}, u32[]{:S(2)}, u32[]{:S(2)}) collective-permute-start(bf16[64,5120]{1,0:T(8,128)(2,1)} %get-tuple-element.31), channel_id=1, source_target_pairs={{0,64},{16,80},{32,96},{48,112},{64,0},{80,16},{96,32},{112,48},{1... | collective-permute-start | bytes 1966088 | tf_op jit(solution)/shard_map/ppermute | solution.py:433
  158.0 1.2 copy-start.7
  159.2 27.8 %copy-start.16 = (bf16[64,5120]{1,0:T(8,128)(2,1)S(1)}, bf16[64,5120]{1,0:T(8,128)(2,1)}, u32[]{:S(2)}) copy-start(bf16[64,5120]{1,0:T(8,128)(2,1)} %get-tuple-element.28) | copy-start | bytes 1966084
  159.2 32.6 %collective-permute-start.15 = (bf16[128,5120]{1,0:T(8,128)(2,1)}, bf16[128,5120]{1,0:T(8,128)(2,1)S(1)}, u32[]{:S(2)}, u32[]{:S(2)}) collective-permute-start(bf16[128,5120]{1,0:T(8,128)(2,1)} %hold.3), channel_id=1, source_target_pairs={{0,16},{16,0},{32,48},{48,32},{64,80},{80,64},{96,112},{112,96},{1... | collective-permute-start | bytes 3932168 | tf_op jit(solution)/shard_map/ppermute | solution.py:437
  187.1 4.8 %copy-start.11 = (bf16[128,5120]{1,0:T(8,128)(2,1)S(1)}, bf16[128,5120]{1,0:T(8,128)(2,1)}, u32[]{:S(2)}) copy-start(bf16[128,5120]{1,0:T(8,128)(2,1)} %get-tuple-element.32) | copy-start | bytes 3932164
  188.8 8.7 %collective-permute-start.14 = (bf16[32,5120]{1,0:T(8,128)(2,1)S(1)}, bf16[32,5120]{1,0:T(8,128)(2,1)S(1)}, u32[]{:S(2)}, u32[]{:S(2)}) collective-permute-start(bf16[32,5120]{1,0:T(8,128)(2,1)S(1)} %slice.47), channel_id=1, source_target_pairs={{0,16},{16,0},{32,48},{48,32},{64,80},{80,64},{96,112},{112,96},{1... | collective-permute-start | bytes 983048 | tf_op jit(solution)/shard_map/ppermute | solution.py:437
  192.3 11.9 %collective-permute-start.18 = (bf16[32,5120]{1,0:T(8,128)(2,1)S(1)}, bf16[32,5120]{1,0:T(8,128)(2,1)S(1)}, u32[]{:S(2)}, u32[]{:S(2)}) collective-permute-start(bf16[32,5120]{1,0:T(8,128)(2,1)S(1)} %get-tuple-element.44), channel_id=1, source_target_pairs={{0,64},{16,80},{32,96},{48,112},{64,0},{80,16},{96,32},{112,48},{1... | collective-permute-start | bytes 983048 | tf_op jit(solution)/shard_map/ppermute | solution.py:433
  193.0 14.7 %collective-permute-start.17 = (bf16[32,5120]{1,0:T(8,128)(2,1)S(1)}, bf16[32,5120]{1,0:T(8,128)(2,1)S(1)}, u32[]{:S(2)}, u32[]{:S(2)}) collective-permute-start(bf16[32,5120]{1,0:T(8,128)(2,1)S(1)} %get-tuple-element.45), channel_id=1, source_target_pairs={{0,32},{16,48},{32,64},{48,80},{64,96},{80,112},{96,0},{112,16},{1... | collective-permute-start | bytes 983048 | tf_op jit(solution)/shard_map/ppermute | solution.py:433
  194.3 13.3 %collective-permute-start.16 = (bf16[32,5120]{1,0:T(8,128)(2,1)S(1)}, bf16[32,5120]{1,0:T(8,128)(2,1)S(1)}, u32[]{:S(2)}, u32[]{:S(2)}) collective-permute-start(bf16[32,5120]{1,0:T(8,128)(2,1)S(1)} %get-tuple-element.46), channel_id=1, source_target_pairs={{0,96},{16,112},{32,0},{48,16},{64,32},{80,48},{96,64},{112,80},{1... | collective-permute-start | bytes 983048 | tf_op jit(solution)/shard_map/ppermute | solution.py:433
  207.6 15.5 %copy-start.3 = (bf16[1,128,5120]{2,1,0:T(8,128)(2,1)S(1)}, bf16[1,128,5120]{2,1,0:T(8,128)(2,1)}, u32[]{:S(2)}) copy-start(bf16[1,128,5120]{2,1,0:T(8,128)(2,1)} %param.16) | copy-start | bytes 3932164
  207.7 15.5 %copy-start.6 = (f32[5120]{0:T(1024)S(1)}, f32[5120]{0:T(1024)}, u32[]{:S(2)}) copy-start(f32[5120]{0:T(1024)} %param.20) | copy-start | bytes 61444
  208.1 15.1 %copy-start.1 = (bf16[1,128,5120]{2,1,0:T(8,128)(2,1)S(1)}, bf16[1,128,5120]{2,1,0:T(8,128)(2,1)}, u32[]{:S(2)}) copy-start(bf16[1,128,5120]{2,1,0:T(8,128)(2,1)} %param.15) | copy-start | bytes 3932164
  226.6 25.5 %all-to-all-start.3 = ((bf16[8,128,640]{2,1,0:T(8,128)(2,1)}), bf16[8,128,640]{2,1,0:T(8,128)(2,1)S(1)}, u32[]{:S(2)}, u32[]{:S(2)}) async-start(bf16[8,128,640]{2,1,0:T(8,128)(2,1)} %get-tuple-element.39), calls=%async_computation.3 | async-start | bytes 2621440 | tf_op jit(solution)/shard_map/all_to_all | solution.py:473
  252.2 1.1 copy-start.10

commit v3 on v2

--- a/solution.py
+++ b/solution.py
@@ -26,7 +26,7 @@
 NQ = SEQ // QB
 GW = GROUP * DH
 HALF = D // 2
-ROWS = 512
+ROWS = 256
 FIRST = 64
 KB = 1024
 TB = 1024
@@ -119,10 +119,9 @@
     )(shard)
 
 
-def project_kernel(*refs):
-    tops = refs[:4]
-    rests = refs[4:12]
-    w_gate, w_in, w_out, grad_gate, grad_up, x_at, r_at, gate, up, backed = refs[12:]
+def project_kernel(n_pieces, *refs):
+    pieces = refs[:n_pieces]
+    w_gate, w_in, w_out, grad_gate, grad_up, x_at, r_at, gate, up, backed = refs[n_pieces:]
     step = pl.program_id(0)
 
     @pl.when(step == 0)
@@ -131,13 +130,12 @@
         up[...] = jnp.zeros_like(up)
         backed[...] = jnp.zeros_like(backed)
 
-    for at in range(8):
-        top = tops[at // 2][(at % 2) * FIRST:(at % 2 + 1) * FIRST, :]
-        low = rests[at]
-        x_at[at * 64:at * 64 + 32, :] = top[:32]
-        x_at[at * 64 + 32:at * 64 + 64, :] = low[:32]
-        r_at[at * 64:at * 64 + 32, :] = top[32:]
-        r_at[at * 64 + 32:at * 64 + 64, :] = low[32:]
+    at = 0
+    for piece in pieces:
+        for low in range(0, piece.shape[0], 64):
+            x_at[at:at + 32, :] = piece[low:low + 32, :]
+            r_at[at:at + 32, :] = piece[low + 32:low + 64, :]
+            at += 32
     gate[...] += nn(x_at[...], w_gate[0])
     up[...] += nn(x_at[...], w_in[0])
     backed[...] += nt(r_at[...], w_out[0])
@@ -160,7 +158,7 @@
         pl.BlockSpec((1, FFD, KB), lambda i: (0, 0, i)),
     ]
     return pl.pallas_call(
-        project_kernel,
+        functools.partial(project_kernel, len(pieces)),
         grid=(D // KB,),
         out_shape=[sds((ROWS, FFD))] * 2,
         in_specs=in_specs,
@@ -175,31 +173,31 @@
     )(*pieces, w_gate, w_in, w_out)
 
 
-TERM_ROWS = (64, 64, 64, 64, 128, 128)
-
-
-def term_kernel(grad_gate, grad_up, w_gate, w_in, *outs):
+def term_kernel(by_z, grad_gate, grad_up, w_gate, w_in, *outs):
     block = nt(grad_gate[...], w_gate[0]) + nt(grad_up[...], w_in[0])
     block = block.astype(BF16)
-    for k in range(4):
+    for z in range(4):
         for side in range(2):
-            at = (2 * k + side) * 64
-            outs[k][side * 32:(side + 1) * 32, :] = block[at:at + 32]
-            outs[4 + side][k * 32:(k + 1) * 32, :] = block[at + 32:at + 64]
-
-
-def terms(grad_gate, grad_up, w_gate, w_in):
+            rows = block[(2 * z + side) * 32:(2 * z + side + 1) * 32]
+            if by_z:
+                outs[z][side * 32:(side + 1) * 32, :] = rows
+            else:
+                outs[side][z * 32:(z + 1) * 32, :] = rows
+
+
+def terms(by_z, grad_gate, grad_up, w_gate, w_in):
     whole = pl.BlockSpec(grad_gate.shape, lambda i: (0, 0))
     weight = pl.BlockSpec((1, TB, FFD), lambda i: (0, i, 0))
-    return pl.pallas_call(
-        term_kernel,
+    sizes = (64,) * 4 if by_z else (128,) * 2
+    return pl.pallas_call(
+        functools.partial(term_kernel, by_z),
         grid=(D // TB,),
-        out_shape=[sds((r, D)) for r in TERM_ROWS],
+        out_shape=[sds((r, D)) for r in sizes],
         in_specs=[whole, whole, weight, weight],
-        out_specs=[pl.BlockSpec((r, TB), lambda i: (0, i)) for r in TERM_ROWS],
-        compiler_params=params(),
+        out_specs=[pl.BlockSpec((r, TB), lambda i: (0, i)) for r in sizes],
+        compiler_params=params(60),
         cost_estimate=pl.CostEstimate(
-            flops=4 * ROWS * D * FFD, bytes_accessed=16 * 1024 * 1024, transcendentals=0
+            flops=4 * ROWS * D * FFD, bytes_accessed=14 * 1024 * 1024, transcendentals=0
         ),
         name="terms",
     )(grad_gate, grad_up, w_gate, w_in)
@@ -428,6 +426,28 @@
     )(x, *others)
 
 
+def place_kernel(block, dq, dk, dv):
+    dq[...] = block[0, :, :GW]
+    dk[...] = block[0, :, GW:GW + DH]
+    dv[...] = block[0, :, GW + DH:]
+
+
+def place(blocks):
+    return pl.pallas_call(
+        place_kernel,
+        grid=(KVH,),
+        out_shape=[sds((TOK, D)), sds((TOK, KVH * DH)), sds((TOK, KVH * DH))],
+        in_specs=[pl.BlockSpec((1, TOK, GW + 2 * DH), lambda i: (i, 0, 0))],
+        out_specs=[
+            pl.BlockSpec((TOK, GW), lambda i: (0, i)),
+            pl.BlockSpec((TOK, DH), lambda i: (0, i)),
+            pl.BlockSpec((TOK, DH), lambda i: (0, i)),
+        ],
+        compiler_params=params(24),
+        name="place",
+    )(blocks)
+
+
 def along_z(x, shift):
     pairs = [(c, ((c // 2 + shift) % 4) * 2 + c % 2) for c in range(8)]
     return lax.ppermute(x, "ctx", pairs)
@@ -446,13 +466,13 @@
     rests = []
     for p in [b] + b_z:
         rests += [p, across_x(p)]
-    return [a_both] + a_z + rests
-
-
-def scatter_sums(groups, tie):
-    a_own, b_own, b_far = groups[0], groups[4], groups[5]
+    return [a_both] + a_z, rests
+
+
+def scatter_sums(a_groups, b_groups, tie):
+    a_own, (b_own, b_far) = a_groups[0], b_groups
     b_got = across_x(hold(b_far, tie))
-    a_got = [along_z(g, -k) for g, k in zip(groups[1:4], SHIFTS)]
+    a_got = [along_z(g, -k) for g, k in zip(a_groups[1:], SHIFTS)]
     b_sum = b_own.astype(F32) + b_got.astype(F32)
     b_low = b_sum.astype(BF16)
     b_back = [
@@ -492,23 +512,25 @@
         stream[0], out_grad[0], route_weight.reshape(TOK, 1), expert_ids[0], gain
     )
     shard = swap_exp(outgoing.reshape(EXPERTS, 8, D)).reshape(TOK, D)
-    pieces = gather_pieces(shard)
-    by_head = hold(cut_heads(query_rows[0], key_rows[0], value_rows[0]), *pieces)
+    a_pieces, b_pieces = gather_pieces(shard)
+    by_head = hold(
+        cut_heads(query_rows[0], key_rows[0], value_rows[0]), *b_pieces
+    )
     qkv = swap_ctx(by_head).reshape(SEQ, GW + 2 * DH)
-    grad_gate, grad_up = project(pieces, expert_gate, expert_in, expert_out)
-    settled = scatter_sums(terms(grad_gate, grad_up, expert_gate, expert_in), qkv)
+    weights = (expert_gate, expert_in, expert_out)
+    b_groups = terms(False, *project(b_pieces, *weights), expert_gate, expert_in)
+    a_pieces[0] = hold(a_pieces[0], b_groups[0])
+    a_groups = terms(True, *project(a_pieces, *weights), expert_gate, expert_in)
+    settled = scatter_sums(a_groups, b_groups, qkv)
     part = swap_exp(settled.reshape(EXPERTS, 8, HALF)).reshape(TOK, HALF)
     probs, attended, q_sorted, kv_sorted = make_probs(span_order, qkv)
     grad_total, grad_cut = finish(stream[0], out_grad[0], gain, picks, part)
     grads = swap_ctx(grad_cut).reshape(SEQ, GW)
     result = attend(span_order, probs, attended, q_sorted, kv_sorted, grads)
-    back = swap_ctx(result.reshape(KVH, TOK, GW + 2 * DH)).transpose(1, 0, 2)
-    return (
-        grad_total[None],
-        back[:, :, :GW].reshape(1, TOK, D),
-        back[:, :, GW:GW + DH].reshape(1, TOK, KVH * DH),
-        back[:, :, GW + DH:].reshape(1, TOK, KVH * DH),
+    grad_query, grad_key, grad_value = place(
+        swap_ctx(result.reshape(KVH, TOK, GW + 2 * DH))
     )
+    return grad_total[None], grad_query[None], grad_key[None], grad_value[None]
 
 
 def solution(mesh):

time: 301 us -> 298 us (0.990)
  waiting for transfers between devices: 104 us -> 86.8 us
  Pallas kernels: 61.5 us -> 77.6 us
  local copies, waits for them, and re-layouts: 11.9 us -> 8.34 us
    ppermute x12, waiting for transfers between devices: 65.6 us -> 48.8 us  [along_z(): return lax.ppermute(x, 'ctx', pairs)]
    pallas_call x2 -> x5, Pallas kernels: 24.9 us -> 41 us  [the longest x2 21.6 us: project(): pl.pallas_call(functools.partial(project_kernel, len(pieces)), grid=(D //...]
    reshape x3 -> x0, local copies, waits for them, and re-layouts: 3.1 us -> none  [the longest x1 1.47 us: body(): back[:, :, :GW].reshape(1, TOK, D)]
    unnamed x35 -> x37, local copies, waits for them, and re-layouts: 5.73 us -> 6.58 us
  transfers between devices with their start and end apart: 21 -> 21, of which waited for: 13 -> 11; matrix products, arithmetic and copies ran while one was open for 1% -> 1% of each run, Pallas kernels for 14% -> 19%
where the time goes in v3:
time: 298 us; the launch traced here: 297 us
  waiting for transfers between devices  86.8 us (29%)
  Pallas kernels  77.6 us (26%)
  blocking collectives  70.2 us (24%)
  starting transfers between devices  51.6 us (17%)
  local copies, waits for them, and re-layouts  8.34 us (3%)
    ppermute x12, waiting for transfers between devices, along_z(): return lax.ppermute(x, 'ctx', pairs)  48.8 us
    all_to_all x2, blocking collectives, swap_exp(): return lax.all_to_all(x, 'exp', split_axis=0, concat_axis=0, tiled=True)  41.7 us
    ppermute x7, waiting for transfers between devices, across_x(): return lax.ppermute(x, 'ctx', [(c, c ^ 1) for c in range(8)])  32.5 us
    all_to_all x1, blocking collectives, swap_ctx(): return lax.all_to_all(x, 'ctx', split_axis=0, concat_axis=0, tiled=True)  28.5 us
    ppermute x12, starting transfers between devices, along_z(): return lax.ppermute(x, 'ctx', pairs)  23.6 us
    pallas_call x2, Pallas kernels, project(): pl.pallas_call(functools.partial(project_kernel, len(pieces)), grid=(D //...  21.6 us
    ppermute x7, starting transfers between devices, across_x(): return lax.ppermute(x, 'ctx', [(c, c ^ 1) for c in range(8)])  17.8 us
    pallas_call x2, Pallas kernels, terms(): pl.pallas_call(functools.partial(term_kernel, by_z), grid=(D // TB,), out...  16.5 us
  transfers between devices with their start and end apart: 21, of which 11 were waited for; matrix products, arithmetic and copies ran while one was open for 1% of the time, Pallas kernels for 19%

profile of v3, /device:TPU:0, one launch (start us, length us, event | category | flops | bytes accessed | tf_op | source)
XLA Modules:
  0.0 297.4 jit_solution(4187329354427635305)
XLA Ops:
  0.6 0.8 copy.19.weight
  2.2 1.3 copy-done
  3.5 1.3 copy-done.2
  5.5 1.2 dispatch.1
  6.7 24.7 %all_to_all.25 = bf16[16,8,5120]{2,1,0:T(8,128)(2,1)S(1)} all-to-all(bf16[16,8,5120]{2,1,0:T(8,128)(2,1)S(1)} %bitcast.26), channel_id=1, replica_groups=mesh['ctx'=8,'exp'=16] {'exp'}, dimensions={0} | all-to-all | bytes 2621440 | tf_op jit(solution)/shard_map/all_to_all | solution.py:489
  31.9 4.0 %collective-permute-start.6 = (bf16[64,5120]{1,0:T(8,128)(2,1)S(1)}, bf16[64,5120]{1,0:T(8,128)(2,1)S(1)}, u32[]{:S(2)}, u32[]{:S(2)}) collective-permute-start(bf16[64,5120]{1,0:T(8,128)(2,1)S(1)} %get-tuple-element.30.refs_0_.refs_1_), channel_id=1, source_target_pairs={{0,64},{16,80},{32,96},{48,112},{64,0},{80,16},{96,32},{112,48},{1... | collective-permute-start | bytes 1966088 | tf_op jit(solution)/shard_map/ppermute | solution.py:453
  35.9 2.7 collective-permute-start
  39.3 1.3 collective-permute-start.2
  40.6 0.8 collective-permute-start.1
  41.4 10.1 %collective-permute-done.6.refs_6_.refs_7_ = bf16[64,5120]{1,0:T(8,128)(2,1)S(1)} collective-permute-done((bf16[64,5120]{1,0:T(8,128)(2,1)S(1)}, bf16[64,5120]{1,0:T(8,128)(2,1)S(1)}, u32[]{:S(2)}, u32[]{:S(2)}) %collective-permute-start.6) | collective-permute-done | bytes 655392 | tf_op jit(solution)/shard_map/ppermute | solution.py:453
  51.5 2.7 collective-permute-start.7
  55.1 2.9 collective-permute-start.10
  58.0 8.6 %collective-permute-done.4.refs_4_.refs_5_ = bf16[64,5120]{1,0:T(8,128)(2,1)S(1)} collective-permute-done((bf16[64,5120]{1,0:T(8,128)(2,1)S(1)}, bf16[64,5120]{1,0:T(8,128)(2,1)S(1)}, u32[]{:S(2)}, u32[]{:S(2)}) %collective-permute-start.4) | collective-permute-done | bytes 655392 | tf_op jit(solution)/shard_map/ppermute | solution.py:453
  66.6 2.6 collective-permute-start.9
  69.2 2.8 collective-permute-start.5
  72.0 11.1 %collective-permute-done.7.refs_7_.refs_8_ = bf16[64,5120]{1,0:T(8,128)(2,1)S(1)} collective-permute-done((bf16[64,5120]{1,0:T(8,128)(2,1)S(1)}, bf16[64,5120]{1,0:T(8,128)(2,1)S(1)}, u32[]{:S(2)}, u32[]{:S(2)}) %collective-permute-start.7) | collective-permute-done | bytes 655392 | tf_op jit(solution)/shard_map/ppermute | solution.py:457
  83.1 2.7 collective-permute-start.3
  85.9 2.9 cut_heads.1.refs_0_
  88.8 8.5 %collective-permute-done.5.refs_5_.refs_6_ = bf16[64,5120]{1,0:T(8,128)(2,1)} collective-permute-done((bf16[64,5120]{1,0:T(8,128)(2,1)S(1)}, bf16[64,5120]{1,0:T(8,128)(2,1)}, u32[]{:S(2)}, u32[]{:S(2)}) %collective-permute-start.5) | collective-permute-done | bytes 655392 | tf_op jit(solution)/shard_map/ppermute | solution.py:457
  97.3 12.2 %collective-permute-done.3.refs_3_.refs_4_ = bf16[64,5120]{1,0:T(8,128)(2,1)S(1)} collective-permute-done((bf16[64,5120]{1,0:T(8,128)(2,1)S(1)}, bf16[64,5120]{1,0:T(8,128)(2,1)S(1)}, u32[]{:S(2)}, u32[]{:S(2)}) %collective-permute-start.3) | collective-permute-done | bytes 655392 | tf_op jit(solution)/shard_map/ppermute | solution.py:457
  109.4 0.8 copy-done.15
  110.3 4.4 %all-to-all-start.1 = ((bf16[8,128,896]{2,1,0:T(8,128)(2,1)}), bf16[8,128,896]{2,1,0:T(8,128)(2,1)S(1)}, u32[]{:S(2)}, u32[]{:S(2)}) async-start(bf16[8,128,896]{2,1,0:T(8,128)(2,1)} %hold.4), calls=%async_computation.1 | async-start | bytes 3670016 | tf_op jit(solution)/shard_map/all_to_all | solution.py:493
  114.7 10.9 %project.2 = (bf16[256,512]{1,0:T(8,128)(2,1)}, bf16[256,512]{1,0:T(8,128)(2,1)}) custom-call(bf16[64,5120]{1,0:T(8,128)(2,1)} %copy-done.4, bf16[64,5120]{1,0:T(8,128)(2,1)} %copy-done.13, bf16[64,5120]{1,0:T(8,128)(2,1)} %copy-done.12, bf16[64,5120]{1,0:T(8,128)(2,1)} %copy-done.15, bf16[64,5120]{1,0:T(8,128)(2,1)} %copy-done.11, ...), custom_call_target="tpu_custom_call" | custom-call | flops 4026531840 | bytes 29360128 | tf_op jit(solution)/shard_map/project/pallas_call | solution.py:160
  125.6 8.3 %terms.2 = (bf16[128,5120]{1,0:T(8,128)(2,1)}, bf16[128,5120]{1,0:T(8,128)(2,1)}) custom-call(bf16[256,512]{1,0:T(8,128)(2,1)} %get-tuple-element.31.grad_gate, bf16[256,512]{1,0:T(8,128)(2,1)} %get-tuple-element.32.grad_up, bf16[1,5120,512]{2,1,0:T(8,128)(2,1)} %w_gate.3, bf16[1,5120,512]{2,1,0:T(8,128)(2,1)} %w_in.3), custom_call_target="tpu_custom_call" | custom-call | flops 2684354560 | bytes 14680064 | tf_op jit(solution)/shard_map/terms/pallas_call | solution.py:192
  134.0 10.8 %project.3 = (bf16[256,512]{1,0:T(8,128)(2,1)}, bf16[256,512]{1,0:T(8,128)(2,1)}) custom-call(bf16[128,5120]{1,0:T(8,128)(2,1)} %hold.3.refs_0_, bf16[128,5120]{1,0:T(8,128)(2,1)} %collective-permute-done.8.refs_1_, bf16[128,5120]{1,0:T(8,128)(2,1)} %collective-permute-done.9.refs_2_, bf16[128,5120]{1,0:T(8,128)(2,1)} %collective-permute-done.10.refs_3_, ...), custom_call_target="tpu_custom_call" | custom-call | flops 4026531840 | bytes 29360128 | tf_op jit(solution)/shard_map/project/pallas_call | solution.py:160
  144.7 8.1 %terms.3 = (bf16[64,5120]{1,0:T(8,128)(2,1)}, bf16[64,5120]{1,0:T(8,128)(2,1)}, bf16[64,5120]{1,0:T(8,128)(2,1)}, bf16[64,5120]{1,0:T(8,128)(2,1)}) custom-call(bf16[256,512]{1,0:T(8,128)(2,1)} %get-tuple-element.34.grad_gate, bf16[256,512]{1,0:T(8,128)(2,1)} %get-tuple-element.35.grad_up, bf16[1,5120,512]{2,1,0:T(8,128)(2,1)} %w_gate.3, ...), custom_call_target="tpu_custom_call" | custom-call | flops 2684354560 | bytes 14680064 | tf_op jit(solution)/shard_map/terms/pallas_call | solution.py:192
  152.9 3.2 %collective-permute-start.11 = (bf16[64,5120]{1,0:T(8,128)(2,1)}, bf16[64,5120]{1,0:T(8,128)(2,1)S(1)}, u32[]{:S(2)}, u32[]{:S(2)}) collective-permute-start(bf16[64,5120]{1,0:T(8,128)(2,1)} %get-tuple-element.37), channel_id=1, source_target_pairs={{0,96},{16,112},{32,0},{48,16},{64,32},{80,48},{96,64},{112,80},{1... | collective-permute-start | bytes 1966088 | tf_op jit(solution)/shard_map/ppermute | solution.py:453
  156.1 2.4 collective-permute-start.13
  158.5 1.2 copy-done.8
  159.8 3.0 collective-permute-start.15
  162.7 19.7 %collective-permute-done.11 = bf16[64,5120]{1,0:T(8,128)(2,1)S(1)} collective-permute-done((bf16[64,5120]{1,0:T(8,128)(2,1)}, bf16[64,5120]{1,0:T(8,128)(2,1)S(1)}, u32[]{:S(2)}, u32[]{:S(2)}) %collective-permute-start.11) | collective-permute-done | bytes 655392 | tf_op jit(solution)/shard_map/ppermute | solution.py:453
  182.5 3.4 %collective-permute-done.12 = bf16[64,5120]{1,0:T(8,128)(2,1)} collective-permute-done((bf16[64,5120]{1,0:T(8,128)(2,1)}, bf16[64,5120]{1,0:T(8,128)(2,1)}, u32[]{:S(2)}, u32[]{:S(2)}) %collective-permute-start.12) | collective-permute-done | bytes 655392 | tf_op jit(solution)/shard_map/ppermute | solution.py:453
  185.9 1.7 convert_add_fusion.1
  187.6 3.0 %collective-permute-start.14 = (bf16[32,5120]{1,0:T(8,128)(2,1)S(1)}, bf16[32,5120]{1,0:T(8,128)(2,1)S(1)}, u32[]{:S(2)}, u32[]{:S(2)}) collective-permute-start(bf16[32,5120]{1,0:T(8,128)(2,1)S(1)} %slice.32), channel_id=1, source_target_pairs={{0,16},{16,0},{32,48},{48,32},{64,80},{80,64},{96,112},{112,96},{1... | collective-permute-start | bytes 983048 | tf_op jit(solution)/shard_map/ppermute | solution.py:457
  191.1 1.2 collective-permute-start.18
  192.3 2.9 collective-permute-start.17
  195.2 2.4 collective-permute-start.16
  197.7 3.6 %collective-permute-done.18.b2 = bf16[32,5120]{1,0:T(8,128)(2,1)S(1)} collective-permute-done((bf16[32,5120]{1,0:T(8,128)(2,1)S(1)}, bf16[32,5120]{1,0:T(8,128)(2,1)S(1)}, u32[]{:S(2)}, u32[]{:S(2)}) %collective-permute-start.18) | collective-permute-done | bytes 327712 | tf_op jit(solution)/shard_map/ppermute | solution.py:453
  201.3 3.4 %collective-permute-done.17.b3 = bf16[32,5120]{1,0:T(8,128)(2,1)S(1)} collective-permute-done((bf16[32,5120]{1,0:T(8,128)(2,1)S(1)}, bf16[32,5120]{1,0:T(8,128)(2,1)S(1)}, u32[]{:S(2)}, u32[]{:S(2)}) %collective-permute-start.17) | collective-permute-done | bytes 327712 | tf_op jit(solution)/shard_map/ppermute | solution.py:453
  205.1 17.1 %all_to_all.26 = bf16[16,8,2560]{2,1,0:T(8,128)(2,1)S(1)} all-to-all(bf16[16,8,2560]{2,1,0:T(8,128)(2,1)S(1)} %bitcast.25), channel_id=1, replica_groups=mesh['ctx'=8,'exp'=16] {'exp'}, dimensions={0} | all-to-all | bytes 1310720 | tf_op jit(solution)/shard_map/all_to_all | solution.py:489
  222.2 3.5 %finish.1 = (bf16[128,5120]{1,0:T(8,128)(2,1)}, bf16[8,128,640]{2,1,0:T(8,128)(2,1)}) custom-call(bf16[128,5120]{1,0:T(8,128)(2,1)S(1)} %bitcast.20, bf16[128,5120]{1,0:T(8,128)(2,1)S(1)} %bitcast.22, f32[1,5120]{1,0:T(1,128)S(1)} %bitcast.28, bf16[256,128]{1,0:T(8,128)(2,1)S(1)} %get-tuple-element.27.picks, bf16[128,2560]{1,0:T(8,128)(2,1)S(1)} %bitcast.24), custom_call_target="tpu_custom_call" | custom-call | tf_op jit(solution)/shard_map/finish/pallas_call | solution.py:252
  225.7 5.7 %all-to-all-start.3 = ((bf16[8,128,640]{2,1,0:T(8,128)(2,1)}), bf16[8,128,640]{2,1,0:T(8,128)(2,1)S(1)}, u32[]{:S(2)}, u32[]{:S(2)}) async-start(bf16[8,128,640]{2,1,0:T(8,128)(2,1)} %get-tuple-element.46), calls=%async_computation.3 | async-start | bytes 2621440 | tf_op jit(solution)/shard_map/all_to_all | solution.py:493
  231.4 14.6 %probs.1 = (bf16[5,4,1024,256]{3,2,1,0:T(8,128)(2,1)}, f32[5,128,1024]{2,1,0:T(8,128)}, bf16[5,1024,128]{2,1,0:T(8,128)(2,1)}, bf16[2,1024,128]{2,1,0:T(8,128)(2,1)}) custom-call(s32[16]{0:T(128)} %order.3, bf16[1024,896]{1,0:T(8,128)(2,1)} %bitcast.30), custom_call_target="tpu_custom_call" | custom-call | flops 1342177280 | bytes 14680064 | tf_op jit(solution)/shard_map/probs/pallas_call | solution.py:312
  246.0 5.5 %all-to-all-done.3 = bf16[8,128,640]{2,1,0:T(8,128)(2,1)S(1)} async-done(((bf16[8,128,640]{2,1,0:T(8,128)(2,1)}), bf16[8,128,640]{2,1,0:T(8,128)(2,1)S(1)}, u32[]{:S(2)}, u32[]{:S(2)}) %all-to-all-start.3) | async-done | bytes 1310752 | tf_op jit(solution)/shard_map/all_to_all | solution.py:493
  251.5 1.1 copy-done.16
  252.5 13.5 %attend.1 = bf16[1024,896]{1,0:T(8,128)(2,1)} custom-call(s32[16]{0:T(128)} %order.3, bf16[5,4,1024,256]{3,2,1,0:T(8,128)(2,1)} %get-tuple-element.42.probs, f32[5,128,1024]{2,1,0:T(8,128)} %get-tuple-element.43.attended, bf16[5,1024,128]{2,1,0:T(8,128)(2,1)} %get-tuple-element.44.q, bf16[2,1024,128]{2,1,0:T(8,128)(2,1)} %get-tuple-element.45.kv, ...), custom_call_target="tpu_custom_call" | custom-call | flops 5368709120 | bytes 16777216 | tf_op jit(solution)/shard_map/attend/pallas_call | solution.py:387
  266.0 28.5 %all_to_all.27.block = bf16[8,128,896]{2,1,0:T(8,128)(2,1)S(1)} all-to-all(bf16[8,128,896]{2,1,0:T(8,128)(2,1)} %bitcast.31), channel_id=1, replica_groups=mesh['ctx'=8,'exp'=16] {'ctx'}, dimensions={0} | all-to-all | bytes 3670016 | tf_op jit(solution)/shard_map/all_to_all | solution.py:493
  294.5 2.9 place.1
  (58 shorter events, 4.6 us)
Async XLA Ops:
  2.2 1.3 copy-start
  3.5 1.3 copy-start.2
  4.8 0.7 copy-start.5
  31.9 23.2 %copy-start.4 = (bf16[64,5120]{1,0:T(8,128)(2,1)}, bf16[64,5120]{1,0:T(8,128)(2,1)S(1)}, u32[]{:S(2)}) copy-start(bf16[64,5120]{1,0:T(8,128)(2,1)S(1)} %get-tuple-element.30.refs_0_.refs_1_) | copy-start | bytes 1966084
  31.9 19.6 %collective-permute-start.6 = (bf16[64,5120]{1,0:T(8,128)(2,1)S(1)}, bf16[64,5120]{1,0:T(8,128)(2,1)S(1)}, u32[]{:S(2)}, u32[]{:S(2)}) collective-permute-start(bf16[64,5120]{1,0:T(8,128)(2,1)S(1)} %get-tuple-element.30.refs_0_.refs_1_), channel_id=1, source_target_pairs={{0,64},{16,80},{32,96},{48,112},{64,0},{80,16},{96,32},{112,48},{1... | collective-permute-start | bytes 1966088 | tf_op jit(solution)/shard_map/ppermute | solution.py:453
  35.9 19.2 %collective-permute-start = (bf16[64,5120]{1,0:T(8,128)(2,1)S(1)}, bf16[64,5120]{1,0:T(8,128)(2,1)S(1)}, u32[]{:S(2)}, u32[]{:S(2)}) collective-permute-start(bf16[64,5120]{1,0:T(8,128)(2,1)S(1)} %get-tuple-element.29), channel_id=1, source_target_pairs={{0,16},{16,0},{32,48},{48,32},{64,80},{80,64},{96,112},{112,96},{1... | collective-permute-start | bytes 1966088 | tf_op jit(solution)/shard_map/ppermute | solution.py:457
  38.6 28.0 %collective-permute-start.4 = (bf16[64,5120]{1,0:T(8,128)(2,1)S(1)}, bf16[64,5120]{1,0:T(8,128)(2,1)S(1)}, u32[]{:S(2)}, u32[]{:S(2)}) collective-permute-start(bf16[64,5120]{1,0:T(8,128)(2,1)S(1)} %get-tuple-element.30.refs_0_.refs_1_), channel_id=1, source_target_pairs={{0,96},{16,112},{32,0},{48,16},{64,32},{80,48},{96,64},{112,80},{1... | collective-permute-start | bytes 1966088 | tf_op jit(solution)/shard_map/ppermute | solution.py:453
  39.3 29.9 %collective-permute-start.2 = (bf16[64,5120]{1,0:T(8,128)(2,1)S(1)}, bf16[64,5120]{1,0:T(8,128)(2,1)S(1)}, u32[]{:S(2)}, u32[]{:S(2)}) collective-permute-start(bf16[64,5120]{1,0:T(8,128)(2,1)S(1)} %get-tuple-element.30.refs_0_.refs_1_), channel_id=1, source_target_pairs={{0,32},{16,48},{32,64},{48,80},{64,96},{80,112},{96,0},{112,16},{1... | collective-permute-start | bytes 1966088 | tf_op jit(solution)/shard_map/ppermute | solution.py:453
  40.6 28.6 %collective-permute-start.1 = (bf16[64,5120]{1,0:T(8,128)(2,1)S(1)}, bf16[64,5120]{1,0:T(8,128)(2,1)S(1)}, u32[]{:S(2)}, u32[]{:S(2)}) collective-permute-start(bf16[64,5120]{1,0:T(8,128)(2,1)S(1)} %get-tuple-element.30.refs_0_.refs_1_), channel_id=1, source_target_pairs={{0,16},{16,0},{32,48},{48,32},{64,80},{80,64},{96,112},{112,96},{1... | collective-permute-start | bytes 1966088 | tf_op jit(solution)/shard_map/ppermute | solution.py:457
  51.5 3.6 %copy-start.10 = (bf16[64,5120]{1,0:T(8,128)(2,1)}, bf16[64,5120]{1,0:T(8,128)(2,1)S(1)}, u32[]{:S(2)}) copy-start(bf16[64,5120]{1,0:T(8,128)(2,1)S(1)} %collective-permute-done.6.refs_6_.refs_7_) | copy-start | bytes 1966084
  51.5 31.6 %collective-permute-start.7 = (bf16[64,5120]{1,0:T(8,128)(2,1)S(1)}, bf16[64,5120]{1,0:T(8,128)(2,1)S(1)}, u32[]{:S(2)}, u32[]{:S(2)}) collective-permute-start(bf16[64,5120]{1,0:T(8,128)(2,1)S(1)} %collective-permute-done.6.refs_6_.refs_7_), channel_id=1, source_target_pairs={{0,16},{16,0},{32,48},{48,32},{64,80},{80,64},{96,112},{112,96},{1... | collective-permute-start | bytes 1966088 | tf_op jit(solution)/shard_map/ppermute | solution.py:457
  55.1 33.7 %copy-start.7 = (bf16[128,5120]{1,0:T(8,128)(2,1)}, bf16[128,5120]{1,0:T(8,128)(2,1)S(1)}, u32[]{:S(2)}) copy-start(bf16[128,5120]{1,0:T(8,128)(2,1)S(1)} %constant_dynamic-update-slice_fusion.refs_0_) | copy-start | bytes 3932164
  55.1 78.8 %collective-permute-start.10 = (bf16[128,5120]{1,0:T(8,128)(2,1)S(1)}, bf16[128,5120]{1,0:T(8,128)(2,1)}, u32[]{:S(2)}, u32[]{:S(2)}) collective-permute-start(bf16[128,5120]{1,0:T(8,128)(2,1)S(1)} %constant_dynamic-update-slice_fusion.refs_0_), channel_id=1, source_target_pairs={{0,64},{16,80},{32,96},{48,112},{64,0},{80,16},{96,32},{112,48},{1... | collective-permute-start | bytes 3932168 | tf_op jit(solution)/shard_map/ppermute | solution.py:453
  66.6 22.2 %copy-start.11 = (bf16[64,5120]{1,0:T(8,128)(2,1)}, bf16[64,5120]{1,0:T(8,128)(2,1)S(1)}, u32[]{:S(2)}) copy-start(bf16[64,5120]{1,0:T(8,128)(2,1)S(1)} %collective-permute-done.4.refs_4_.refs_5_) | copy-start | bytes 1966084
  66.6 67.3 %collective-permute-start.9 = (bf16[128,5120]{1,0:T(8,128)(2,1)S(1)}, bf16[128,5120]{1,0:T(8,128)(2,1)}, u32[]{:S(2)}, u32[]{:S(2)}) collective-permute-start(bf16[128,5120]{1,0:T(8,128)(2,1)S(1)} %constant_dynamic-update-slice_fusion.refs_0_), channel_id=1, source_target_pairs={{0,96},{16,112},{32,0},{48,16},{64,32},{80,48},{96,64},{112,80},{1... | collective-permute-start | bytes 3932168 | tf_op jit(solution)/shard_map/ppermute | solution.py:453
  69.2 19.6 %copy-start.12 = (bf16[64,5120]{1,0:T(8,128)(2,1)}, bf16[64,5120]{1,0:T(8,128)(2,1)S(1)}, u32[]{:S(2)}) copy-start(bf16[64,5120]{1,0:T(8,128)(2,1)S(1)} %collective-permute-done.2.refs_2_.refs_3_) | copy-start | bytes 1966084
  69.2 64.7 %collective-permute-start.8 = (bf16[128,5120]{1,0:T(8,128)(2,1)S(1)}, bf16[128,5120]{1,0:T(8,128)(2,1)}, u32[]{:S(2)}, u32[]{:S(2)}) collective-permute-start(bf16[128,5120]{1,0:T(8,128)(2,1)S(1)} %constant_dynamic-update-slice_fusion.refs_0_), channel_id=1, source_target_pairs={{0,32},{16,48},{32,64},{48,80},{64,96},{80,112},{96,0},{112,16},{1... | collective-permute-start | bytes 3932168 | tf_op jit(solution)/shard_map/ppermute | solution.py:453
  69.2 13.9 %copy-start.13 = (bf16[64,5120]{1,0:T(8,128)(2,1)}, bf16[64,5120]{1,0:T(8,128)(2,1)S(1)}, u32[]{:S(2)}) copy-start(bf16[64,5120]{1,0:T(8,128)(2,1)S(1)} %collective-permute-done.1.refs_1_.refs_2_) | copy-start | bytes 1966084
  69.2 28.0 %collective-permute-start.5 = (bf16[64,5120]{1,0:T(8,128)(2,1)S(1)}, bf16[64,5120]{1,0:T(8,128)(2,1)}, u32[]{:S(2)}, u32[]{:S(2)}) collective-permute-start(bf16[64,5120]{1,0:T(8,128)(2,1)S(1)} %collective-permute-done.4.refs_4_.refs_5_), channel_id=1, source_target_pairs={{0,16},{16,0},{32,48},{48,32},{64,80},{80,64},{96,112},{112,96},{1... | collective-permute-start | bytes 1966088 | tf_op jit(solution)/shard_map/ppermute | solution.py:457
  83.1 2.7 copy-start.14
  83.1 26.3 %collective-permute-start.3 = (bf16[64,5120]{1,0:T(8,128)(2,1)S(1)}, bf16[64,5120]{1,0:T(8,128)(2,1)S(1)}, u32[]{:S(2)}, u32[]{:S(2)}) collective-permute-start(bf16[64,5120]{1,0:T(8,128)(2,1)S(1)} %collective-permute-done.2.refs_2_.refs_3_), channel_id=1, source_target_pairs={{0,16},{16,0},{32,48},{48,32},{64,80},{80,64},{96,112},{112,96},{1... | collective-permute-start | bytes 1966088 | tf_op jit(solution)/shard_map/ppermute | solution.py:457
  109.4 0.8 copy-start.15
  110.3 48.2 %all-to-all-start.1 = ((bf16[8,128,896]{2,1,0:T(8,128)(2,1)}), bf16[8,128,896]{2,1,0:T(8,128)(2,1)S(1)}, u32[]{:S(2)}, u32[]{:S(2)}) async-start(bf16[8,128,896]{2,1,0:T(8,128)(2,1)} %hold.4), calls=%async_computation.1 | async-start | bytes 3670016 | tf_op jit(solution)/shard_map/all_to_all | solution.py:493
  152.9 29.6 %collective-permute-start.11 = (bf16[64,5120]{1,0:T(8,128)(2,1)}, bf16[64,5120]{1,0:T(8,128)(2,1)S(1)}, u32[]{:S(2)}, u32[]{:S(2)}) collective-permute-start(bf16[64,5120]{1,0:T(8,128)(2,1)} %get-tuple-element.37), channel_id=1, source_target_pairs={{0,96},{16,112},{32,0},{48,16},{64,32},{80,48},{96,64},{112,80},{1... | collective-permute-start | bytes 1966088 | tf_op jit(solution)/shard_map/ppermute | solution.py:453
  156.1 29.8 %collective-permute-start.12 = (bf16[64,5120]{1,0:T(8,128)(2,1)}, bf16[64,5120]{1,0:T(8,128)(2,1)}, u32[]{:S(2)}, u32[]{:S(2)}) collective-permute-start(bf16[64,5120]{1,0:T(8,128)(2,1)} %get-tuple-element.38), channel_id=1, source_target_pairs={{0,32},{16,48},{32,64},{48,80},{64,96},{80,112},{96,0},{112,16},{1... | collective-permute-start | bytes 1966088 | tf_op jit(solution)/shard_map/ppermute | solution.py:453
  156.1 29.8 %collective-permute-start.13 = (bf16[64,5120]{1,0:T(8,128)(2,1)}, bf16[64,5120]{1,0:T(8,128)(2,1)}, u32[]{:S(2)}, u32[]{:S(2)}) collective-permute-start(bf16[64,5120]{1,0:T(8,128)(2,1)} %get-tuple-element.39), channel_id=1, source_target_pairs={{0,64},{16,80},{32,96},{48,112},{64,0},{80,16},{96,32},{112,48},{1... | collective-permute-start | bytes 1966088 | tf_op jit(solution)/shard_map/ppermute | solution.py:453
  158.5 1.2 copy-start.8
  159.8 26.1 %copy-start.17 = (bf16[64,5120]{1,0:T(8,128)(2,1)S(1)}, bf16[64,5120]{1,0:T(8,128)(2,1)}, u32[]{:S(2)}) copy-start(bf16[64,5120]{1,0:T(8,128)(2,1)} %get-tuple-element.36) | copy-start | bytes 1966084
  159.8 30.9 %collective-permute-start.15 = (bf16[128,5120]{1,0:T(8,128)(2,1)}, bf16[128,5120]{1,0:T(8,128)(2,1)S(1)}, u32[]{:S(2)}, u32[]{:S(2)}) collective-permute-start(bf16[128,5120]{1,0:T(8,128)(2,1)} %hold.5), channel_id=1, source_target_pairs={{0,16},{16,0},{32,48},{48,32},{64,80},{80,64},{96,112},{112,96},{1... | collective-permute-start | bytes 3932168 | tf_op jit(solution)/shard_map/ppermute | solution.py:457
  185.9 4.8 %copy-start.9 = (bf16[128,5120]{1,0:T(8,128)(2,1)S(1)}, bf16[128,5120]{1,0:T(8,128)(2,1)}, u32[]{:S(2)}) copy-start(bf16[128,5120]{1,0:T(8,128)(2,1)} %get-tuple-element.33.refs_1_) | copy-start | bytes 3932164
  187.6 10.0 %collective-permute-start.14 = (bf16[32,5120]{1,0:T(8,128)(2,1)S(1)}, bf16[32,5120]{1,0:T(8,128)(2,1)S(1)}, u32[]{:S(2)}, u32[]{:S(2)}) collective-permute-start(bf16[32,5120]{1,0:T(8,128)(2,1)S(1)} %slice.32), channel_id=1, source_target_pairs={{0,16},{16,0},{32,48},{48,32},{64,80},{80,64},{96,112},{112,96},{1... | collective-permute-start | bytes 983048 | tf_op jit(solution)/shard_map/ppermute | solution.py:457
  191.1 10.1 %collective-permute-start.18 = (bf16[32,5120]{1,0:T(8,128)(2,1)S(1)}, bf16[32,5120]{1,0:T(8,128)(2,1)S(1)}, u32[]{:S(2)}, u32[]{:S(2)}) collective-permute-start(bf16[32,5120]{1,0:T(8,128)(2,1)S(1)} %get-tuple-element.52), channel_id=1, source_target_pairs={{0,64},{16,80},{32,96},{48,112},{64,0},{80,16},{96,32},{112,48},{1... | collective-permute-start | bytes 983048 | tf_op jit(solution)/shard_map/ppermute | solution.py:453
  192.3 12.4 %collective-permute-start.17 = (bf16[32,5120]{1,0:T(8,128)(2,1)S(1)}, bf16[32,5120]{1,0:T(8,128)(2,1)S(1)}, u32[]{:S(2)}, u32[]{:S(2)}) collective-permute-start(bf16[32,5120]{1,0:T(8,128)(2,1)S(1)} %get-tuple-element.53), channel_id=1, source_target_pairs={{0,32},{16,48},{32,64},{48,80},{64,96},{80,112},{96,0},{112,16},{1... | collective-permute-start | bytes 983048 | tf_op jit(solution)/shard_map/ppermute | solution.py:453
  195.2 9.5 %collective-permute-start.16 = (bf16[32,5120]{1,0:T(8,128)(2,1)S(1)}, bf16[32,5120]{1,0:T(8,128)(2,1)S(1)}, u32[]{:S(2)}, u32[]{:S(2)}) collective-permute-start(bf16[32,5120]{1,0:T(8,128)(2,1)S(1)} %get-tuple-element.54), channel_id=1, source_target_pairs={{0,96},{16,112},{32,0},{48,16},{64,32},{80,48},{96,64},{112,80},{1... | collective-permute-start | bytes 983048 | tf_op jit(solution)/shard_map/ppermute | solution.py:453
  204.7 17.5 %copy-start.3 = (bf16[1,128,5120]{2,1,0:T(8,128)(2,1)S(1)}, bf16[1,128,5120]{2,1,0:T(8,128)(2,1)}, u32[]{:S(2)}) copy-start(bf16[1,128,5120]{2,1,0:T(8,128)(2,1)} %param.16) | copy-start | bytes 3932164
  204.7 17.5 %copy-start.6 = (f32[5120]{0:T(1024)S(1)}, f32[5120]{0:T(1024)}, u32[]{:S(2)}) copy-start(f32[5120]{0:T(1024)} %param.20) | copy-start | bytes 61444
  205.1 17.1 %copy-start.1 = (bf16[1,128,5120]{2,1,0:T(8,128)(2,1)S(1)}, bf16[1,128,5120]{2,1,0:T(8,128)(2,1)}, u32[]{:S(2)}) copy-start(bf16[1,128,5120]{2,1,0:T(8,128)(2,1)} %param.15) | copy-start | bytes 3932164
  225.7 25.8 %all-to-all-start.3 = ((bf16[8,128,640]{2,1,0:T(8,128)(2,1)}), bf16[8,128,640]{2,1,0:T(8,128)(2,1)S(1)}, u32[]{:S(2)}, u32[]{:S(2)}) async-start(bf16[8,128,640]{2,1,0:T(8,128)(2,1)} %get-tuple-element.46), calls=%async_computation.3 | async-start | bytes 2621440 | tf_op jit(solution)/shard_map/all_to_all | solution.py:493
  251.5 1.1 copy-start.16

commit v4 on v3

--- a/solution.py
+++ b/solution.py
@@ -28,8 +28,8 @@
 HALF = D // 2
 ROWS = 256
 FIRST = 64
-KB = 1024
-TB = 1024
+KB = 1280
+TB = 2560
 SHIFTS = (1, 3, 2)
 FACTOR = DH ** (-0.5)
 

time: 298 us -> 294 us (0.987)
  Pallas kernels: 77.6 us -> 73.8 us
  transfers between devices with their start and end apart: 21 -> 21, of which waited for: 11 -> 11; matrix products, arithmetic and copies ran while one was open for 1% -> 1% of each run, Pallas kernels for 19% -> 18%
where the time goes in v4:
time: 294 us
  waiting for transfers between devices  87 us (30%)
  Pallas kernels  73.8 us (25%)
  blocking collectives  70.1 us (24%)
  starting transfers between devices  51.4 us (17%)
  local copies, waits for them, and re-layouts  8.34 us (3%)
    ppermute x12, waiting for transfers between devices, along_z(): return lax.ppermute(x, 'ctx', pairs)  49.1 us
    all_to_all x2, blocking collectives, swap_exp(): return lax.all_to_all(x, 'exp', split_axis=0, concat_axis=0, tiled=True)  41.6 us
    ppermute x7, waiting for transfers between devices, across_x(): return lax.ppermute(x, 'ctx', [(c, c ^ 1) for c in range(8)])  32.5 us
    all_to_all x1, blocking collectives, swap_ctx(): return lax.all_to_all(x, 'ctx', split_axis=0, concat_axis=0, tiled=True)  28.5 us
    ppermute x12, starting transfers between devices, along_z(): return lax.ppermute(x, 'ctx', pairs)  23.3 us
    pallas_call x2, Pallas kernels, project(): pl.pallas_call(functools.partial(project_kernel, len(pieces)), grid=(D //...  20.6 us
    ppermute x7, starting transfers between devices, across_x(): return lax.ppermute(x, 'ctx', [(c, c ^ 1) for c in range(8)])  17.8 us
    pallas_call x1, Pallas kernels, make_probs(): pl.pallas_call(probs_kernel, grid_spec=pltpu.PrefetchScalarGridSpec(num_s...  14.6 us
  transfers between devices with their start and end apart: 21, of which 11 were waited for; matrix products, arithmetic and copies ran while one was open for 1% of the time, Pallas kernels for 18%

profile of v4, /device:TPU:0, one launch (start us, length us, event | category | flops | bytes accessed | tf_op | source)
XLA Modules:
  0.0 293.6 jit_solution(11823533528013914109)
XLA Ops:
  0.6 0.8 copy.19.weight
  2.2 1.3 copy-done
  3.5 1.3 copy-done.2
  5.5 1.2 dispatch.1
  6.7 24.7 %all_to_all.25 = bf16[16,8,5120]{2,1,0:T(8,128)(2,1)S(1)} all-to-all(bf16[16,8,5120]{2,1,0:T(8,128)(2,1)S(1)} %bitcast.26), channel_id=1, replica_groups=mesh['ctx'=8,'exp'=16] {'exp'}, dimensions={0} | all-to-all | bytes 2621440 | tf_op jit(solution)/shard_map/all_to_all | solution.py:489
  31.9 4.0 %collective-permute-start.6 = (bf16[64,5120]{1,0:T(8,128)(2,1)S(1)}, bf16[64,5120]{1,0:T(8,128)(2,1)S(1)}, u32[]{:S(2)}, u32[]{:S(2)}) collective-permute-start(bf16[64,5120]{1,0:T(8,128)(2,1)S(1)} %get-tuple-element.30.refs_0_.refs_1_), channel_id=1, source_target_pairs={{0,64},{16,80},{32,96},{48,112},{64,0},{80,16},{96,32},{112,48},{1... | collective-permute-start | bytes 1966088 | tf_op jit(solution)/shard_map/ppermute | solution.py:453
  35.9 2.7 collective-permute-start
  39.3 1.3 collective-permute-start.2
  40.6 0.8 collective-permute-start.1
  41.4 10.1 %collective-permute-done.6.refs_6_.refs_7_ = bf16[64,5120]{1,0:T(8,128)(2,1)S(1)} collective-permute-done((bf16[64,5120]{1,0:T(8,128)(2,1)S(1)}, bf16[64,5120]{1,0:T(8,128)(2,1)S(1)}, u32[]{:S(2)}, u32[]{:S(2)}) %collective-permute-start.6) | collective-permute-done | bytes 655392 | tf_op jit(solution)/shard_map/ppermute | solution.py:453
  51.5 2.7 collective-permute-start.7
  55.1 2.9 collective-permute-start.10
  58.0 8.6 %collective-permute-done.4.refs_4_.refs_5_ = bf16[64,5120]{1,0:T(8,128)(2,1)S(1)} collective-permute-done((bf16[64,5120]{1,0:T(8,128)(2,1)S(1)}, bf16[64,5120]{1,0:T(8,128)(2,1)S(1)}, u32[]{:S(2)}, u32[]{:S(2)}) %collective-permute-start.4) | collective-permute-done | bytes 655392 | tf_op jit(solution)/shard_map/ppermute | solution.py:453
  66.6 2.6 collective-permute-start.9
  69.2 2.8 collective-permute-start.5
  72.0 11.1 %collective-permute-done.7.refs_7_.refs_8_ = bf16[64,5120]{1,0:T(8,128)(2,1)S(1)} collective-permute-done((bf16[64,5120]{1,0:T(8,128)(2,1)S(1)}, bf16[64,5120]{1,0:T(8,128)(2,1)S(1)}, u32[]{:S(2)}, u32[]{:S(2)}) %collective-permute-start.7) | collective-permute-done | bytes 655392 | tf_op jit(solution)/shard_map/ppermute | solution.py:457
  83.1 2.7 collective-permute-start.3
  85.9 2.9 cut_heads.1.refs_0_
  88.8 8.5 %collective-permute-done.5.refs_5_.refs_6_ = bf16[64,5120]{1,0:T(8,128)(2,1)} collective-permute-done((bf16[64,5120]{1,0:T(8,128)(2,1)S(1)}, bf16[64,5120]{1,0:T(8,128)(2,1)}, u32[]{:S(2)}, u32[]{:S(2)}) %collective-permute-start.5) | collective-permute-done | bytes 655392 | tf_op jit(solution)/shard_map/ppermute | solution.py:457
  97.3 12.2 %collective-permute-done.3.refs_3_.refs_4_ = bf16[64,5120]{1,0:T(8,128)(2,1)S(1)} collective-permute-done((bf16[64,5120]{1,0:T(8,128)(2,1)S(1)}, bf16[64,5120]{1,0:T(8,128)(2,1)S(1)}, u32[]{:S(2)}, u32[]{:S(2)}) %collective-permute-start.3) | collective-permute-done | bytes 655392 | tf_op jit(solution)/shard_map/ppermute | solution.py:457
  109.4 0.8 copy-done.15
  110.3 4.4 %all-to-all-start.1 = ((bf16[8,128,896]{2,1,0:T(8,128)(2,1)}), bf16[8,128,896]{2,1,0:T(8,128)(2,1)S(1)}, u32[]{:S(2)}, u32[]{:S(2)}) async-start(bf16[8,128,896]{2,1,0:T(8,128)(2,1)} %hold.4), calls=%async_computation.1 | async-start | bytes 3670016 | tf_op jit(solution)/shard_map/all_to_all | solution.py:493
  114.7 10.4 %project.2 = (bf16[256,512]{1,0:T(8,128)(2,1)}, bf16[256,512]{1,0:T(8,128)(2,1)}) custom-call(bf16[64,5120]{1,0:T(8,128)(2,1)} %copy-done.4, bf16[64,5120]{1,0:T(8,128)(2,1)} %copy-done.13, bf16[64,5120]{1,0:T(8,128)(2,1)} %copy-done.12, bf16[64,5120]{1,0:T(8,128)(2,1)} %copy-done.15, bf16[64,5120]{1,0:T(8,128)(2,1)} %copy-done.11, ...), custom_call_target="tpu_custom_call" | custom-call | flops 4026531840 | bytes 29360128 | tf_op jit(solution)/shard_map/project/pallas_call | solution.py:160
  125.1 6.9 %terms.2 = (bf16[128,5120]{1,0:T(8,128)(2,1)}, bf16[128,5120]{1,0:T(8,128)(2,1)}) custom-call(bf16[256,512]{1,0:T(8,128)(2,1)} %get-tuple-element.31.grad_gate, bf16[256,512]{1,0:T(8,128)(2,1)} %get-tuple-element.32.grad_up, bf16[1,5120,512]{2,1,0:T(8,128)(2,1)} %w_gate.3, bf16[1,5120,512]{2,1,0:T(8,128)(2,1)} %w_in.3), custom_call_target="tpu_custom_call" | custom-call | flops 2684354560 | bytes 14680064 | tf_op jit(solution)/shard_map/terms/pallas_call | solution.py:192
  132.0 10.3 %project.3 = (bf16[256,512]{1,0:T(8,128)(2,1)}, bf16[256,512]{1,0:T(8,128)(2,1)}) custom-call(bf16[128,5120]{1,0:T(8,128)(2,1)} %hold.3.refs_0_, bf16[128,5120]{1,0:T(8,128)(2,1)} %collective-permute-done.8.refs_1_, bf16[128,5120]{1,0:T(8,128)(2,1)} %collective-permute-done.9.refs_2_, bf16[128,5120]{1,0:T(8,128)(2,1)} %collective-permute-done.10.refs_3_, ...), custom_call_target="tpu_custom_call" | custom-call | flops 4026531840 | bytes 29360128 | tf_op jit(solution)/shard_map/project/pallas_call | solution.py:160
  142.3 6.8 %terms.3 = (bf16[64,5120]{1,0:T(8,128)(2,1)}, bf16[64,5120]{1,0:T(8,128)(2,1)}, bf16[64,5120]{1,0:T(8,128)(2,1)}, bf16[64,5120]{1,0:T(8,128)(2,1)}) custom-call(bf16[256,512]{1,0:T(8,128)(2,1)} %get-tuple-element.34.grad_gate, bf16[256,512]{1,0:T(8,128)(2,1)} %get-tuple-element.35.grad_up, bf16[1,5120,512]{2,1,0:T(8,128)(2,1)} %w_gate.3, ...), custom_call_target="tpu_custom_call" | custom-call | flops 2684354560 | bytes 14680064 | tf_op jit(solution)/shard_map/terms/pallas_call | solution.py:192
  149.1 3.2 %collective-permute-start.11 = (bf16[64,5120]{1,0:T(8,128)(2,1)}, bf16[64,5120]{1,0:T(8,128)(2,1)S(1)}, u32[]{:S(2)}, u32[]{:S(2)}) collective-permute-start(bf16[64,5120]{1,0:T(8,128)(2,1)} %get-tuple-element.37), channel_id=1, source_target_pairs={{0,96},{16,112},{32,0},{48,16},{64,32},{80,48},{96,64},{112,80},{1... | collective-permute-start | bytes 1966088 | tf_op jit(solution)/shard_map/ppermute | solution.py:453
  152.3 2.3 collective-permute-start.13
  154.7 1.2 copy-done.8
  155.9 3.0 %collective-permute-start.15 = (bf16[128,5120]{1,0:T(8,128)(2,1)}, bf16[128,5120]{1,0:T(8,128)(2,1)S(1)}, u32[]{:S(2)}, u32[]{:S(2)}) collective-permute-start(bf16[128,5120]{1,0:T(8,128)(2,1)} %hold.5), channel_id=1, source_target_pairs={{0,16},{16,0},{32,48},{48,32},{64,80},{80,64},{96,112},{112,96},{1... | collective-permute-start | bytes 3932168 | tf_op jit(solution)/shard_map/ppermute | solution.py:457
  158.9 19.8 %collective-permute-done.11 = bf16[64,5120]{1,0:T(8,128)(2,1)S(1)} collective-permute-done((bf16[64,5120]{1,0:T(8,128)(2,1)}, bf16[64,5120]{1,0:T(8,128)(2,1)S(1)}, u32[]{:S(2)}, u32[]{:S(2)}) %collective-permute-start.11) | collective-permute-done | bytes 655392 | tf_op jit(solution)/shard_map/ppermute | solution.py:453
  178.6 3.4 %collective-permute-done.12 = bf16[64,5120]{1,0:T(8,128)(2,1)} collective-permute-done((bf16[64,5120]{1,0:T(8,128)(2,1)}, bf16[64,5120]{1,0:T(8,128)(2,1)}, u32[]{:S(2)}, u32[]{:S(2)}) %collective-permute-start.12) | collective-permute-done | bytes 655392 | tf_op jit(solution)/shard_map/ppermute | solution.py:453
  182.0 1.7 convert_add_fusion.1
  183.8 3.0 %collective-permute-start.14 = (bf16[32,5120]{1,0:T(8,128)(2,1)S(1)}, bf16[32,5120]{1,0:T(8,128)(2,1)S(1)}, u32[]{:S(2)}, u32[]{:S(2)}) collective-permute-start(bf16[32,5120]{1,0:T(8,128)(2,1)S(1)} %slice.32), channel_id=1, source_target_pairs={{0,16},{16,0},{32,48},{48,32},{64,80},{80,64},{96,112},{112,96},{1... | collective-permute-start | bytes 983048 | tf_op jit(solution)/shard_map/ppermute | solution.py:457
  187.3 1.2 collective-permute-start.18
  188.5 2.5 collective-permute-start.17
  191.0 2.6 collective-permute-start.16
  193.7 3.8 %collective-permute-done.18.b2 = bf16[32,5120]{1,0:T(8,128)(2,1)S(1)} collective-permute-done((bf16[32,5120]{1,0:T(8,128)(2,1)S(1)}, bf16[32,5120]{1,0:T(8,128)(2,1)S(1)}, u32[]{:S(2)}, u32[]{:S(2)}) %collective-permute-start.18) | collective-permute-done | bytes 327712 | tf_op jit(solution)/shard_map/ppermute | solution.py:453
  197.5 3.4 %collective-permute-done.17.b3 = bf16[32,5120]{1,0:T(8,128)(2,1)S(1)} collective-permute-done((bf16[32,5120]{1,0:T(8,128)(2,1)S(1)}, bf16[32,5120]{1,0:T(8,128)(2,1)S(1)}, u32[]{:S(2)}, u32[]{:S(2)}) %collective-permute-start.17) | collective-permute-done | bytes 327712 | tf_op jit(solution)/shard_map/ppermute | solution.py:453
  201.3 16.9 %all_to_all.26 = bf16[16,8,2560]{2,1,0:T(8,128)(2,1)S(1)} all-to-all(bf16[16,8,2560]{2,1,0:T(8,128)(2,1)S(1)} %bitcast.25), channel_id=1, replica_groups=mesh['ctx'=8,'exp'=16] {'exp'}, dimensions={0} | all-to-all | bytes 1310720 | tf_op jit(solution)/shard_map/all_to_all | solution.py:489
  218.3 3.5 %finish.1 = (bf16[128,5120]{1,0:T(8,128)(2,1)}, bf16[8,128,640]{2,1,0:T(8,128)(2,1)}) custom-call(bf16[128,5120]{1,0:T(8,128)(2,1)S(1)} %bitcast.20, bf16[128,5120]{1,0:T(8,128)(2,1)S(1)} %bitcast.22, f32[1,5120]{1,0:T(1,128)S(1)} %bitcast.28, bf16[256,128]{1,0:T(8,128)(2,1)S(1)} %get-tuple-element.27.picks, bf16[128,2560]{1,0:T(8,128)(2,1)S(1)} %bitcast.24), custom_call_target="tpu_custom_call" | custom-call | tf_op jit(solution)/shard_map/finish/pallas_call | solution.py:252
  221.8 5.8 %all-to-all-start.3 = ((bf16[8,128,640]{2,1,0:T(8,128)(2,1)}), bf16[8,128,640]{2,1,0:T(8,128)(2,1)S(1)}, u32[]{:S(2)}, u32[]{:S(2)}) async-start(bf16[8,128,640]{2,1,0:T(8,128)(2,1)} %get-tuple-element.46), calls=%async_computation.3 | async-start | bytes 2621440 | tf_op jit(solution)/shard_map/all_to_all | solution.py:493
  227.5 14.6 %probs.1 = (bf16[5,4,1024,256]{3,2,1,0:T(8,128)(2,1)}, f32[5,128,1024]{2,1,0:T(8,128)}, bf16[5,1024,128]{2,1,0:T(8,128)(2,1)}, bf16[2,1024,128]{2,1,0:T(8,128)(2,1)}) custom-call(s32[16]{0:T(128)} %order.3, bf16[1024,896]{1,0:T(8,128)(2,1)} %bitcast.30), custom_call_target="tpu_custom_call" | custom-call | flops 1342177280 | bytes 14680064 | tf_op jit(solution)/shard_map/probs/pallas_call | solution.py:312
  242.1 5.5 %all-to-all-done.3 = bf16[8,128,640]{2,1,0:T(8,128)(2,1)S(1)} async-done(((bf16[8,128,640]{2,1,0:T(8,128)(2,1)}), bf16[8,128,640]{2,1,0:T(8,128)(2,1)S(1)}, u32[]{:S(2)}, u32[]{:S(2)}) %all-to-all-start.3) | async-done | bytes 1310752 | tf_op jit(solution)/shard_map/all_to_all | solution.py:493
  247.6 1.1 copy-done.16
  248.6 13.5 %attend.1 = bf16[1024,896]{1,0:T(8,128)(2,1)} custom-call(s32[16]{0:T(128)} %order.3, bf16[5,4,1024,256]{3,2,1,0:T(8,128)(2,1)} %get-tuple-element.42.probs, f32[5,128,1024]{2,1,0:T(8,128)} %get-tuple-element.43.attended, bf16[5,1024,128]{2,1,0:T(8,128)(2,1)} %get-tuple-element.44.q, bf16[2,1024,128]{2,1,0:T(8,128)(2,1)} %get-tuple-element.45.kv, ...), custom_call_target="tpu_custom_call" | custom-call | flops 5368709120 | bytes 16777216 | tf_op jit(solution)/shard_map/attend/pallas_call | solution.py:387
  262.2 28.5 %all_to_all.27.block = bf16[8,128,896]{2,1,0:T(8,128)(2,1)S(1)} all-to-all(bf16[8,128,896]{2,1,0:T(8,128)(2,1)} %bitcast.31), channel_id=1, replica_groups=mesh['ctx'=8,'exp'=16] {'ctx'}, dimensions={0} | all-to-all | bytes 3670016 | tf_op jit(solution)/shard_map/all_to_all | solution.py:493
  290.7 2.9 place.1
  (58 shorter events, 4.6 us)
Async XLA Ops:
  2.2 1.3 copy-start
  3.5 1.3 copy-start.2
  4.8 0.7 copy-start.5
  31.9 23.2 %copy-start.4 = (bf16[64,5120]{1,0:T(8,128)(2,1)}, bf16[64,5120]{1,0:T(8,128)(2,1)S(1)}, u32[]{:S(2)}) copy-start(bf16[64,5120]{1,0:T(8,128)(2,1)S(1)} %get-tuple-element.30.refs_0_.refs_1_) | copy-start | bytes 1966084
  31.9 19.6 %collective-permute-start.6 = (bf16[64,5120]{1,0:T(8,128)(2,1)S(1)}, bf16[64,5120]{1,0:T(8,128)(2,1)S(1)}, u32[]{:S(2)}, u32[]{:S(2)}) collective-permute-start(bf16[64,5120]{1,0:T(8,128)(2,1)S(1)} %get-tuple-element.30.refs_0_.refs_1_), channel_id=1, source_target_pairs={{0,64},{16,80},{32,96},{48,112},{64,0},{80,16},{96,32},{112,48},{1... | collective-permute-start | bytes 1966088 | tf_op jit(solution)/shard_map/ppermute | solution.py:453
  35.9 19.2 %collective-permute-start = (bf16[64,5120]{1,0:T(8,128)(2,1)S(1)}, bf16[64,5120]{1,0:T(8,128)(2,1)S(1)}, u32[]{:S(2)}, u32[]{:S(2)}) collective-permute-start(bf16[64,5120]{1,0:T(8,128)(2,1)S(1)} %get-tuple-element.29), channel_id=1, source_target_pairs={{0,16},{16,0},{32,48},{48,32},{64,80},{80,64},{96,112},{112,96},{1... | collective-permute-start | bytes 1966088 | tf_op jit(solution)/shard_map/ppermute | solution.py:457
  38.6 28.0 %collective-permute-start.4 = (bf16[64,5120]{1,0:T(8,128)(2,1)S(1)}, bf16[64,5120]{1,0:T(8,128)(2,1)S(1)}, u32[]{:S(2)}, u32[]{:S(2)}) collective-permute-start(bf16[64,5120]{1,0:T(8,128)(2,1)S(1)} %get-tuple-element.30.refs_0_.refs_1_), channel_id=1, source_target_pairs={{0,96},{16,112},{32,0},{48,16},{64,32},{80,48},{96,64},{112,80},{1... | collective-permute-start | bytes 1966088 | tf_op jit(solution)/shard_map/ppermute | solution.py:453
  39.3 29.9 %collective-permute-start.2 = (bf16[64,5120]{1,0:T(8,128)(2,1)S(1)}, bf16[64,5120]{1,0:T(8,128)(2,1)S(1)}, u32[]{:S(2)}, u32[]{:S(2)}) collective-permute-start(bf16[64,5120]{1,0:T(8,128)(2,1)S(1)} %get-tuple-element.30.refs_0_.refs_1_), channel_id=1, source_target_pairs={{0,32},{16,48},{32,64},{48,80},{64,96},{80,112},{96,0},{112,16},{1... | collective-permute-start | bytes 1966088 | tf_op jit(solution)/shard_map/ppermute | solution.py:453
  40.6 28.6 %collective-permute-start.1 = (bf16[64,5120]{1,0:T(8,128)(2,1)S(1)}, bf16[64,5120]{1,0:T(8,128)(2,1)S(1)}, u32[]{:S(2)}, u32[]{:S(2)}) collective-permute-start(bf16[64,5120]{1,0:T(8,128)(2,1)S(1)} %get-tuple-element.30.refs_0_.refs_1_), channel_id=1, source_target_pairs={{0,16},{16,0},{32,48},{48,32},{64,80},{80,64},{96,112},{112,96},{1... | collective-permute-start | bytes 1966088 | tf_op jit(solution)/shard_map/ppermute | solution.py:457
  51.5 3.6 %copy-start.10 = (bf16[64,5120]{1,0:T(8,128)(2,1)}, bf16[64,5120]{1,0:T(8,128)(2,1)S(1)}, u32[]{:S(2)}) copy-start(bf16[64,5120]{1,0:T(8,128)(2,1)S(1)} %collective-permute-done.6.refs_6_.refs_7_) | copy-start | bytes 1966084
  51.5 31.6 %collective-permute-start.7 = (bf16[64,5120]{1,0:T(8,128)(2,1)S(1)}, bf16[64,5120]{1,0:T(8,128)(2,1)S(1)}, u32[]{:S(2)}, u32[]{:S(2)}) collective-permute-start(bf16[64,5120]{1,0:T(8,128)(2,1)S(1)} %collective-permute-done.6.refs_6_.refs_7_), channel_id=1, source_target_pairs={{0,16},{16,0},{32,48},{48,32},{64,80},{80,64},{96,112},{112,96},{1... | collective-permute-start | bytes 1966088 | tf_op jit(solution)/shard_map/ppermute | solution.py:457
  55.1 33.7 %copy-start.7 = (bf16[128,5120]{1,0:T(8,128)(2,1)}, bf16[128,5120]{1,0:T(8,128)(2,1)S(1)}, u32[]{:S(2)}) copy-start(bf16[128,5120]{1,0:T(8,128)(2,1)S(1)} %constant_dynamic-update-slice_fusion.refs_0_) | copy-start | bytes 3932164
  55.1 76.9 %collective-permute-start.10 = (bf16[128,5120]{1,0:T(8,128)(2,1)S(1)}, bf16[128,5120]{1,0:T(8,128)(2,1)}, u32[]{:S(2)}, u32[]{:S(2)}) collective-permute-start(bf16[128,5120]{1,0:T(8,128)(2,1)S(1)} %constant_dynamic-update-slice_fusion.refs_0_), channel_id=1, source_target_pairs={{0,64},{16,80},{32,96},{48,112},{64,0},{80,16},{96,32},{112,48},{1... | collective-permute-start | bytes 3932168 | tf_op jit(solution)/shard_map/ppermute | solution.py:453
  66.6 22.2 %copy-start.11 = (bf16[64,5120]{1,0:T(8,128)(2,1)}, bf16[64,5120]{1,0:T(8,128)(2,1)S(1)}, u32[]{:S(2)}) copy-start(bf16[64,5120]{1,0:T(8,128)(2,1)S(1)} %collective-permute-done.4.refs_4_.refs_5_) | copy-start | bytes 1966084
  66.6 65.4 %collective-permute-start.9 = (bf16[128,5120]{1,0:T(8,128)(2,1)S(1)}, bf16[128,5120]{1,0:T(8,128)(2,1)}, u32[]{:S(2)}, u32[]{:S(2)}) collective-permute-start(bf16[128,5120]{1,0:T(8,128)(2,1)S(1)} %constant_dynamic-update-slice_fusion.refs_0_), channel_id=1, source_target_pairs={{0,96},{16,112},{32,0},{48,16},{64,32},{80,48},{96,64},{112,80},{1... | collective-permute-start | bytes 3932168 | tf_op jit(solution)/shard_map/ppermute | solution.py:453
  69.2 19.6 %copy-start.12 = (bf16[64,5120]{1,0:T(8,128)(2,1)}, bf16[64,5120]{1,0:T(8,128)(2,1)S(1)}, u32[]{:S(2)}) copy-start(bf16[64,5120]{1,0:T(8,128)(2,1)S(1)} %collective-permute-done.2.refs_2_.refs_3_) | copy-start | bytes 1966084
  69.2 62.8 %collective-permute-start.8 = (bf16[128,5120]{1,0:T(8,128)(2,1)S(1)}, bf16[128,5120]{1,0:T(8,128)(2,1)}, u32[]{:S(2)}, u32[]{:S(2)}) collective-permute-start(bf16[128,5120]{1,0:T(8,128)(2,1)S(1)} %constant_dynamic-update-slice_fusion.refs_0_), channel_id=1, source_target_pairs={{0,32},{16,48},{32,64},{48,80},{64,96},{80,112},{96,0},{112,16},{1... | collective-permute-start | bytes 3932168 | tf_op jit(solution)/shard_map/ppermute | solution.py:453
  69.2 13.9 %copy-start.13 = (bf16[64,5120]{1,0:T(8,128)(2,1)}, bf16[64,5120]{1,0:T(8,128)(2,1)S(1)}, u32[]{:S(2)}) copy-start(bf16[64,5120]{1,0:T(8,128)(2,1)S(1)} %collective-permute-done.1.refs_1_.refs_2_) | copy-start | bytes 1966084
  69.2 28.0 %collective-permute-start.5 = (bf16[64,5120]{1,0:T(8,128)(2,1)S(1)}, bf16[64,5120]{1,0:T(8,128)(2,1)}, u32[]{:S(2)}, u32[]{:S(2)}) collective-permute-start(bf16[64,5120]{1,0:T(8,128)(2,1)S(1)} %collective-permute-done.4.refs_4_.refs_5_), channel_id=1, source_target_pairs={{0,16},{16,0},{32,48},{48,32},{64,80},{80,64},{96,112},{112,96},{1... | collective-permute-start | bytes 1966088 | tf_op jit(solution)/shard_map/ppermute | solution.py:457
  83.1 2.7 copy-start.14
  83.1 26.3 %collective-permute-start.3 = (bf16[64,5120]{1,0:T(8,128)(2,1)S(1)}, bf16[64,5120]{1,0:T(8,128)(2,1)S(1)}, u32[]{:S(2)}, u32[]{:S(2)}) collective-permute-start(bf16[64,5120]{1,0:T(8,128)(2,1)S(1)} %collective-permute-done.2.refs_2_.refs_3_), channel_id=1, source_target_pairs={{0,16},{16,0},{32,48},{48,32},{64,80},{80,64},{96,112},{112,96},{1... | collective-permute-start | bytes 1966088 | tf_op jit(solution)/shard_map/ppermute | solution.py:457
  109.4 0.8 copy-start.15
  110.3 44.4 %all-to-all-start.1 = ((bf16[8,128,896]{2,1,0:T(8,128)(2,1)}), bf16[8,128,896]{2,1,0:T(8,128)(2,1)S(1)}, u32[]{:S(2)}, u32[]{:S(2)}) async-start(bf16[8,128,896]{2,1,0:T(8,128)(2,1)} %hold.4), calls=%async_computation.1 | async-start | bytes 3670016 | tf_op jit(solution)/shard_map/all_to_all | solution.py:493
  149.1 29.5 %collective-permute-start.11 = (bf16[64,5120]{1,0:T(8,128)(2,1)}, bf16[64,5120]{1,0:T(8,128)(2,1)S(1)}, u32[]{:S(2)}, u32[]{:S(2)}) collective-permute-start(bf16[64,5120]{1,0:T(8,128)(2,1)} %get-tuple-element.37), channel_id=1, source_target_pairs={{0,96},{16,112},{32,0},{48,16},{64,32},{80,48},{96,64},{112,80},{1... | collective-permute-start | bytes 1966088 | tf_op jit(solution)/shard_map/ppermute | solution.py:453
  152.3 29.7 %collective-permute-start.12 = (bf16[64,5120]{1,0:T(8,128)(2,1)}, bf16[64,5120]{1,0:T(8,128)(2,1)}, u32[]{:S(2)}, u32[]{:S(2)}) collective-permute-start(bf16[64,5120]{1,0:T(8,128)(2,1)} %get-tuple-element.38), channel_id=1, source_target_pairs={{0,32},{16,48},{32,64},{48,80},{64,96},{80,112},{96,0},{112,16},{1... | collective-permute-start | bytes 1966088 | tf_op jit(solution)/shard_map/ppermute | solution.py:453
  152.3 29.7 %collective-permute-start.13 = (bf16[64,5120]{1,0:T(8,128)(2,1)}, bf16[64,5120]{1,0:T(8,128)(2,1)}, u32[]{:S(2)}, u32[]{:S(2)}) collective-permute-start(bf16[64,5120]{1,0:T(8,128)(2,1)} %get-tuple-element.39), channel_id=1, source_target_pairs={{0,64},{16,80},{32,96},{48,112},{64,0},{80,16},{96,32},{112,48},{1... | collective-permute-start | bytes 1966088 | tf_op jit(solution)/shard_map/ppermute | solution.py:453
  154.7 1.2 copy-start.8
  155.9 26.1 %copy-start.17 = (bf16[64,5120]{1,0:T(8,128)(2,1)S(1)}, bf16[64,5120]{1,0:T(8,128)(2,1)}, u32[]{:S(2)}) copy-start(bf16[64,5120]{1,0:T(8,128)(2,1)} %get-tuple-element.36) | copy-start | bytes 1966084
  155.9 30.9 %collective-permute-start.15 = (bf16[128,5120]{1,0:T(8,128)(2,1)}, bf16[128,5120]{1,0:T(8,128)(2,1)S(1)}, u32[]{:S(2)}, u32[]{:S(2)}) collective-permute-start(bf16[128,5120]{1,0:T(8,128)(2,1)} %hold.5), channel_id=1, source_target_pairs={{0,16},{16,0},{32,48},{48,32},{64,80},{80,64},{96,112},{112,96},{1... | collective-permute-start | bytes 3932168 | tf_op jit(solution)/shard_map/ppermute | solution.py:457
  182.0 4.8 %copy-start.9 = (bf16[128,5120]{1,0:T(8,128)(2,1)S(1)}, bf16[128,5120]{1,0:T(8,128)(2,1)}, u32[]{:S(2)}) copy-start(bf16[128,5120]{1,0:T(8,128)(2,1)} %get-tuple-element.33.refs_1_) | copy-start | bytes 3932164
  183.8 9.9 %collective-permute-start.14 = (bf16[32,5120]{1,0:T(8,128)(2,1)S(1)}, bf16[32,5120]{1,0:T(8,128)(2,1)S(1)}, u32[]{:S(2)}, u32[]{:S(2)}) collective-permute-start(bf16[32,5120]{1,0:T(8,128)(2,1)S(1)} %slice.32), channel_id=1, source_target_pairs={{0,16},{16,0},{32,48},{48,32},{64,80},{80,64},{96,112},{112,96},{1... | collective-permute-start | bytes 983048 | tf_op jit(solution)/shard_map/ppermute | solution.py:457
  187.3 10.3 %collective-permute-start.18 = (bf16[32,5120]{1,0:T(8,128)(2,1)S(1)}, bf16[32,5120]{1,0:T(8,128)(2,1)S(1)}, u32[]{:S(2)}, u32[]{:S(2)}) collective-permute-start(bf16[32,5120]{1,0:T(8,128)(2,1)S(1)} %get-tuple-element.52), channel_id=1, source_target_pairs={{0,64},{16,80},{32,96},{48,112},{64,0},{80,16},{96,32},{112,48},{1... | collective-permute-start | bytes 983048 | tf_op jit(solution)/shard_map/ppermute | solution.py:453
  188.5 12.4 %collective-permute-start.17 = (bf16[32,5120]{1,0:T(8,128)(2,1)S(1)}, bf16[32,5120]{1,0:T(8,128)(2,1)S(1)}, u32[]{:S(2)}, u32[]{:S(2)}) collective-permute-start(bf16[32,5120]{1,0:T(8,128)(2,1)S(1)} %get-tuple-element.53), channel_id=1, source_target_pairs={{0,32},{16,48},{32,64},{48,80},{64,96},{80,112},{96,0},{112,16},{1... | collective-permute-start | bytes 983048 | tf_op jit(solution)/shard_map/ppermute | solution.py:453
  191.0 9.9 %collective-permute-start.16 = (bf16[32,5120]{1,0:T(8,128)(2,1)S(1)}, bf16[32,5120]{1,0:T(8,128)(2,1)S(1)}, u32[]{:S(2)}, u32[]{:S(2)}) collective-permute-start(bf16[32,5120]{1,0:T(8,128)(2,1)S(1)} %get-tuple-element.54), channel_id=1, source_target_pairs={{0,96},{16,112},{32,0},{48,16},{64,32},{80,48},{96,64},{112,80},{1... | collective-permute-start | bytes 983048 | tf_op jit(solution)/shard_map/ppermute | solution.py:453
  200.9 17.4 %copy-start.3 = (bf16[1,128,5120]{2,1,0:T(8,128)(2,1)S(1)}, bf16[1,128,5120]{2,1,0:T(8,128)(2,1)}, u32[]{:S(2)}) copy-start(bf16[1,128,5120]{2,1,0:T(8,128)(2,1)} %param.16) | copy-start | bytes 3932164
  200.9 17.4 %copy-start.6 = (f32[5120]{0:T(1024)S(1)}, f32[5120]{0:T(1024)}, u32[]{:S(2)}) copy-start(f32[5120]{0:T(1024)} %param.20) | copy-start | bytes 61444
  201.3 17.0 %copy-start.1 = (bf16[1,128,5120]{2,1,0:T(8,128)(2,1)S(1)}, bf16[1,128,5120]{2,1,0:T(8,128)(2,1)}, u32[]{:S(2)}) copy-start(bf16[1,128,5120]{2,1,0:T(8,128)(2,1)} %param.15) | copy-start | bytes 3932164
  221.8 25.8 %all-to-all-start.3 = ((bf16[8,128,640]{2,1,0:T(8,128)(2,1)}), bf16[8,128,640]{2,1,0:T(8,128)(2,1)S(1)}, u32[]{:S(2)}, u32[]{:S(2)}) async-start(bf16[8,128,640]{2,1,0:T(8,128)(2,1)} %get-tuple-element.46), calls=%async_computation.3 | async-start | bytes 2621440 | tf_op jit(solution)/shard_map/all_to_all | solution.py:493
  247.6 1.1 copy-start.16

commit v5 on v4

--- a/solution.py
+++ b/solution.py
@@ -427,21 +427,22 @@
 
 
 def place_kernel(block, dq, dk, dv):
-    dq[...] = block[0, :, :GW]
-    dk[...] = block[0, :, GW:GW + DH]
-    dv[...] = block[0, :, GW + DH:]
+    for k in range(2):
+        dq[:, k * GW:(k + 1) * GW] = block[k, :, :GW]
+        dk[:, k * DH:(k + 1) * DH] = block[k, :, GW:GW + DH]
+        dv[:, k * DH:(k + 1) * DH] = block[k, :, GW + DH:]
 
 
 def place(blocks):
     return pl.pallas_call(
         place_kernel,
-        grid=(KVH,),
+        grid=(KVH // 2,),
         out_shape=[sds((TOK, D)), sds((TOK, KVH * DH)), sds((TOK, KVH * DH))],
-        in_specs=[pl.BlockSpec((1, TOK, GW + 2 * DH), lambda i: (i, 0, 0))],
+        in_specs=[pl.BlockSpec((2, TOK, GW + 2 * DH), lambda i: (i, 0, 0))],
         out_specs=[
-            pl.BlockSpec((TOK, GW), lambda i: (0, i)),
-            pl.BlockSpec((TOK, DH), lambda i: (0, i)),
-            pl.BlockSpec((TOK, DH), lambda i: (0, i)),
+            pl.BlockSpec((TOK, 2 * GW), lambda i: (0, i)),
+            pl.BlockSpec((TOK, 2 * DH), lambda i: (0, i)),
+            pl.BlockSpec((TOK, 2 * DH), lambda i: (0, i)),
         ],
         compiler_params=params(24),
         name="place",

time: 294 us -> 293 us (level)
  no operation moved by 1% of the time
where the time goes in v5:
time: 293 us; the launch traced here: 292 us
  waiting for transfers between devices  87 us (30%)
  Pallas kernels  72.7 us (25%)
  blocking collectives  70.1 us (24%)
  starting transfers between devices  51.4 us (18%)
  local copies, waits for them, and re-layouts  8.34 us (3%)
    ppermute x12, waiting for transfers between devices, along_z(): return lax.ppermute(x, 'ctx', pairs)  49.1 us
    all_to_all x2, blocking collectives, swap_exp(): return lax.all_to_all(x, 'exp', split_axis=0, concat_axis=0, tiled=True)  41.6 us
    ppermute x7, waiting for transfers between devices, across_x(): return lax.ppermute(x, 'ctx', [(c, c ^ 1) for c in range(8)])  32.5 us
    all_to_all x1, blocking collectives, swap_ctx(): return lax.all_to_all(x, 'ctx', split_axis=0, concat_axis=0, tiled=True)  28.5 us
    ppermute x12, starting transfers between devices, along_z(): return lax.ppermute(x, 'ctx', pairs)  23.3 us
    pallas_call x2, Pallas kernels, project(): pl.pallas_call(functools.partial(project_kernel, len(pieces)), grid=(D //...  20.6 us
    ppermute x7, starting transfers between devices, across_x(): return lax.ppermute(x, 'ctx', [(c, c ^ 1) for c in range(8)])  17.8 us
    pallas_call x1, Pallas kernels, make_probs(): pl.pallas_call(probs_kernel, grid_spec=pltpu.PrefetchScalarGridSpec(num_s...  14.6 us
  transfers between devices with their start and end apart: 21, of which 11 were waited for; matrix products, arithmetic and copies ran while one was open for 1% of the time, Pallas kernels for 18%

profile of v5, /device:TPU:0, one launch (start us, length us, event | category | flops | bytes accessed | tf_op | source)
XLA Modules:
  0.0 292.4 jit_solution(12852691061595757611)
XLA Ops:
  0.6 0.8 copy.19.weight
  2.2 1.3 copy-done
  3.5 1.3 copy-done.2
  5.5 1.2 dispatch.1
  6.7 24.7 %all_to_all.25 = bf16[16,8,5120]{2,1,0:T(8,128)(2,1)S(1)} all-to-all(bf16[16,8,5120]{2,1,0:T(8,128)(2,1)S(1)} %bitcast.26), channel_id=1, replica_groups=mesh['ctx'=8,'exp'=16] {'exp'}, dimensions={0} | all-to-all | bytes 2621440 | tf_op jit(solution)/shard_map/all_to_all | solution.py:490
  31.9 4.0 %collective-permute-start.6 = (bf16[64,5120]{1,0:T(8,128)(2,1)S(1)}, bf16[64,5120]{1,0:T(8,128)(2,1)S(1)}, u32[]{:S(2)}, u32[]{:S(2)}) collective-permute-start(bf16[64,5120]{1,0:T(8,128)(2,1)S(1)} %get-tuple-element.30.refs_0_.refs_1_), channel_id=1, source_target_pairs={{0,64},{16,80},{32,96},{48,112},{64,0},{80,16},{96,32},{112,48},{1... | collective-permute-start | bytes 1966088 | tf_op jit(solution)/shard_map/ppermute | solution.py:454
  35.9 2.7 collective-permute-start
  39.3 1.3 collective-permute-start.2
  40.6 0.8 collective-permute-start.1
  41.4 10.1 %collective-permute-done.6.refs_6_.refs_7_ = bf16[64,5120]{1,0:T(8,128)(2,1)S(1)} collective-permute-done((bf16[64,5120]{1,0:T(8,128)(2,1)S(1)}, bf16[64,5120]{1,0:T(8,128)(2,1)S(1)}, u32[]{:S(2)}, u32[]{:S(2)}) %collective-permute-start.6) | collective-permute-done | bytes 655392 | tf_op jit(solution)/shard_map/ppermute | solution.py:454
  51.5 2.7 collective-permute-start.7
  55.1 2.9 collective-permute-start.10
  58.0 8.6 %collective-permute-done.4.refs_4_.refs_5_ = bf16[64,5120]{1,0:T(8,128)(2,1)S(1)} collective-permute-done((bf16[64,5120]{1,0:T(8,128)(2,1)S(1)}, bf16[64,5120]{1,0:T(8,128)(2,1)S(1)}, u32[]{:S(2)}, u32[]{:S(2)}) %collective-permute-start.4) | collective-permute-done | bytes 655392 | tf_op jit(solution)/shard_map/ppermute | solution.py:454
  66.6 2.6 collective-permute-start.9
  69.2 2.8 collective-permute-start.5
  72.0 11.1 %collective-permute-done.7.refs_7_.refs_8_ = bf16[64,5120]{1,0:T(8,128)(2,1)S(1)} collective-permute-done((bf16[64,5120]{1,0:T(8,128)(2,1)S(1)}, bf16[64,5120]{1,0:T(8,128)(2,1)S(1)}, u32[]{:S(2)}, u32[]{:S(2)}) %collective-permute-start.7) | collective-permute-done | bytes 655392 | tf_op jit(solution)/shard_map/ppermute | solution.py:458
  83.1 2.7 collective-permute-start.3
  85.9 2.9 cut_heads.1.refs_0_
  88.8 8.5 %collective-permute-done.5.refs_5_.refs_6_ = bf16[64,5120]{1,0:T(8,128)(2,1)} collective-permute-done((bf16[64,5120]{1,0:T(8,128)(2,1)S(1)}, bf16[64,5120]{1,0:T(8,128)(2,1)}, u32[]{:S(2)}, u32[]{:S(2)}) %collective-permute-start.5) | collective-permute-done | bytes 655392 | tf_op jit(solution)/shard_map/ppermute | solution.py:458
  97.3 12.2 %collective-permute-done.3.refs_3_.refs_4_ = bf16[64,5120]{1,0:T(8,128)(2,1)S(1)} collective-permute-done((bf16[64,5120]{1,0:T(8,128)(2,1)S(1)}, bf16[64,5120]{1,0:T(8,128)(2,1)S(1)}, u32[]{:S(2)}, u32[]{:S(2)}) %collective-permute-start.3) | collective-permute-done | bytes 655392 | tf_op jit(solution)/shard_map/ppermute | solution.py:458
  109.4 0.8 copy-done.15
  110.3 4.4 %all-to-all-start.1 = ((bf16[8,128,896]{2,1,0:T(8,128)(2,1)}), bf16[8,128,896]{2,1,0:T(8,128)(2,1)S(1)}, u32[]{:S(2)}, u32[]{:S(2)}) async-start(bf16[8,128,896]{2,1,0:T(8,128)(2,1)} %hold.4), calls=%async_computation.1 | async-start | bytes 3670016 | tf_op jit(solution)/shard_map/all_to_all | solution.py:494
  114.7 10.4 %project.2 = (bf16[256,512]{1,0:T(8,128)(2,1)}, bf16[256,512]{1,0:T(8,128)(2,1)}) custom-call(bf16[64,5120]{1,0:T(8,128)(2,1)} %copy-done.4, bf16[64,5120]{1,0:T(8,128)(2,1)} %copy-done.13, bf16[64,5120]{1,0:T(8,128)(2,1)} %copy-done.12, bf16[64,5120]{1,0:T(8,128)(2,1)} %copy-done.15, bf16[64,5120]{1,0:T(8,128)(2,1)} %copy-done.11, ...), custom_call_target="tpu_custom_call" | custom-call | flops 4026531840 | bytes 29360128 | tf_op jit(solution)/shard_map/project/pallas_call | solution.py:160
  125.1 6.9 %terms.2 = (bf16[128,5120]{1,0:T(8,128)(2,1)}, bf16[128,5120]{1,0:T(8,128)(2,1)}) custom-call(bf16[256,512]{1,0:T(8,128)(2,1)} %get-tuple-element.31.grad_gate, bf16[256,512]{1,0:T(8,128)(2,1)} %get-tuple-element.32.grad_up, bf16[1,5120,512]{2,1,0:T(8,128)(2,1)} %w_gate.3, bf16[1,5120,512]{2,1,0:T(8,128)(2,1)} %w_in.3), custom_call_target="tpu_custom_call" | custom-call | flops 2684354560 | bytes 14680064 | tf_op jit(solution)/shard_map/terms/pallas_call | solution.py:192
  132.0 10.3 %project.3 = (bf16[256,512]{1,0:T(8,128)(2,1)}, bf16[256,512]{1,0:T(8,128)(2,1)}) custom-call(bf16[128,5120]{1,0:T(8,128)(2,1)} %hold.3.refs_0_, bf16[128,5120]{1,0:T(8,128)(2,1)} %collective-permute-done.8.refs_1_, bf16[128,5120]{1,0:T(8,128)(2,1)} %collective-permute-done.9.refs_2_, bf16[128,5120]{1,0:T(8,128)(2,1)} %collective-permute-done.10.refs_3_, ...), custom_call_target="tpu_custom_call" | custom-call | flops 4026531840 | bytes 29360128 | tf_op jit(solution)/shard_map/project/pallas_call | solution.py:160
  142.3 6.8 %terms.3 = (bf16[64,5120]{1,0:T(8,128)(2,1)}, bf16[64,5120]{1,0:T(8,128)(2,1)}, bf16[64,5120]{1,0:T(8,128)(2,1)}, bf16[64,5120]{1,0:T(8,128)(2,1)}) custom-call(bf16[256,512]{1,0:T(8,128)(2,1)} %get-tuple-element.34.grad_gate, bf16[256,512]{1,0:T(8,128)(2,1)} %get-tuple-element.35.grad_up, bf16[1,5120,512]{2,1,0:T(8,128)(2,1)} %w_gate.3, ...), custom_call_target="tpu_custom_call" | custom-call | flops 2684354560 | bytes 14680064 | tf_op jit(solution)/shard_map/terms/pallas_call | solution.py:192
  149.1 3.2 %collective-permute-start.11 = (bf16[64,5120]{1,0:T(8,128)(2,1)}, bf16[64,5120]{1,0:T(8,128)(2,1)S(1)}, u32[]{:S(2)}, u32[]{:S(2)}) collective-permute-start(bf16[64,5120]{1,0:T(8,128)(2,1)} %get-tuple-element.37), channel_id=1, source_target_pairs={{0,96},{16,112},{32,0},{48,16},{64,32},{80,48},{96,64},{112,80},{1... | collective-permute-start | bytes 1966088 | tf_op jit(solution)/shard_map/ppermute | solution.py:454
  152.3 2.3 collective-permute-start.13
  154.7 1.2 copy-done.8
  155.9 3.0 %collective-permute-start.15 = (bf16[128,5120]{1,0:T(8,128)(2,1)}, bf16[128,5120]{1,0:T(8,128)(2,1)S(1)}, u32[]{:S(2)}, u32[]{:S(2)}) collective-permute-start(bf16[128,5120]{1,0:T(8,128)(2,1)} %hold.5), channel_id=1, source_target_pairs={{0,16},{16,0},{32,48},{48,32},{64,80},{80,64},{96,112},{112,96},{1... | collective-permute-start | bytes 3932168 | tf_op jit(solution)/shard_map/ppermute | solution.py:458
  158.9 19.8 %collective-permute-done.11 = bf16[64,5120]{1,0:T(8,128)(2,1)S(1)} collective-permute-done((bf16[64,5120]{1,0:T(8,128)(2,1)}, bf16[64,5120]{1,0:T(8,128)(2,1)S(1)}, u32[]{:S(2)}, u32[]{:S(2)}) %collective-permute-start.11) | collective-permute-done | bytes 655392 | tf_op jit(solution)/shard_map/ppermute | solution.py:454
  178.6 3.4 %collective-permute-done.12 = bf16[64,5120]{1,0:T(8,128)(2,1)} collective-permute-done((bf16[64,5120]{1,0:T(8,128)(2,1)}, bf16[64,5120]{1,0:T(8,128)(2,1)}, u32[]{:S(2)}, u32[]{:S(2)}) %collective-permute-start.12) | collective-permute-done | bytes 655392 | tf_op jit(solution)/shard_map/ppermute | solution.py:454
  182.0 1.7 convert_add_fusion.1
  183.8 3.0 %collective-permute-start.14 = (bf16[32,5120]{1,0:T(8,128)(2,1)S(1)}, bf16[32,5120]{1,0:T(8,128)(2,1)S(1)}, u32[]{:S(2)}, u32[]{:S(2)}) collective-permute-start(bf16[32,5120]{1,0:T(8,128)(2,1)S(1)} %slice.32), channel_id=1, source_target_pairs={{0,16},{16,0},{32,48},{48,32},{64,80},{80,64},{96,112},{112,96},{1... | collective-permute-start | bytes 983048 | tf_op jit(solution)/shard_map/ppermute | solution.py:458
  187.3 1.2 collective-permute-start.18
  188.5 2.5 collective-permute-start.17
  191.0 2.6 collective-permute-start.16
  193.7 3.8 %collective-permute-done.18.b2 = bf16[32,5120]{1,0:T(8,128)(2,1)S(1)} collective-permute-done((bf16[32,5120]{1,0:T(8,128)(2,1)S(1)}, bf16[32,5120]{1,0:T(8,128)(2,1)S(1)}, u32[]{:S(2)}, u32[]{:S(2)}) %collective-permute-start.18) | collective-permute-done | bytes 327712 | tf_op jit(solution)/shard_map/ppermute | solution.py:454
  197.5 3.4 %collective-permute-done.17.b3 = bf16[32,5120]{1,0:T(8,128)(2,1)S(1)} collective-permute-done((bf16[32,5120]{1,0:T(8,128)(2,1)S(1)}, bf16[32,5120]{1,0:T(8,128)(2,1)S(1)}, u32[]{:S(2)}, u32[]{:S(2)}) %collective-permute-start.17) | collective-permute-done | bytes 327712 | tf_op jit(solution)/shard_map/ppermute | solution.py:454
  201.3 16.9 %all_to_all.26 = bf16[16,8,2560]{2,1,0:T(8,128)(2,1)S(1)} all-to-all(bf16[16,8,2560]{2,1,0:T(8,128)(2,1)S(1)} %bitcast.25), channel_id=1, replica_groups=mesh['ctx'=8,'exp'=16] {'exp'}, dimensions={0} | all-to-all | bytes 1310720 | tf_op jit(solution)/shard_map/all_to_all | solution.py:490
  218.3 3.5 %finish.1 = (bf16[128,5120]{1,0:T(8,128)(2,1)}, bf16[8,128,640]{2,1,0:T(8,128)(2,1)}) custom-call(bf16[128,5120]{1,0:T(8,128)(2,1)S(1)} %bitcast.20, bf16[128,5120]{1,0:T(8,128)(2,1)S(1)} %bitcast.22, f32[1,5120]{1,0:T(1,128)S(1)} %bitcast.28, bf16[256,128]{1,0:T(8,128)(2,1)S(1)} %get-tuple-element.27.picks, bf16[128,2560]{1,0:T(8,128)(2,1)S(1)} %bitcast.24), custom_call_target="tpu_custom_call" | custom-call | tf_op jit(solution)/shard_map/finish/pallas_call | solution.py:252
  221.8 5.8 %all-to-all-start.3 = ((bf16[8,128,640]{2,1,0:T(8,128)(2,1)}), bf16[8,128,640]{2,1,0:T(8,128)(2,1)S(1)}, u32[]{:S(2)}, u32[]{:S(2)}) async-start(bf16[8,128,640]{2,1,0:T(8,128)(2,1)} %get-tuple-element.46), calls=%async_computation.3 | async-start | bytes 2621440 | tf_op jit(solution)/shard_map/all_to_all | solution.py:494
  227.5 14.6 %probs.1 = (bf16[5,4,1024,256]{3,2,1,0:T(8,128)(2,1)}, f32[5,128,1024]{2,1,0:T(8,128)}, bf16[5,1024,128]{2,1,0:T(8,128)(2,1)}, bf16[2,1024,128]{2,1,0:T(8,128)(2,1)}) custom-call(s32[16]{0:T(128)} %order.3, bf16[1024,896]{1,0:T(8,128)(2,1)} %bitcast.30), custom_call_target="tpu_custom_call" | custom-call | flops 1342177280 | bytes 14680064 | tf_op jit(solution)/shard_map/probs/pallas_call | solution.py:312
  242.1 5.5 %all-to-all-done.3 = bf16[8,128,640]{2,1,0:T(8,128)(2,1)S(1)} async-done(((bf16[8,128,640]{2,1,0:T(8,128)(2,1)}), bf16[8,128,640]{2,1,0:T(8,128)(2,1)S(1)}, u32[]{:S(2)}, u32[]{:S(2)}) %all-to-all-start.3) | async-done | bytes 1310752 | tf_op jit(solution)/shard_map/all_to_all | solution.py:494
  247.6 1.1 copy-done.16
  248.6 13.5 %attend.1 = bf16[1024,896]{1,0:T(8,128)(2,1)} custom-call(s32[16]{0:T(128)} %order.3, bf16[5,4,1024,256]{3,2,1,0:T(8,128)(2,1)} %get-tuple-element.42.probs, f32[5,128,1024]{2,1,0:T(8,128)} %get-tuple-element.43.attended, bf16[5,1024,128]{2,1,0:T(8,128)(2,1)} %get-tuple-element.44.q, bf16[2,1024,128]{2,1,0:T(8,128)(2,1)} %get-tuple-element.45.kv, ...), custom_call_target="tpu_custom_call" | custom-call | flops 5368709120 | bytes 16777216 | tf_op jit(solution)/shard_map/attend/pallas_call | solution.py:387
  262.2 28.5 %all_to_all.27.block = bf16[8,128,896]{2,1,0:T(8,128)(2,1)S(1)} all-to-all(bf16[8,128,896]{2,1,0:T(8,128)(2,1)} %bitcast.31), channel_id=1, replica_groups=mesh['ctx'=8,'exp'=16] {'ctx'}, dimensions={0} | all-to-all | bytes 3670016 | tf_op jit(solution)/shard_map/all_to_all | solution.py:494
  290.7 1.8 place.1
  (58 shorter events, 4.6 us)
Async XLA Ops:
  2.2 1.3 copy-start
  3.5 1.3 copy-start.2
  4.8 0.7 copy-start.5
  31.9 23.2 %copy-start.4 = (bf16[64,5120]{1,0:T(8,128)(2,1)}, bf16[64,5120]{1,0:T(8,128)(2,1)S(1)}, u32[]{:S(2)}) copy-start(bf16[64,5120]{1,0:T(8,128)(2,1)S(1)} %get-tuple-element.30.refs_0_.refs_1_) | copy-start | bytes 1966084
  31.9 19.6 %collective-permute-start.6 = (bf16[64,5120]{1,0:T(8,128)(2,1)S(1)}, bf16[64,5120]{1,0:T(8,128)(2,1)S(1)}, u32[]{:S(2)}, u32[]{:S(2)}) collective-permute-start(bf16[64,5120]{1,0:T(8,128)(2,1)S(1)} %get-tuple-element.30.refs_0_.refs_1_), channel_id=1, source_target_pairs={{0,64},{16,80},{32,96},{48,112},{64,0},{80,16},{96,32},{112,48},{1... | collective-permute-start | bytes 1966088 | tf_op jit(solution)/shard_map/ppermute | solution.py:454
  35.9 19.2 %collective-permute-start = (bf16[64,5120]{1,0:T(8,128)(2,1)S(1)}, bf16[64,5120]{1,0:T(8,128)(2,1)S(1)}, u32[]{:S(2)}, u32[]{:S(2)}) collective-permute-start(bf16[64,5120]{1,0:T(8,128)(2,1)S(1)} %get-tuple-element.29), channel_id=1, source_target_pairs={{0,16},{16,0},{32,48},{48,32},{64,80},{80,64},{96,112},{112,96},{1... | collective-permute-start | bytes 1966088 | tf_op jit(solution)/shard_map/ppermute | solution.py:458
  38.6 28.0 %collective-permute-start.4 = (bf16[64,5120]{1,0:T(8,128)(2,1)S(1)}, bf16[64,5120]{1,0:T(8,128)(2,1)S(1)}, u32[]{:S(2)}, u32[]{:S(2)}) collective-permute-start(bf16[64,5120]{1,0:T(8,128)(2,1)S(1)} %get-tuple-element.30.refs_0_.refs_1_), channel_id=1, source_target_pairs={{0,96},{16,112},{32,0},{48,16},{64,32},{80,48},{96,64},{112,80},{1... | collective-permute-start | bytes 1966088 | tf_op jit(solution)/shard_map/ppermute | solution.py:454
  39.3 29.9 %collective-permute-start.2 = (bf16[64,5120]{1,0:T(8,128)(2,1)S(1)}, bf16[64,5120]{1,0:T(8,128)(2,1)S(1)}, u32[]{:S(2)}, u32[]{:S(2)}) collective-permute-start(bf16[64,5120]{1,0:T(8,128)(2,1)S(1)} %get-tuple-element.30.refs_0_.refs_1_), channel_id=1, source_target_pairs={{0,32},{16,48},{32,64},{48,80},{64,96},{80,112},{96,0},{112,16},{1... | collective-permute-start | bytes 1966088 | tf_op jit(solution)/shard_map/ppermute | solution.py:454
  40.6 28.6 %collective-permute-start.1 = (bf16[64,5120]{1,0:T(8,128)(2,1)S(1)}, bf16[64,5120]{1,0:T(8,128)(2,1)S(1)}, u32[]{:S(2)}, u32[]{:S(2)}) collective-permute-start(bf16[64,5120]{1,0:T(8,128)(2,1)S(1)} %get-tuple-element.30.refs_0_.refs_1_), channel_id=1, source_target_pairs={{0,16},{16,0},{32,48},{48,32},{64,80},{80,64},{96,112},{112,96},{1... | collective-permute-start | bytes 1966088 | tf_op jit(solution)/shard_map/ppermute | solution.py:458
  51.5 3.6 %copy-start.10 = (bf16[64,5120]{1,0:T(8,128)(2,1)}, bf16[64,5120]{1,0:T(8,128)(2,1)S(1)}, u32[]{:S(2)}) copy-start(bf16[64,5120]{1,0:T(8,128)(2,1)S(1)} %collective-permute-done.6.refs_6_.refs_7_) | copy-start | bytes 1966084
  51.5 31.6 %collective-permute-start.7 = (bf16[64,5120]{1,0:T(8,128)(2,1)S(1)}, bf16[64,5120]{1,0:T(8,128)(2,1)S(1)}, u32[]{:S(2)}, u32[]{:S(2)}) collective-permute-start(bf16[64,5120]{1,0:T(8,128)(2,1)S(1)} %collective-permute-done.6.refs_6_.refs_7_), channel_id=1, source_target_pairs={{0,16},{16,0},{32,48},{48,32},{64,80},{80,64},{96,112},{112,96},{1... | collective-permute-start | bytes 1966088 | tf_op jit(solution)/shard_map/ppermute | solution.py:458
  55.1 33.7 %copy-start.7 = (bf16[128,5120]{1,0:T(8,128)(2,1)}, bf16[128,5120]{1,0:T(8,128)(2,1)S(1)}, u32[]{:S(2)}) copy-start(bf16[128,5120]{1,0:T(8,128)(2,1)S(1)} %constant_dynamic-update-slice_fusion.refs_0_) | copy-start | bytes 3932164
  55.1 76.9 %collective-permute-start.10 = (bf16[128,5120]{1,0:T(8,128)(2,1)S(1)}, bf16[128,5120]{1,0:T(8,128)(2,1)}, u32[]{:S(2)}, u32[]{:S(2)}) collective-permute-start(bf16[128,5120]{1,0:T(8,128)(2,1)S(1)} %constant_dynamic-update-slice_fusion.refs_0_), channel_id=1, source_target_pairs={{0,64},{16,80},{32,96},{48,112},{64,0},{80,16},{96,32},{112,48},{1... | collective-permute-start | bytes 3932168 | tf_op jit(solution)/shard_map/ppermute | solution.py:454
  66.6 22.2 %copy-start.11 = (bf16[64,5120]{1,0:T(8,128)(2,1)}, bf16[64,5120]{1,0:T(8,128)(2,1)S(1)}, u32[]{:S(2)}) copy-start(bf16[64,5120]{1,0:T(8,128)(2,1)S(1)} %collective-permute-done.4.refs_4_.refs_5_) | copy-start | bytes 1966084
  66.6 65.4 %collective-permute-start.9 = (bf16[128,5120]{1,0:T(8,128)(2,1)S(1)}, bf16[128,5120]{1,0:T(8,128)(2,1)}, u32[]{:S(2)}, u32[]{:S(2)}) collective-permute-start(bf16[128,5120]{1,0:T(8,128)(2,1)S(1)} %constant_dynamic-update-slice_fusion.refs_0_), channel_id=1, source_target_pairs={{0,96},{16,112},{32,0},{48,16},{64,32},{80,48},{96,64},{112,80},{1... | collective-permute-start | bytes 3932168 | tf_op jit(solution)/shard_map/ppermute | solution.py:454
  69.2 19.6 %copy-start.12 = (bf16[64,5120]{1,0:T(8,128)(2,1)}, bf16[64,5120]{1,0:T(8,128)(2,1)S(1)}, u32[]{:S(2)}) copy-start(bf16[64,5120]{1,0:T(8,128)(2,1)S(1)} %collective-permute-done.2.refs_2_.refs_3_) | copy-start | bytes 1966084
  69.2 62.8 %collective-permute-start.8 = (bf16[128,5120]{1,0:T(8,128)(2,1)S(1)}, bf16[128,5120]{1,0:T(8,128)(2,1)}, u32[]{:S(2)}, u32[]{:S(2)}) collective-permute-start(bf16[128,5120]{1,0:T(8,128)(2,1)S(1)} %constant_dynamic-update-slice_fusion.refs_0_), channel_id=1, source_target_pairs={{0,32},{16,48},{32,64},{48,80},{64,96},{80,112},{96,0},{112,16},{1... | collective-permute-start | bytes 3932168 | tf_op jit(solution)/shard_map/ppermute | solution.py:454
  69.2 13.9 %copy-start.13 = (bf16[64,5120]{1,0:T(8,128)(2,1)}, bf16[64,5120]{1,0:T(8,128)(2,1)S(1)}, u32[]{:S(2)}) copy-start(bf16[64,5120]{1,0:T(8,128)(2,1)S(1)} %collective-permute-done.1.refs_1_.refs_2_) | copy-start | bytes 1966084
  69.2 28.0 %collective-permute-start.5 = (bf16[64,5120]{1,0:T(8,128)(2,1)S(1)}, bf16[64,5120]{1,0:T(8,128)(2,1)}, u32[]{:S(2)}, u32[]{:S(2)}) collective-permute-start(bf16[64,5120]{1,0:T(8,128)(2,1)S(1)} %collective-permute-done.4.refs_4_.refs_5_), channel_id=1, source_target_pairs={{0,16},{16,0},{32,48},{48,32},{64,80},{80,64},{96,112},{112,96},{1... | collective-permute-start | bytes 1966088 | tf_op jit(solution)/shard_map/ppermute | solution.py:458
  83.1 2.7 copy-start.14
  83.1 26.3 %collective-permute-start.3 = (bf16[64,5120]{1,0:T(8,128)(2,1)S(1)}, bf16[64,5120]{1,0:T(8,128)(2,1)S(1)}, u32[]{:S(2)}, u32[]{:S(2)}) collective-permute-start(bf16[64,5120]{1,0:T(8,128)(2,1)S(1)} %collective-permute-done.2.refs_2_.refs_3_), channel_id=1, source_target_pairs={{0,16},{16,0},{32,48},{48,32},{64,80},{80,64},{96,112},{112,96},{1... | collective-permute-start | bytes 1966088 | tf_op jit(solution)/shard_map/ppermute | solution.py:458
  109.4 0.8 copy-start.15
  110.3 44.4 %all-to-all-start.1 = ((bf16[8,128,896]{2,1,0:T(8,128)(2,1)}), bf16[8,128,896]{2,1,0:T(8,128)(2,1)S(1)}, u32[]{:S(2)}, u32[]{:S(2)}) async-start(bf16[8,128,896]{2,1,0:T(8,128)(2,1)} %hold.4), calls=%async_computation.1 | async-start | bytes 3670016 | tf_op jit(solution)/shard_map/all_to_all | solution.py:494
  149.1 29.5 %collective-permute-start.11 = (bf16[64,5120]{1,0:T(8,128)(2,1)}, bf16[64,5120]{1,0:T(8,128)(2,1)S(1)}, u32[]{:S(2)}, u32[]{:S(2)}) collective-permute-start(bf16[64,5120]{1,0:T(8,128)(2,1)} %get-tuple-element.37), channel_id=1, source_target_pairs={{0,96},{16,112},{32,0},{48,16},{64,32},{80,48},{96,64},{112,80},{1... | collective-permute-start | bytes 1966088 | tf_op jit(solution)/shard_map/ppermute | solution.py:454
  152.3 29.7 %collective-permute-start.12 = (bf16[64,5120]{1,0:T(8,128)(2,1)}, bf16[64,5120]{1,0:T(8,128)(2,1)}, u32[]{:S(2)}, u32[]{:S(2)}) collective-permute-start(bf16[64,5120]{1,0:T(8,128)(2,1)} %get-tuple-element.38), channel_id=1, source_target_pairs={{0,32},{16,48},{32,64},{48,80},{64,96},{80,112},{96,0},{112,16},{1... | collective-permute-start | bytes 1966088 | tf_op jit(solution)/shard_map/ppermute | solution.py:454
  152.3 29.7 %collective-permute-start.13 = (bf16[64,5120]{1,0:T(8,128)(2,1)}, bf16[64,5120]{1,0:T(8,128)(2,1)}, u32[]{:S(2)}, u32[]{:S(2)}) collective-permute-start(bf16[64,5120]{1,0:T(8,128)(2,1)} %get-tuple-element.39), channel_id=1, source_target_pairs={{0,64},{16,80},{32,96},{48,112},{64,0},{80,16},{96,32},{112,48},{1... | collective-permute-start | bytes 1966088 | tf_op jit(solution)/shard_map/ppermute | solution.py:454
  154.7 1.2 copy-start.8
  155.9 26.1 %copy-start.17 = (bf16[64,5120]{1,0:T(8,128)(2,1)S(1)}, bf16[64,5120]{1,0:T(8,128)(2,1)}, u32[]{:S(2)}) copy-start(bf16[64,5120]{1,0:T(8,128)(2,1)} %get-tuple-element.36) | copy-start | bytes 1966084
  155.9 30.9 %collective-permute-start.15 = (bf16[128,5120]{1,0:T(8,128)(2,1)}, bf16[128,5120]{1,0:T(8,128)(2,1)S(1)}, u32[]{:S(2)}, u32[]{:S(2)}) collective-permute-start(bf16[128,5120]{1,0:T(8,128)(2,1)} %hold.5), channel_id=1, source_target_pairs={{0,16},{16,0},{32,48},{48,32},{64,80},{80,64},{96,112},{112,96},{1... | collective-permute-start | bytes 3932168 | tf_op jit(solution)/shard_map/ppermute | solution.py:458
  182.0 4.8 %copy-start.9 = (bf16[128,5120]{1,0:T(8,128)(2,1)S(1)}, bf16[128,5120]{1,0:T(8,128)(2,1)}, u32[]{:S(2)}) copy-start(bf16[128,5120]{1,0:T(8,128)(2,1)} %get-tuple-element.33.refs_1_) | copy-start | bytes 3932164
  183.8 9.9 %collective-permute-start.14 = (bf16[32,5120]{1,0:T(8,128)(2,1)S(1)}, bf16[32,5120]{1,0:T(8,128)(2,1)S(1)}, u32[]{:S(2)}, u32[]{:S(2)}) collective-permute-start(bf16[32,5120]{1,0:T(8,128)(2,1)S(1)} %slice.32), channel_id=1, source_target_pairs={{0,16},{16,0},{32,48},{48,32},{64,80},{80,64},{96,112},{112,96},{1... | collective-permute-start | bytes 983048 | tf_op jit(solution)/shard_map/ppermute | solution.py:458
  187.3 10.3 %collective-permute-start.18 = (bf16[32,5120]{1,0:T(8,128)(2,1)S(1)}, bf16[32,5120]{1,0:T(8,128)(2,1)S(1)}, u32[]{:S(2)}, u32[]{:S(2)}) collective-permute-start(bf16[32,5120]{1,0:T(8,128)(2,1)S(1)} %get-tuple-element.52), channel_id=1, source_target_pairs={{0,64},{16,80},{32,96},{48,112},{64,0},{80,16},{96,32},{112,48},{1... | collective-permute-start | bytes 983048 | tf_op jit(solution)/shard_map/ppermute | solution.py:454
  188.5 12.4 %collective-permute-start.17 = (bf16[32,5120]{1,0:T(8,128)(2,1)S(1)}, bf16[32,5120]{1,0:T(8,128)(2,1)S(1)}, u32[]{:S(2)}, u32[]{:S(2)}) collective-permute-start(bf16[32,5120]{1,0:T(8,128)(2,1)S(1)} %get-tuple-element.53), channel_id=1, source_target_pairs={{0,32},{16,48},{32,64},{48,80},{64,96},{80,112},{96,0},{112,16},{1... | collective-permute-start | bytes 983048 | tf_op jit(solution)/shard_map/ppermute | solution.py:454
  191.0 9.9 %collective-permute-start.16 = (bf16[32,5120]{1,0:T(8,128)(2,1)S(1)}, bf16[32,5120]{1,0:T(8,128)(2,1)S(1)}, u32[]{:S(2)}, u32[]{:S(2)}) collective-permute-start(bf16[32,5120]{1,0:T(8,128)(2,1)S(1)} %get-tuple-element.54), channel_id=1, source_target_pairs={{0,96},{16,112},{32,0},{48,16},{64,32},{80,48},{96,64},{112,80},{1... | collective-permute-start | bytes 983048 | tf_op jit(solution)/shard_map/ppermute | solution.py:454
  200.9 17.4 %copy-start.3 = (bf16[1,128,5120]{2,1,0:T(8,128)(2,1)S(1)}, bf16[1,128,5120]{2,1,0:T(8,128)(2,1)}, u32[]{:S(2)}) copy-start(bf16[1,128,5120]{2,1,0:T(8,128)(2,1)} %param.16) | copy-start | bytes 3932164
  200.9 17.4 %copy-start.6 = (f32[5120]{0:T(1024)S(1)}, f32[5120]{0:T(1024)}, u32[]{:S(2)}) copy-start(f32[5120]{0:T(1024)} %param.20) | copy-start | bytes 61444
  201.3 17.0 %copy-start.1 = (bf16[1,128,5120]{2,1,0:T(8,128)(2,1)S(1)}, bf16[1,128,5120]{2,1,0:T(8,128)(2,1)}, u32[]{:S(2)}) copy-start(bf16[1,128,5120]{2,1,0:T(8,128)(2,1)} %param.15) | copy-start | bytes 3932164
  221.8 25.8 %all-to-all-start.3 = ((bf16[8,128,640]{2,1,0:T(8,128)(2,1)}), bf16[8,128,640]{2,1,0:T(8,128)(2,1)S(1)}, u32[]{:S(2)}, u32[]{:S(2)}) async-start(bf16[8,128,640]{2,1,0:T(8,128)(2,1)} %get-tuple-element.46), calls=%async_computation.3 | async-start | bytes 2621440 | tf_op jit(solution)/shard_map/all_to_all | solution.py:494
  247.6 1.1 copy-start.16
